TPU v7x, 32 devices: a whole 2x2x4 slice. The times are simulated.
32 devices in a mesh: gx: 8 (over y, x, core), gy: 4 (over z).
Axes of the slice: x: 2, y: 2, z: 4, core: 2. Of those that a mesh axis runs over, the one named last changes fastest.
Arguments:
- particles: float32 [7, 524288], P(None, ('gx', 'gy')), may hold values from -3 to 3, as said below
- mig_count: int32 [32, 4], P(('gx', 'gy')), may hold values from 1 to 512, as said below
- mig_rows: int32 [32, 4, 512], P(('gx', 'gy')), may hold values from 0 to 16383, as said below
- active_ids: int32 [32, 2, 8], P(('gx', 'gy')), may hold values from 0 to 127, as said below
- active_count: int32 [32, 2], P(('gx', 'gy')), may hold values from 1 to 8, as said below
- local_nbrs: int32 [32, 2, 8, 3], P(('gx', 'gy')), may hold values from 0 to 127
- ghost_slots: int32 [32, 2, 8, 4], P(('gx', 'gy')), may hold values from 0 to 31
- export_blocks: int32 [32, 4, 8], P(('gx', 'gy')), may hold values from 0 to 127
Outputs:
- density: float32 [524288], P(('gx', 'gy'))
- accel: float32 [3, 524288], P(None, ('gx', 'gy'))
Inputs may be any that keep to these rules, and one draw needn't show every extreme that they name: `mig_count`: each level's count is the same for both devices of a pair, and device 0 and its partners exchange exactly 512 at every level. `mig_rows`: the slots of one device at one level are distinct. `active_ids`: the 16 ids of one device are distinct. `active_count`: the two bins of one device hold at most 12 blocks together; device 0 holds 8 in bin 0 and 12 in all. `particles`: Rows: positions first, then mass, smoothing length, internal energy and previous density, these four positive.
All inputs are finite; a program needn't handle non-finite values.
Results may differ from a plain program's by a relative error of at most 0.00002.
Values sent between devices are 32-bit elements; how exact they have to be, the bound alone decides.
No kernel may reach another device: no remote copies, remote signals or barrier semaphores. Data moves between devices by JAX's collectives and lax.ppermute only.
A program may use at most 128 MiB of HBM per device.

v0:
```python
import math

import jax
import jax.numpy as jnp
from jax import lax
from jax.sharding import PartitionSpec as P

BLK = 128
TOTACT = 12


KERNEL_NORM = 21.0 / (16.0 * math.pi)
GAMMA_LESS = 2.0 / 3.0


def swapped(block, axis, apart):
    count = lax.axis_size(axis)
    route = []
    for low in range(count):
        high = low | 1 << apart
        if high != low and high < count:
            route += [(low, high), (high, low)]
    return lax.ppermute(block, axis, route)


def density_tile(centre_pos, smooth, others):
    offset = centre_pos[:, :, None] - others[0:3, None, :]
    distance = jnp.sqrt(jnp.sum(offset * offset, axis=0))
    scaled = distance / smooth[:, None]
    falloff = jnp.maximum(1.0 - 0.5 * scaled, 0.0)
    square = falloff * falloff
    kernel = (
        KERNEL_NORM / (smooth * smooth * smooth)[:, None] * (square * square) * (1.0 + 2.0 * scaled)
    )
    return jnp.sum(kernel * others[3][None, :], axis=1)


def pair_force(centre, others):
    offset = centre[0:3, :, None] - others[0:3, None, :]
    distance = jnp.sqrt(jnp.sum(offset * offset, axis=0))
    pair_smooth = 0.5 * (centre[4][:, None] + others[4][None, :])
    scaled = distance / pair_smooth
    falloff = jnp.maximum(1.0 - 0.5 * scaled, 0.0)
    inverse = 1.0 / pair_smooth
    inv_square = inverse * inverse
    gradient = (
        -5.0 * KERNEL_NORM * (falloff * falloff * falloff) * (inv_square * inv_square * inverse)
    )
    pressure = (
        GAMMA_LESS * (centre[5] / centre[6])[:, None]
        + GAMMA_LESS * (others[5] / others[6])[None, :]
    )
    weight = -(centre[3][:, None] * others[3][None, :]) * pressure * gradient
    pushes = weight[None] * offset
    return (jnp.sum(pushes, axis=2), -jnp.sum(pushes, axis=1))


def slot_densities(own_blocks, ghosts, slot_ids, near_ids, far_ids):

    def per_slot(inputs):
        active, near, far = inputs
        centre = own_blocks[active]
        neighbours = jnp.concatenate(
            [centre[None, 0:4], own_blocks[near][:, 0:4], ghosts[far][:, 0:4]], axis=0
        )
        tile_sums = jax.vmap(lambda block_row: density_tile(centre[0:3], centre[4], block_row))(
            neighbours
        )
        return jnp.sum(tile_sums, axis=0)

    return lax.map(per_slot, (slot_ids, near_ids, far_ids))


def slot_forces(own_blocks, ghosts, slot_ids, near_ids, far_ids, live_slot):

    def per_slot(inputs):
        active, near, far, alive = inputs
        centre = own_blocks[active]
        neighbours = jnp.concatenate([own_blocks[near], ghosts[far]], axis=0)
        self_push = pair_force(centre, centre)[0]
        on_centre, on_others = jax.vmap(lambda block_row: pair_force(centre, block_row))(neighbours)
        factor = jnp.where(alive, 1.0, 0.0).astype(jnp.float32)
        count_near = near.shape[0]
        centre_sum = (self_push + jnp.sum(on_centre, axis=0)) * factor
        return (centre_sum, on_others[:count_near] * factor, on_others[count_near:] * factor)

    return lax.map(per_slot, (slot_ids, near_ids, far_ids, live_slot))


def settle(current, moving_rows, outgoing, arrived, count):
    lane_ids = jnp.arange(outgoing.shape[1], dtype=jnp.int32)
    staying = lane_ids < count
    return current.at[:, moving_rows].set(jnp.where(staying[None, :], arrived, outgoing))


def shards(
    particles, mig_count, mig_rows, active_ids, active_count, local_nbrs, ghost_slots, export_blocks
):
    current = particles
    section_num = 0
    for which_bit in (1, 0):
        moving_rows = mig_rows[0, section_num]
        outgoing = current[:, moving_rows]
        arrived = swapped(outgoing, "gx", which_bit)
        current = settle(current, moving_rows, outgoing, arrived, mig_count[0, section_num])
        section_num += 1
    for which_bit in (1, 0):
        moving_rows = mig_rows[0, section_num]
        outgoing = current[:, moving_rows]
        arrived = swapped(outgoing, "gy", which_bit)
        current = settle(current, moving_rows, outgoing, arrived, mig_count[0, section_num])
        section_num += 1
    peers = lax.axis_size("gy")
    blocks = current.reshape(7, -1, BLK).transpose(1, 0, 2)
    block_count = blocks.shape[0]
    exported = export_blocks[0].reshape(-1)
    sendable = blocks[exported].reshape(peers, -1, 7, BLK)
    ghosts = lax.all_to_all(
        sendable[:, :, 0:6], "gy", split_axis=0, concat_axis=0, tiled=True
    ).reshape(-1, 6, BLK)
    slot_total = active_ids.shape[1] * active_ids.shape[2]
    slot_ids = active_ids[0].reshape(-1)
    live_slot = (
        jnp.arange(active_ids.shape[2], dtype=jnp.int32)[None, :] < active_count[0][:, None]
    ).reshape(-1)
    near_ids = local_nbrs[0].reshape(slot_total, -1)
    far_ids = ghost_slots[0].reshape(slot_total, -1)
    ordinal = jnp.arange(slot_total, dtype=jnp.int32)
    order_key = jnp.where(live_slot, ordinal, ordinal + slot_total)
    picked = jnp.argsort(order_key)[:TOTACT]
    slot_ids = slot_ids[picked]
    live_slot = live_slot[picked]
    near_ids = near_ids[picked]
    far_ids = far_ids[picked]
    fresh = slot_densities(blocks, ghosts, slot_ids, near_ids, far_ids)
    previous = blocks[:, 6]
    density = previous.at[slot_ids].set(jnp.where(live_slot[:, None], fresh, previous[slot_ids]))
    blocks = blocks.at[:, 6].set(density)
    ghosts = lax.all_to_all(
        blocks[exported].reshape(peers, -1, 7, BLK), "gy", split_axis=0, concat_axis=0, tiled=True
    ).reshape(-1, 7, BLK)
    on_centre, on_near, on_far = slot_forces(blocks, ghosts, slot_ids, near_ids, far_ids, live_slot)
    totals = jnp.zeros((block_count, 3, BLK), dtype=jnp.float32).at[slot_ids].add(on_centre)
    totals = totals.at[near_ids.reshape(-1)].add(on_near.reshape(-1, 3, BLK))
    returned = (
        jnp.zeros((ghosts.shape[0], 3, BLK), dtype=jnp.float32)
        .at[far_ids.reshape(-1)]
        .add(on_far.reshape(-1, 3, BLK))
    )
    returned = lax.all_to_all(
        returned.reshape(peers, -1, 3, BLK), "gy", split_axis=0, concat_axis=0, tiled=True
    )
    totals = totals.at[exported].add(returned.reshape(-1, 3, BLK))
    accel = totals / blocks[:, 3][:, None, :]
    return (density.reshape(-1), accel.transpose(1, 0, 2).reshape(3, -1))


def solution(mesh):
    placed = (
        P(None, ("gx", "gy")),
        P(("gx", "gy"), None),
        P(("gx", "gy"), None, None),
        P(("gx", "gy"), None, None),
        P(("gx", "gy"), None),
        P(("gx", "gy"), None, None, None),
        P(("gx", "gy"), None, None, None),
        P(("gx", "gy"), None, None),
    )
    return jax.shard_map(
        shards,
        mesh=mesh,
        in_specs=placed,
        out_specs=(P(("gx", "gy")), P(None, ("gx", "gy"))),
        check_vma=False,
    )
```

profile of v0, /device:TPU:0, one launch (start us, length us, event | category | flops | bytes accessed | tf_op | source)
XLA Modules:
  0.0 283.8 jit_solution(11387269128059164633)
XLA Ops:
  0.7 5.7 %copy.55 = f32[7,16384]{0,1:T(8,128)} copy(f32[7,16384]{1,0:T(8,128)} %param.14) | data formatting | bytes 917504 | tf_op args[0]
  6.4 4.4 %gather_fusion.4 = f32[512,7]{1,0:T(8,128)S(1)} fusion(f32[7,16384]{0,1:T(8,128)} %copy.55, s32[1024]{0:T(1024)S(1)} %pad_clamp_fusion.10), kind=kCustom, calls=%fused_computation.4 | custom fusion | bytes 30720 | tf_op jit(solution)/shard_map/gather | solution.py:103
  10.8 3.0 %collective-permute-start = (f32[7,512]{0,1:T(8,128)S(1)}, f32[7,512]{0,1:T(8,128)S(1)}, u32[]{:S(2)}, u32[]{:S(2)}) collective-permute-start(f32[7,512]{0,1:T(8,128)S(1)} %bitcast.228), channel_id=1, source_target_pairs={{0,8},{8,0},{4,12},{12,4},{16,24},{24,16},{20,28},{28,20},{1,9},{9... | collective-permute-start | bytes 43016 | tf_op jit(solution)/shard_map/ppermute | solution.py:23
  14.7 1.3 sort.17
  16.7 3.5 %collective-permute-done = f32[7,512]{0,1:T(8,128)S(1)} collective-permute-done((f32[7,512]{0,1:T(8,128)S(1)}, f32[7,512]{0,1:T(8,128)S(1)}, u32[]{:S(2)}, u32[]{:S(2)}) %collective-permute-start) | collective-permute-done | bytes 14368 | tf_op jit(solution)/shard_map/ppermute | solution.py:23
  20.2 8.4 %scatter_custom_fusion = f32[7,16384]{0,1:T(8,128)} fusion(f32[7,16384]{0,1:T(8,128)} %copy.55, s32[512]{0:T(512)S(1)} %bitcast.244, f32[7,512]{0,1:T(8,128)S(1)} %collective-permute-done, pred[512]{0:T(512)(128)(4,1)S(1)} %iota_compare_fusion.3, f32[512,7]{1,0:T(8,128)S(1)} %gather_fusion.4), kind=kCustom, calls=%fused_computation.97 | custom fusion | flops 3584 | bytes 983552 | tf_op jit(solution)/shard_map/scatter | solution.py:93
  28.5 4.4 %gather_fusion.5 = f32[512,7]{1,0:T(8,128)S(1)} fusion(f32[7,16384]{0,1:T(8,128)} %scatter_custom_fusion, s32[1024]{0:T(1024)S(1)} %pad_clamp_fusion.9), kind=kCustom, calls=%fused_computation.5 | custom fusion | bytes 30720 | tf_op jit(solution)/shard_map/gather | solution.py:103
  33.7 0.9 collective-permute-done.1
  34.6 8.4 %scatter_custom_fusion.1 = f32[7,16384]{0,1:T(8,128)} fusion(f32[7,16384]{0,1:T(8,128)} %scatter_custom_fusion, s32[512]{0:T(512)S(1)} %bitcast.242, f32[7,512]{0,1:T(8,128)S(1)} %collective-permute-done.1, pred[512]{0:T(512)(128)(4,1)S(1)} %iota_compare_fusion.2, f32[512,7]{1,0:T(8,128)S(1)} %gather_fusion.5), kind=kCustom, calls=%fused_computation.95 | custom fusion | flops 3584 | bytes 983552 | tf_op jit(solution)/shard_map/scatter | solution.py:93
  43.0 4.4 %gather_fusion.6 = f32[512,7]{1,0:T(8,128)S(1)} fusion(f32[7,16384]{0,1:T(8,128)} %scatter_custom_fusion.1, s32[1024]{0:T(1024)S(1)} %pad_clamp_fusion.8), kind=kCustom, calls=%fused_computation.6 | custom fusion | bytes 30720 | tf_op jit(solution)/shard_map/gather | solution.py:109
  47.4 2.9 %collective-permute-start.2 = (f32[7,512]{0,1:T(8,128)S(1)}, f32[7,512]{0,1:T(8,128)S(1)}, u32[]{:S(2)}, u32[]{:S(2)}) collective-permute-start(f32[7,512]{0,1:T(8,128)S(1)} %bitcast.231), channel_id=1, source_target_pairs={{0,2},{2,0},{1,3},{3,1},{4,6},{6,4},{5,7},{7,5},{8,10},{10,8},{9,1... | collective-permute-start | bytes 43016 | tf_op jit(solution)/shard_map/ppermute | solution.py:23
  50.9 11.6 %collective-permute-done.2 = f32[7,512]{0,1:T(8,128)S(1)} collective-permute-done((f32[7,512]{0,1:T(8,128)S(1)}, f32[7,512]{0,1:T(8,128)S(1)}, u32[]{:S(2)}, u32[]{:S(2)}) %collective-permute-start.2) | collective-permute-done | bytes 14368 | tf_op jit(solution)/shard_map/ppermute | solution.py:23
  62.5 8.4 %scatter_custom_fusion.2 = f32[7,16384]{0,1:T(8,128)} fusion(f32[7,16384]{0,1:T(8,128)} %scatter_custom_fusion.1, s32[512]{0:T(512)S(1)} %bitcast.240, f32[7,512]{0,1:T(8,128)S(1)} %collective-permute-done.2, pred[512]{0:T(512)(128)(4,1)S(1)} %iota_compare_fusion.1, f32[512,7]{1,0:T(8,128)S(1)} %gather_fusion.6), kind=kCustom, calls=%fused_computation.93 | custom fusion | flops 3584 | bytes 983552 | tf_op jit(solution)/shard_map/scatter | solution.py:93
  70.9 4.4 %gather_fusion.7 = f32[512,7]{1,0:T(8,128)S(1)} fusion(f32[7,16384]{0,1:T(8,128)} %scatter_custom_fusion.2, s32[1024]{0:T(1024)S(1)} %pad_clamp_fusion.7), kind=kCustom, calls=%fused_computation.7 | custom fusion | bytes 30720 | tf_op jit(solution)/shard_map/gather | solution.py:109
  77.5 5.6 %collective-permute-done.3 = f32[7,512]{0,1:T(8,128)S(1)} collective-permute-done((f32[7,512]{0,1:T(8,128)S(1)}, f32[7,512]{0,1:T(8,128)S(1)}, u32[]{:S(2)}, u32[]{:S(2)}) %collective-permute-start.3) | collective-permute-done | bytes 14368 | tf_op jit(solution)/shard_map/ppermute | solution.py:23
  83.1 8.4 %scatter_custom_fusion.3 = f32[7,16384]{0,1:T(8,128)} fusion(f32[7,16384]{0,1:T(8,128)} %scatter_custom_fusion.2, s32[512]{0:T(512)S(1)} %bitcast.238, f32[7,512]{0,1:T(8,128)S(1)} %collective-permute-done.3, pred[512]{0:T(512)(128)(4,1)S(1)} %iota_compare_fusion, f32[512,7]{1,0:T(8,128)S(1)} %gather_fusion.7), kind=kCustom, calls=%fused_computation.91 | custom fusion | flops 3584 | bytes 983552 | tf_op jit(solution)/shard_map/scatter | solution.py:93
  91.5 5.5 %copy.56 = f32[7,128,128]{2,0,1:T(8,128)S(1)} copy(f32[7,128,128]{0,2,1:T(8,128)} %bitcast.209) | data formatting | bytes 917504 | tf_op jit(solution)/shard_map/reshape | solution.py:114
  98.3 5.3 %all-to-all-start = ((f32[4,8,6,128]{3,1,2,0:T(8,128)}), f32[4,8,6,128]{3,1,2,0:T(8,128)S(1)}, u32[]{:S(2)}, u32[]{:S(2)}) async-start(f32[4,8,6,128]{3,1,2,0:T(8,128)} %copy.78), calls=%async_computation | async-start | bytes 196608 | tf_op jit(solution)/shard_map/all_to_all | solution.py:118
  105.8 8.8 %slice.183 = f32[128,1,128]{1,2,0:T(8,128)} slice(f32[128,7,128]{1,2,0:T(8,128)} %bitcast.210), slice={[0:128], [6:7], [0:128]} | slice | bytes 131072 | tf_op jit(solution)/shard_map/slice | solution.py:136
  114.6 5.2 %copy.77 = f32[128,1,128]{2,0,1:T(8,128)S(1)} copy(f32[128,1,128]{1,2,0:T(8,128)} %slice.183) | data formatting | bytes 131072
  119.9 54.6 %while.25 = (s32[]{:T(128)}, f32[12,128]{1,0:T(8,128)S(1)}, s32[12]{0:T(128)S(1)}, f32[128,7,128]{2,1,0:T(8,128)S(1)}, s32[12,3]{1,0:T(8,128)S(1)}, /*index=5*/s...) while((s32[]{:T(128)}, f32[12,128]{1,0:T(8,128)S(1)}, s32[12]{0:T(128)S(1)}, ...), condition=%wide.region_8.9_spmd, body=%wide.region_5.8_spmd.sunk | while | flops 2634010 | bytes 1221915 | solution.py:71
  174.4 0.9 scatter_custom_fusion.4
  175.4 1.4 scatter.45
  178.1 5.1 %all-to-all-start.1 = ((f32[4,8,7,128]{3,1,2,0:T(8,128)}), f32[4,8,7,128]{3,1,2,0:T(8,128)S(1)}, u32[]{:S(2)}, u32[]{:S(2)}) async-start(f32[4,8,7,128]{3,1,2,0:T(8,128)} %copy.64), calls=%async_computation.1 | async-start | bytes 229376 | tf_op jit(solution)/shard_map/all_to_all | solution.py:139
  183.2 5.9 %all-to-all-done.1 = f32[4,8,7,128]{3,1,2,0:T(8,128)S(1)} async-done(((f32[4,8,7,128]{3,1,2,0:T(8,128)}), f32[4,8,7,128]{3,1,2,0:T(8,128)S(1)}, u32[]{:S(2)}, u32[]{:S(2)}) %all-to-all-start.1) | async-done | bytes 114720 | tf_op jit(solution)/shard_map/all_to_all | solution.py:139
  189.1 80.4 %while.26 = (s32[]{:T(128)}, f32[12,3,128]{2,1,0:T(4,128)S(1)}, f32[12,3,3,128]{3,2,1,0:T(4,128)S(1)}, f32[12,4,3,128]{3,2,1,0:T(4,128)S(1)}, s32[12]{0:T(128)S(...) while((s32[]{:T(128)}, f32[12,3,128]{2,1,0:T(4,128)S(1)}, ...), condition=%wide.region_16.17_spmd, body=%wide.region_10.16_spmd.sunk | while | flops 5069467 | bytes 2405226 | solution.py:87
  269.5 2.2 scatter_fusion.2
  272.4 3.3 %all-to-all-start.2 = ((f32[4,8,3,128]{3,1,2,0:T(8,128)}), f32[4,8,3,128]{3,1,2,0:T(8,128)S(1)}, u32[]{:S(2)}, u32[]{:S(2)}) async-start(f32[4,8,3,128]{3,1,2,0:T(8,128)} %copy.67), calls=%async_computation.2 | async-start | bytes 98304 | tf_op jit(solution)/shard_map/all_to_all | solution.py:150
  275.8 1.0 scatter_fusion
  276.8 2.2 scatter_fusion.1
  279.0 2.3 all-to-all-done.2
  281.4 1.6 scatter_fusion.3
  (622 shorter events, 88.1 us)
Async XLA Ops:
  0.6 5.8 %copy-start.1 = (s32[1,4,512]{2,1,0:T(4,128)S(1)}, s32[1,4,512]{2,1,0:T(4,128)}, u32[]{:S(2)}) copy-start(s32[1,4,512]{2,1,0:T(4,128)} %param.16) | copy-start | bytes 24580
  0.6 13.2 %copy-start.2 = (s32[1,4]{1,0:T(1,128)S(1)}, s32[1,4]{1,0:T(1,128)}, u32[]{:S(2)}) copy-start(s32[1,4]{1,0:T(1,128)} %param.15) | copy-start | bytes 52
  0.7 13.8 %copy-start.7 = (s32[1,2]{1,0:T(1,128)S(1)}, s32[1,2]{1,0:T(1,128)}, u32[]{:S(2)}) copy-start(s32[1,2]{1,0:T(1,128)} %param.18) | copy-start | bytes 28
  0.7 15.3 %copy-start.5 = (s32[1,4,8]{2,1,0:T(4,128)S(1)}, s32[1,4,8]{2,1,0:T(4,128)}, u32[]{:S(2)}) copy-start(s32[1,4,8]{2,1,0:T(4,128)} %param.21) | copy-start | bytes 388
  10.8 9.3 %collective-permute-start = (f32[7,512]{0,1:T(8,128)S(1)}, f32[7,512]{0,1:T(8,128)S(1)}, u32[]{:S(2)}, u32[]{:S(2)}) collective-permute-start(f32[7,512]{0,1:T(8,128)S(1)} %bitcast.228), channel_id=1, source_target_pairs={{0,8},{8,0},{4,12},{12,4},{16,24},{24,16},{20,28},{28,20},{1,9},{9... | collective-permute-start | bytes 43016 | tf_op jit(solution)/shard_map/ppermute | solution.py:23
  33.0 1.6 collective-permute-start.1
  33.7 43.1 %copy-start.6 = (s32[1,2,8]{2,1,0:T(2,128)S(1)}, s32[1,2,8]{2,1,0:T(2,128)}, u32[]{:S(2)}) copy-start(s32[1,2,8]{2,1,0:T(2,128)} %param.17) | copy-start | bytes 196
  47.4 15.1 %collective-permute-start.2 = (f32[7,512]{0,1:T(8,128)S(1)}, f32[7,512]{0,1:T(8,128)S(1)}, u32[]{:S(2)}, u32[]{:S(2)}) collective-permute-start(f32[7,512]{0,1:T(8,128)S(1)} %bitcast.231), channel_id=1, source_target_pairs={{0,2},{2,0},{1,3},{3,1},{4,6},{6,4},{5,7},{7,5},{8,10},{10,8},{9,1... | collective-permute-start | bytes 43016 | tf_op jit(solution)/shard_map/ppermute | solution.py:23
  75.3 7.8 %collective-permute-start.3 = (f32[7,512]{0,1:T(8,128)S(1)}, f32[7,512]{0,1:T(8,128)S(1)}, u32[]{:S(2)}, u32[]{:S(2)}) collective-permute-start(f32[7,512]{0,1:T(8,128)S(1)} %bitcast.229), channel_id=1, source_target_pairs={{0,1},{1,0},{2,3},{3,2},{4,5},{5,4},{6,7},{7,6},{8,9},{9,8},{10,11... | collective-permute-start | bytes 43016 | tf_op jit(solution)/shard_map/ppermute | solution.py:23
  77.5 26.8 %copy-start.4 = (s32[1,2,8,3]{2,1,3,0:T(2,128)S(1)}, s32[1,2,8,3]{2,1,3,0:T(2,128)}, u32[]{:S(2)}) copy-start(s32[1,2,8,3]{2,1,3,0:T(2,128)} %param.19) | copy-start | bytes 580
  77.5 27.4 %copy-start.3 = (s32[1,2,8,4]{2,3,1,0:T(4,128)S(1)}, s32[1,2,8,4]{2,3,1,0:T(4,128)}, u32[]{:S(2)}) copy-start(s32[1,2,8,4]{2,3,1,0:T(4,128)} %param.20) | copy-start | bytes 772
  98.3 21.5 %all-to-all-start = ((f32[4,8,6,128]{3,1,2,0:T(8,128)}), f32[4,8,6,128]{3,1,2,0:T(8,128)S(1)}, u32[]{:S(2)}, u32[]{:S(2)}) async-start(f32[4,8,6,128]{3,1,2,0:T(8,128)} %copy.78), calls=%async_computation | async-start | bytes 196608 | tf_op jit(solution)/shard_map/all_to_all | solution.py:118
  175.4 108.4 %copy-start = (f32[128,128]{1,0:T(8,128)}, f32[128,128]{1,0:T(8,128)S(1)}, u32[]{:S(2)}) copy-start(f32[128,128]{1,0:T(8,128)S(1)} %scatter_custom_fusion.4) | copy-start | bytes 196612
  178.1 11.0 %all-to-all-start.1 = ((f32[4,8,7,128]{3,1,2,0:T(8,128)}), f32[4,8,7,128]{3,1,2,0:T(8,128)S(1)}, u32[]{:S(2)}, u32[]{:S(2)}) async-start(f32[4,8,7,128]{3,1,2,0:T(8,128)} %copy.64), calls=%async_computation.1 | async-start | bytes 229376 | tf_op jit(solution)/shard_map/all_to_all | solution.py:139
  272.4 8.9 %all-to-all-start.2 = ((f32[4,8,3,128]{3,1,2,0:T(8,128)}), f32[4,8,3,128]{3,1,2,0:T(8,128)S(1)}, u32[]{:S(2)}, u32[]{:S(2)}) async-start(f32[4,8,3,128]{3,1,2,0:T(8,128)} %copy.67), calls=%async_computation.2 | async-start | bytes 98304 | tf_op jit(solution)/shard_map/all_to_all | solution.py:150
where the time goes:
time: 285 us; the launch traced here: 284 us
  local copies, waits for them, and re-layouts  100 us (35%)
  other arithmetic  74.3 us (26%)
  loops' own time  58.2 us (20%)
  waiting for transfers between devices  29.7 us (10%)
  starting transfers between devices  20.4 us (7%)
    scatter x4, other arithmetic, settle(): current.at[:, moving_rows]  33.6 us
    another operation x1, loops' own time, slot_forces(): return lax.map(per_slot, (slot_ids, near_ids, far_ids, live_slot))  33.3 us
    another operation x1, loops' own time, slot_densities(): return lax.map(per_slot, (slot_ids, near_ids, far_ids))  25 us
    ppermute x4, waiting for transfers between devices, swapped(): return lax.ppermute(block, axis, route)  21.6 us
    gather x4, local copies, waits for them, and re-layouts, shards(): outgoing = current[:, moving_rows]  17.6 us
    dynamic_slice x24, local copies, waits for them, and re-layouts, slot_densities(): return lax.map(per_slot, (slot_ids, near_ids, far_ids))  14.1 us
    gather x24, local copies, waits for them, and re-layouts, per_slot(): neighbours = jnp.concatenate([own_blocks[near], ghosts[far]], axis=0)  13.2 us
    unnamed x19, local copies, waits for them, and re-layouts  11.6 us
  transfers between devices with their start and end apart: 7, of which 6 were waited for; matrix products, arithmetic and copies ran while one was open for 9% of the time, Pallas kernels for 0%

commit v1 on v0

v1 whole, which is shorter than its diff:
```python
import math

import jax
import jax.numpy as jnp
from jax import lax
from jax.experimental import pallas as pl
from jax.experimental.pallas import tpu as pltpu
from jax.sharding import PartitionSpec as P

BLK = 128
TOTACT = 12
KERNEL_NORM = 21.0 / (16.0 * math.pi)
FORCE_NORM = 5.0 * KERNEL_NORM * 32.0 * (2.0 / 3.0)
TINY = 1e-30
F32 = jnp.float32
I32 = jnp.int32
VMEM = pltpu.VMEM
SMEM = pltpu.SMEM


def call(kernel, out_shape, *args, smem=(), scratch=(), limit=16 << 20):
    in_specs = [pl.BlockSpec(memory_space=SMEM if n in smem else VMEM) for n in range(len(args))]
    return pl.pallas_call(
        kernel,
        out_shape=out_shape,
        in_specs=in_specs,
        out_specs=jax.tree.map(lambda _: pl.BlockSpec(memory_space=VMEM), out_shape),
        scratch_shapes=list(scratch),
        compiler_params=pltpu.CompilerParams(vmem_limit_bytes=limit),
    )(*args)


def shape(*dims, dtype=F32):
    return jax.ShapeDtypeStruct(dims, dtype)


def wide(row):
    return jnp.broadcast_to(row, (8, BLK))


def lanes(block):
    return pl.ds(pl.multiple_of(block * BLK, BLK), BLK)


def chunk(c):
    return slice(c * BLK, (c + 1) * BLK)


def take(values, index):
    return jnp.take_along_axis(values, index, axis=1)


def patch(values, code, tables):
    lane = code & (BLK - 1)
    which = code >> 7
    for n, table in enumerate(tables):
        values = jnp.where(which == n, take(table, lane), values)
    return values


def tables_of(ref, count, start=0):
    return [ref[:, chunk(start + c)] for c in range(count)]


def columns(state, slots):
    block = slots >> 7
    lane = slots & (BLK - 1)
    found = jnp.zeros((8, BLK), F32)
    for b in range(state.shape[1] // BLK):
        found = jnp.where(block == b, take(state[:, chunk(b)], lane), found)
    return found


def load_state(state, particles):
    state[0:7, :] = particles[...]
    state[7:8, :] = jnp.zeros((1, state.shape[1]), F32)


def first_kernel(particles, rows, out, state):
    load_state(state, particles)
    for c in range(rows.shape[1] // BLK):
        out[:, chunk(c)] = columns(state, wide(rows[0:1, chunk(c)]))


def code_table(rows, counts, level, blocks):
    mig = rows.shape[1]
    slots = rows[level : level + 1, :]
    k = lax.broadcasted_iota(I32, (1, mig), 1)
    live = k < counts[0:1, level : level + 1]
    low = jnp.where(live, k & (BLK - 1), 0).astype(F32)
    high = jnp.where(live, (k >> 7) + 1, 0).astype(F32)
    in_block = lax.broadcasted_iota(I32, (blocks, mig), 0) == (slots >> 7)
    in_lane = lax.broadcasted_iota(I32, (BLK, mig), 0) == (slots & (BLK - 1))
    left = jnp.concatenate([jnp.where(in_block, low, 0.0), jnp.where(in_block, high, 0.0)], axis=0)
    right = jnp.where(in_lane, 1.0, 0.0)
    both = lax.dot_general(
        left.astype(jnp.bfloat16),
        right.astype(jnp.bfloat16),
        (((1,), (1,)), ((), ())),
        preferred_element_type=F32,
    )
    low, high = both[:blocks], both[blocks:]
    return jnp.where(high > 0.5, (high - 1.0) * BLK + low, -1.0).astype(I32)


def code_at(table, slots):
    block = slots >> 7
    lane = slots & (BLK - 1)
    row = lax.broadcasted_iota(I32, (8, BLK), 0)
    found = jnp.full((8, BLK), -1, I32)
    for v in range(table.shape[0] // 8):
        piece = take(table[8 * v : 8 * v + 8, :], lane)
        found = jnp.where(block == row + 8 * v, piece, found)
    return jnp.max(found, axis=0, keepdims=True)


def tables_kernel(particles, rows, counts, cols, marks, early, late, state):
    mig = rows.shape[1]
    blocks = early.shape[0]
    load_state(state, particles)
    code0 = code_table(rows, counts, 0, blocks)
    code1 = code_table(rows, counts, 1, blocks)
    code2 = code_table(rows, counts, 2, blocks)
    code3 = code_table(rows, counts, 3, blocks)
    early[...] = jnp.where(code1 >= 0, code1 + mig, code0)
    late[...] = jnp.where(code3 >= 0, code3 + mig, code2)
    for c in range(mig // BLK):
        slots = [wide(rows[level : level + 1, chunk(c)]) for level in range(4)]
        marks[0:1, chunk(c)] = code_at(code0, slots[1])
        marks[1:2, chunk(c)] = code_at(early, slots[2])
        marks[2:3, chunk(c)] = code_at(early, slots[3])
        marks[3:4, chunk(c)] = code_at(code2, slots[3])
        for level in (1, 2, 3):
            cols[level - 1, :, chunk(c)] = columns(state, slots[level])


def second_kernel(cols, marks, got0, out):
    count = got0.shape[1] // BLK
    for c in range(count):
        out[:, chunk(c)] = patch(
            cols[0, :, chunk(c)], wide(marks[0:1, chunk(c)]), tables_of(got0, count)
        )


def make_export_kernel(peers, slots, meta_exports):
    def export_kernel(meta, particles, cols, marks, got0, got1, early, late, *outs):
        count = got0.shape[1] // BLK
        tables = tables_of(got0, count) + tables_of(got1, count)
        row = lax.broadcasted_iota(I32, (8, BLK), 0)
        for c in range(count):
            two = patch(cols[1, :, chunk(c)], wide(marks[1:2, chunk(c)]), tables)
            three = patch(cols[2, :, chunk(c)], wide(marks[2:3, chunk(c)]), tables)
            three = jnp.where(row == 7, wide(marks[3:4, chunk(c)]).astype(F32), three)
            for out in outs:
                out[:, chunk(c)] = two
                out[:, chunk(count + c)] = three
        me = meta[0]
        for q, out in enumerate(outs):
            for t in range(slots):
                block = meta[meta_exports + (me ^ q) * slots + t]
                out[:, chunk(2 * count + t)] = early_block(
                    particles, early, late, tables, block
                )

    return export_kernel


def early_block(particles, early, late, tables, block):
    values = jnp.concatenate(
        [particles[:, lanes(block)], late[pl.ds(block, 1), :].astype(F32)], axis=0
    )
    row = lax.broadcasted_iota(I32, (8, BLK), 0)
    patched = patch(values, wide(early[pl.ds(block, 1), :]), tables)
    return jnp.where(row == 7, values, patched)


def make_density_kernel(peers, slots, lay):
    def density_kernel(
        meta, particles, early, late, got0, got1, *refs
    ):
        sent = refs[:peers]
        near, density = refs[peers : peers + 2]
        exports = refs[peers + 2 : 2 * peers + 2]
        late_three, ghosts = refs[2 * peers + 2 :]
        count = got0.shape[1] // BLK
        blocks = density.shape[0]
        row = lax.broadcasted_iota(I32, (8, BLK), 0)
        me = meta[0]
        first = tables_of(got0, count) + tables_of(got1, count)

        for q in range(peers):
            tables = tables_of(sent[q ^ 2], count)
            for c in range(count):
                values = sent[q][:, chunk(count + c)]
                code = wide(values[7:8, :]).astype(I32)
                late_three[q, :, chunk(c)] = patch(values, code, tables)

        def settle(values, q):
            code = wide(values[7:8, :]).astype(I32)
            tables = tables_of(sent[q ^ 2], count)
            tables += [late_three[q ^ 1, :, chunk(c)] for c in range(count)]
            return patch(values, code, tables)

        for q in range(peers):
            for t in range(slots):
                ghosts[:, chunk(q * slots + t)] = settle(sent[q][:, chunk(2 * count + t)], q)

        last = [got0[6:7, chunk(c)] for c in range(count)]
        last += [got1[6:7, chunk(c)] for c in range(count)]
        later = [sent[2][6:7, chunk(c)] for c in range(count)]
        later += [late_three[1, 6:7, chunk(c)] for c in range(count)]
        for b in range(blocks):
            density[b : b + 1, :] = particles[6:7, chunk(b)]
        last = [wide(x) for x in last]
        later = [wide(x) for x in later]
        for v in range(blocks // 8):
            part = slice(8 * v, 8 * v + 8)
            values = patch(density[part, :], early[part, :], last)
            density[part, :] = patch(values, late[part, :], later)

        live = meta[1] + meta[2]

        def slot_of(n):
            return jnp.where(n < meta[1], n, n - meta[1] + lay["nact"])

        def gather_slot(n, _):
            s = slot_of(n)
            a = meta[lay["ids"] + s]
            near[n, :, 0, :] = settle(early_block(particles, early, late, first, a), 0)
            for t in range(lay["nloc"]):
                b = meta[lay["nbrs"] + s * lay["nloc"] + t]
                near[n, :, 1 + t, :] = settle(early_block(particles, early, late, first, b), 0)
            for t in range(lay["ngh"]):
                g = meta[lay["far"] + s * lay["ngh"] + t] ^ (me * slots)
                near[n, :, 1 + lay["nloc"] + t, :] = ghosts[:, lanes(g)]
            return 0

        lax.fori_loop(0, live, gather_slot, 0)

        def slot_density(n, _):
            a = meta[lay["ids"] + slot_of(n)]
            x, y, z, m = (near[n, q] for q in range(4))
            cx, cy, cz, h = (wide(near[n, q, 0:1, :]) for q in (0, 1, 2, 4))
            half = 0.5 / h
            sums = [jnp.zeros((8, BLK), F32) for _ in range(4)]
            for r in range(BLK):
                dx = cx - pltpu.roll(x, r, 1)
                dy = cy - pltpu.roll(y, r, 1)
                dz = cz - pltpu.roll(z, r, 1)
                square = dx * dx + dy * dy + dz * dz
                t = square * lax.rsqrt(jnp.maximum(square, TINY)) * half
                fall = jnp.maximum(1.0 - t, 0.0)
                fall = fall * fall
                sums[r % 4] += fall * fall * (1.0 + 4.0 * t) * pltpu.roll(m, r, 1)
            total = (sums[0] + sums[1]) + (sums[2] + sums[3])
            total = jnp.sum(total, axis=0, keepdims=True)
            h = h[0:1, :]
            density[pl.ds(a, 1), :] = total * (KERNEL_NORM / (h * h * h))
            return 0

        lax.fori_loop(0, live, slot_density, 0)

        for q in range(peers):
            for t in range(slots):
                b = meta[lay["exports"] + (me ^ q) * slots + t]
                exports[q][t : t + 1, :] = density[pl.ds(b, 1), :]

    return density_kernel


def make_force_kernel(peers, slots, lay):
    def force_kernel(meta, near, density, *refs):
        rho = refs[:peers]
        totals = refs[peers]
        returns = refs[peers + 1 : 2 * peers + 1]
        far_rho, work, back = refs[2 * peers + 1 :]
        me = meta[0]
        for q in range(peers):
            far_rho[q * slots : (q + 1) * slots, :] = rho[q][...]
        totals[...] = jnp.zeros_like(totals)
        back[...] = jnp.zeros_like(back)
        live = meta[1] + meta[2]

        def slot_force(n, _):
            s = jnp.where(n < meta[1], n, n - meta[1] + lay["nact"])
            a = meta[lay["ids"] + s]
            nbrs = [meta[lay["nbrs"] + s * lay["nloc"] + t] for t in range(lay["nloc"])]
            far = [
                meta[lay["far"] + s * lay["ngh"] + t] ^ (me * slots) for t in range(lay["ngh"])
            ]
            for t, b in enumerate([a] + nbrs):
                work[0, t : t + 1, :] = density[pl.ds(b, 1), :]
            for t, g in enumerate(far):
                work[0, 1 + len(nbrs) + t : 2 + len(nbrs) + t, :] = far_rho[pl.ds(g, 1), :]
            x, y, z, m, h, u = (near[n, q] for q in range(6))
            p = u / work[0]
            cx, cy, cz, cm, ch, cp = (wide(v[0:1, :]) for v in (x, y, z, m, h, p))
            centre = [jnp.zeros((8, BLK), F32) for _ in range(3)]
            others = [jnp.zeros((8, BLK), F32) for _ in range(3)]
            for r in range(BLK):
                d = [c - pltpu.roll(v, r, 1) for c, v in ((cx, x), (cy, y), (cz, z))]
                square = d[0] * d[0] + d[1] * d[1] + d[2] * d[2]
                inverse = 1.0 / (ch + pltpu.roll(h, r, 1))
                t = square * lax.rsqrt(jnp.maximum(square, TINY)) * inverse
                fall = jnp.maximum(1.0 - t, 0.0)
                inv2 = inverse * inverse
                weight = fall * fall * fall * (inv2 * inv2 * inverse)
                weight = weight * (cp + pltpu.roll(p, r, 1)) * (cm * pltpu.roll(m, r, 1))
                for k in range(3):
                    push = weight * d[k]
                    centre[k] = centre[k] + push
                    others[k] = others[k] + pltpu.roll(push, (BLK - r) % BLK, 1)
            scale_centre = FORCE_NORM / cm[0:1, :]
            scale_others = -FORCE_NORM / m
            for k in range(3):
                work[k] = others[k] * scale_others
            for k in range(3):
                work[k, 0:1, :] = jnp.sum(centre[k], axis=0, keepdims=True) * scale_centre
            for t, b in enumerate([a] + nbrs):
                totals[0:3, lanes(b)] += work[0:3, t, :]
            for t, g in enumerate(far):
                back[0:3, lanes(g)] += work[0:3, 1 + len(nbrs) + t, :]
            return 0

        lax.fori_loop(0, live, slot_force, 0)
        for q in range(peers):
            returns[q][...] = back[:, q * slots * BLK : (q + 1) * slots * BLK]

    return force_kernel


def make_final_kernel(peers, slots, lay):
    def final_kernel(meta, totals, *refs):
        got = refs[:peers]
        out, work = refs[peers:]
        me = meta[0]
        work[...] = totals[...]
        for q in range(peers):
            for t in range(slots):
                b = meta[lay["exports"] + (me ^ q) * slots + t]
                work[:, lanes(b)] += got[q][:, chunk(t)]
        out[...] = work[0:3, :]

    return final_kernel


def crossed(block, axis, bits):
    size = lax.axis_size(axis)
    return lax.ppermute(block, axis, [(i, i ^ bits) for i in range(size) if i ^ bits < size])


def shards(
    particles, mig_count, mig_rows, active_ids, active_count, local_nbrs, ghost_slots, export_blocks
):
    peers = lax.axis_size("gy")
    slots = export_blocks.shape[2]
    per_dev = particles.shape[1]
    blocks = per_dev // BLK
    mig = mig_rows.shape[2]
    rows = mig_rows[0]
    nact = active_ids.shape[2]
    total = active_ids.shape[1] * nact
    lay = {"nact": nact, "nloc": local_nbrs.shape[3], "ngh": ghost_slots.shape[3], "ids": 3}
    lay["nbrs"] = lay["ids"] + total
    lay["far"] = lay["nbrs"] + total * lay["nloc"]
    lay["exports"] = lay["far"] + total * lay["ngh"]
    meta = jnp.concatenate(
        [
            lax.axis_index("gy").astype(I32).reshape(1),
            active_count.reshape(-1),
            active_ids.reshape(-1),
            local_nbrs.reshape(-1),
            ghost_slots.reshape(-1),
            export_blocks.reshape(-1),
        ]
    )
    state = VMEM((8, per_dev), F32)
    sent0 = call(first_kernel, shape(8, mig), particles, rows, scratch=[state])
    got0 = crossed(sent0, "gx", 2)
    cols, marks, early, late = call(
        tables_kernel,
        [
            shape(3, 8, mig),
            shape(8, mig, dtype=I32),
            shape(blocks, BLK, dtype=I32),
            shape(blocks, BLK, dtype=I32),
        ],
        particles,
        rows,
        mig_count,
        scratch=[state],
    )
    sent1 = call(second_kernel, shape(8, mig), cols, marks, got0)
    got1 = crossed(sent1, "gx", 1)
    packs = call(
        make_export_kernel(peers, slots, lay["exports"]),
        [shape(8, 2 * mig + slots * BLK)] * peers,
        meta,
        particles,
        cols,
        marks,
        got0,
        got1,
        early,
        late,
        smem=(0,),
    )
    order = list(range(peers - 1, 0, -1))
    arrived = {q: crossed(packs[q], "gy", q) for q in order}
    sent = [packs[0]] + [arrived[q] for q in range(1, peers)]
    wide_total = peers * slots * BLK
    results = call(
        make_density_kernel(peers, slots, lay),
        [shape(TOTACT, 8, 8, BLK), shape(blocks, BLK)] + [shape(slots, BLK)] * peers,
        meta,
        particles,
        early,
        late,
        got0,
        got1,
        *sent,
        smem=(0,),
        scratch=[VMEM((peers, 8, mig), F32), VMEM((8, wide_total), F32)],
    )
    near, density, exports = results[0], results[1], results[2:]
    arrived = {q: crossed(exports[q], "gy", q) for q in order}
    rho = [exports[0]] + [arrived[q] for q in range(1, peers)]
    results = call(
        make_force_kernel(peers, slots, lay),
        [shape(8, per_dev)] + [shape(8, slots * BLK)] * peers,
        meta,
        near,
        density,
        *rho,
        smem=(0,),
        scratch=[VMEM((peers * slots, BLK), F32), VMEM((8, 8, BLK), F32), VMEM((8, wide_total), F32)],
    )
    totals, returns = results[0], results[1:]
    arrived = {q: crossed(returns[q], "gy", q) for q in order}
    got = [returns[0]] + [arrived[q] for q in range(1, peers)]
    accel = call(
        make_final_kernel(peers, slots, lay),
        shape(3, per_dev),
        meta,
        totals,
        *got,
        smem=(0,),
        scratch=[state],
    )
    return density.reshape(-1), accel


def solution(mesh):
    both = ("gx", "gy")
    placed = (
        P(None, both),
        P(both, None),
        P(both, None, None),
        P(both, None, None),
        P(both, None),
        P(both, None, None, None),
        P(both, None, None, None),
        P(both, None, None),
    )
    return jax.shard_map(
        shards,
        mesh=mesh,
        in_specs=placed,
        out_specs=(P(both), P(None, both)),
        check_vma=False,
    )
```

time: 285 us -> 173 us (0.61)
  Pallas kernels: 0 us -> 139 us
  local copies, waits for them, and re-layouts: 100 us -> 5.01 us
  other arithmetic: 74.3 us -> 0 us
  loops' own time: 58.2 us -> 0 us
  waiting for transfers between devices: 29.7 us -> 9.78 us
  starting transfers between devices: 20.4 us -> 16.3 us
    pallas_call x0 -> x7, Pallas kernels: none -> 139 us  [call(): pl.pallas_call(kernel, out_shape=out_shape, in_specs=in_specs, out_specs=...]
    another operation x2 -> x0, loops' own time: 58.2 us -> none  [the longest x1 33.3 us: slot_forces(): return lax.map(per_slot, (slot_ids, near_ids, far_ids, live_slot))]
    gather x58 -> x0, local copies, waits for them, and re-layouts: 47.7 us -> none  [the longest x4 17.6 us: shards(): outgoing = current[:, moving_rows]]
    scatter x5 -> x0, other arithmetic: 34.5 us -> none  [the longest x4 33.6 us: settle(): current.at[:, moving_rows]]
    dynamic_slice x60 -> x0, local copies, waits for them, and re-layouts: 21.4 us -> none  [the longest x24 14.1 us: slot_densities(): return lax.map(per_slot, (slot_ids, near_ids, far_ids))]
    reduce_sum x72 -> x0, other arithmetic: 18.8 us -> none  [the longest x24 7.25 us: pair_force(): return (jnp.sum(pushes, axis=2), -jnp.sum(pushes, axis=1))]
    all_to_all x3 -> x0, starting transfers between devices: 13.7 us -> none  [the longest x1 5.3 us: shards(): lax.all_to_all(sendable[:, :, 0:6], 'gy', split_axis=0, concat_axis=0, ti...]
    ppermute x4 -> x11, waiting for transfers between devices: 21.6 us -> 9.78 us  [crossed(): lax.ppermute(block, axis, [(i, i ^ bits) for i in range(size) if i ^ bits...]
  transfers between devices with their start and end apart: 7 -> 11, of which waited for: 6 -> 7; matrix products, arithmetic and copies ran while one was open for 9% -> 0% of each run, Pallas kernels for 0% -> 1%
where the time goes in v1:
time: 173 us; the launch traced here: 171 us
  Pallas kernels  139 us (80%)
  starting transfers between devices  16.3 us (9%)
  waiting for transfers between devices  9.78 us (6%)
  local copies, waits for them, and re-layouts  5.01 us (3%)
    pallas_call x7, Pallas kernels, call(): pl.pallas_call(kernel, out_shape=out_shape, in_specs=in_specs, out_specs=...  139 us
    ppermute x11, starting transfers between devices, crossed(): lax.ppermute(block, axis, [(i, i ^ bits) for i in range(size) if i ^ bits...  16.3 us
    ppermute x11, waiting for transfers between devices, crossed(): lax.ppermute(block, axis, [(i, i ^ bits) for i in range(size) if i ^ bits...  9.78 us
    unnamed x22, local copies, waits for them, and re-layouts  4.6 us
  transfers between devices with their start and end apart: 11, of which 7 were waited for; matrix products, arithmetic and copies ran while one was open for 0% of the time, Pallas kernels for 1%

profile of v1, /device:TPU:0, one launch (start us, length us, event | category | flops | bytes accessed | tf_op | source)
XLA Modules:
  0.0 170.8 jit_solution(11977400616765709538)
XLA Ops:
  0.6 1.0 copy-done
  1.7 0.7 copy-done.3
  2.4 0.6 shard_map.96
  3.0 3.0 %collective-permute-start = (f32[8,512]{1,0:T(8,128)S(1)}, f32[8,512]{1,0:T(8,128)S(1)}, u32[]{:S(2)}, u32[]{:S(2)}) collective-permute-start(f32[8,512]{1,0:T(8,128)S(1)} %shard_map.96), channel_id=1, source_target_pairs={{0,8},{4,12},{8,0},{12,4},{16,24},{20,28},{24,16},{28,20},{1,9},{5... | collective-permute-start | bytes 49160 | tf_op jit(solution)/shard_map/ppermute | solution.py:349
  6.0 2.2 %shard_map.95 = (f32[3,8,512]{2,1,0:T(8,128)S(1)}, s32[8,512]{1,0:T(8,128)S(1)}, s32[128,128]{1,0:T(8,128)S(1)}, s32[128,128]{1,0:T(8,128)S(1)}) custom-call(f32[7,16384]{1,0:T(8,128)S(1)} %copy-done, s32[4,512]{1,0:T(4,128)S(1)} %bitcast.10, s32[1,4]{1,0:T(1,128)S(1)} %copy-done.4), custom_call_target="tpu_custom_call" | custom-call | tf_op jit(solution)/shard_map/pallas_call | solution.py:23
  8.2 0.1 shard_map.97
  8.5 0.5 copy-done.9
  9.0 0.1 copy-done.7
  9.2 0.1 copy.12
  9.3 0.1 reshape.28
  9.4 0.6 copy-done.5
  10.0 0.1 copy.13
  10.1 0.1 reshape.29
  10.2 0.6 copy-done.8
  10.9 1.1 shard_map.98
  12.0 1.7 collective-permute-start.2
  13.7 2.6 %collective-permute-start.3 = (f32[8,2048]{1,0:T(8,128)S(1)}, f32[8,2048]{1,0:T(8,128)S(1)}, u32[]{:S(2)}, u32[]{:S(2)}) collective-permute-start(f32[8,2048]{1,0:T(8,128)S(1)} %get-tuple-element.27), channel_id=1, source_target_pairs={{0,2},{1,3},{2,0},{3,1},{4,6},{5,7},{6,4},{7,5},{8,10},{9,11},{10,... | collective-permute-start | bytes 196616 | tf_op jit(solution)/shard_map/ppermute | solution.py:349
  16.2 0.2 collective-permute-start.4
  16.4 0.1 collective-permute-done.2.refs_1_
  16.5 4.1 %collective-permute-done.3.refs_2_ = f32[8,2048]{1,0:T(8,128)S(1)} collective-permute-done((f32[8,2048]{1,0:T(8,128)S(1)}, f32[8,2048]{1,0:T(8,128)S(1)}, u32[]{:S(2)}, u32[]{:S(2)}) %collective-permute-start.3) | collective-permute-done | bytes 65568 | tf_op jit(solution)/shard_map/ppermute | solution.py:349
  20.6 1.7 %collective-permute-done.4.refs_3_ = f32[8,2048]{1,0:T(8,128)S(1)} collective-permute-done((f32[8,2048]{1,0:T(8,128)S(1)}, f32[8,2048]{1,0:T(8,128)S(1)}, u32[]{:S(2)}, u32[]{:S(2)}) %collective-permute-start.4) | collective-permute-done | bytes 65568 | tf_op jit(solution)/shard_map/ppermute | solution.py:349
  22.4 12.7 %shard_map.99 = (f32[12,8,8,128]{3,2,1,0:T(8,128)S(1)}, f32[128,128]{1,0:T(8,128)}, f32[8,128]{1,0:T(8,128)S(1)}, f32[8,128]{1,0:T(8,128)S(1)}, f32[8,128]{1,0:T(8,128)S(1)}, /*index=5*/f32[8,128]{1,0:T(8,128)S(1)}) custom-call(s32[163]{0:T(256)S(1)} %concatenate.3.meta, f32[7,16384]{1,0:T(8,128)S(1)} %copy-done.1, s32[128,128]{1,0:T(8,128)S(1)} %get-tuple-element.21.early, ...), custom_call_target="tpu_custom_call" | custom-call | tf_op jit(solution)/shard_map/pallas_call | solution.py:23
  35.1 0.4 collective-permute-start.6
  35.5 4.0 %collective-permute-start.7 = (f32[8,128]{1,0:T(8,128)S(1)}, f32[8,128]{1,0:T(8,128)S(1)}, u32[]{:S(2)}, u32[]{:S(2)}) collective-permute-start(f32[8,128]{1,0:T(8,128)S(1)} %get-tuple-element.34), channel_id=1, source_target_pairs={{0,3},{1,2},{2,1},{3,0},{4,7},{5,6},{6,5},{7,4},{8,11},{9,10},{10,... | collective-permute-start | bytes 12296 | tf_op jit(solution)/shard_map/ppermute | solution.py:349
  39.5 0.1 collective-permute-done.6.refs_2_
  39.6 1.5 collective-permute-done.7.refs_3_
  41.1 0.8 copy-done.2
  42.0 120.7 %shard_map.100 = (f32[8,16384]{1,0:T(8,128)S(1)}, f32[8,1024]{1,0:T(8,128)S(1)}, f32[8,1024]{1,0:T(8,128)S(1)}, f32[8,1024]{1,0:T(8,128)S(1)}, f32[8,1024]{1,0:T(8,128)S(1)}) custom-call(s32[163]{0:T(256)S(1)} %concatenate.3.meta, f32[12,8,8,128]{3,2,1,0:T(8,128)S(1)} %get-tuple-element.30.near, f32[128,128]{1,0:T(8,128)S(1)} %copy-done.2, ...), custom_call_target="tpu_custom_call" | custom-call | tf_op jit(solution)/shard_map/pallas_call | solution.py:23
  162.9 4.3 %collective-permute-start.10 = (f32[8,1024]{1,0:T(8,128)S(1)}, f32[8,1024]{1,0:T(8,128)S(1)}, u32[]{:S(2)}, u32[]{:S(2)}) collective-permute-start(f32[8,1024]{1,0:T(8,128)S(1)} %get-tuple-element.39), channel_id=1, source_target_pairs={{0,3},{1,2},{2,1},{3,0},{4,7},{5,6},{6,5},{7,4},{8,11},{9,10},{10,... | collective-permute-start | bytes 98312 | tf_op jit(solution)/shard_map/ppermute | solution.py:349
  167.2 0.5 collective-permute-done.9.refs_2_
  167.7 1.7 %collective-permute-done.10.refs_3_ = f32[8,1024]{1,0:T(8,128)S(1)} collective-permute-done((f32[8,1024]{1,0:T(8,128)S(1)}, f32[8,1024]{1,0:T(8,128)S(1)}, u32[]{:S(2)}, u32[]{:S(2)}) %collective-permute-start.10) | collective-permute-done | bytes 32800 | tf_op jit(solution)/shard_map/ppermute | solution.py:349
  169.4 1.4 shard_map.101
  (24 shorter events, 0.5 us)
Async XLA Ops:
  0.6 1.0 copy-start
  1.7 0.7 copy-start.3
  2.4 3.6 %copy-start.4 = (s32[1,4]{1,0:T(1,128)S(1)}, s32[1,4]{1,0:T(1,128)}, u32[]{:S(2)}) copy-start(s32[1,4]{1,0:T(1,128)} %counts.1) | copy-start | bytes 52
  2.4 8.5 %copy-start.1 = (f32[7,16384]{1,0:T(8,128)S(1)}, f32[7,16384]{1,0:T(8,128)}, u32[]{:S(2)}) copy-start(f32[7,16384]{1,0:T(8,128)} %particles.7) | copy-start | bytes 1376260
  3.0 5.2 %collective-permute-start = (f32[8,512]{1,0:T(8,128)S(1)}, f32[8,512]{1,0:T(8,128)S(1)}, u32[]{:S(2)}, u32[]{:S(2)}) collective-permute-start(f32[8,512]{1,0:T(8,128)S(1)} %shard_map.96), channel_id=1, source_target_pairs={{0,8},{4,12},{8,0},{12,4},{16,24},{20,28},{24,16},{28,20},{1,9},{5... | collective-permute-start | bytes 49160 | tf_op jit(solution)/shard_map/ppermute | solution.py:349
  8.2 0.7 copy-start.9
  8.3 2.5 %collective-permute-start.1 = (f32[8,512]{1,0:T(8,128)S(1)}, f32[8,512]{1,0:T(8,128)S(1)}, u32[]{:S(2)}, u32[]{:S(2)}) collective-permute-start(f32[8,512]{1,0:T(8,128)S(1)} %shard_map.97), channel_id=1, source_target_pairs={{0,4},{4,0},{8,12},{12,8},{16,20},{20,16},{24,28},{28,24},{1,5},{5... | collective-permute-start | bytes 49160 | tf_op jit(solution)/shard_map/ppermute | solution.py:349
  8.4 0.7 copy-start.7
  8.4 0.8 copy-start.6
  9.3 0.7 copy-start.5
  10.2 0.7 copy-start.8
  12.0 4.6 %collective-permute-start.2 = (f32[8,2048]{1,0:T(8,128)S(1)}, f32[8,2048]{1,0:T(8,128)S(1)}, u32[]{:S(2)}, u32[]{:S(2)}) collective-permute-start(f32[8,2048]{1,0:T(8,128)S(1)} %get-tuple-element.26), channel_id=1, source_target_pairs={{0,1},{1,0},{2,3},{3,2},{4,5},{5,4},{6,7},{7,6},{8,9},{9,8},{10,11... | collective-permute-start | bytes 196616 | tf_op jit(solution)/shard_map/ppermute | solution.py:349
  13.7 7.0 %collective-permute-start.3 = (f32[8,2048]{1,0:T(8,128)S(1)}, f32[8,2048]{1,0:T(8,128)S(1)}, u32[]{:S(2)}, u32[]{:S(2)}) collective-permute-start(f32[8,2048]{1,0:T(8,128)S(1)} %get-tuple-element.27), channel_id=1, source_target_pairs={{0,2},{1,3},{2,0},{3,1},{4,6},{5,7},{6,4},{7,5},{8,10},{9,11},{10,... | collective-permute-start | bytes 196616 | tf_op jit(solution)/shard_map/ppermute | solution.py:349
  16.2 6.1 %collective-permute-start.4 = (f32[8,2048]{1,0:T(8,128)S(1)}, f32[8,2048]{1,0:T(8,128)S(1)}, u32[]{:S(2)}, u32[]{:S(2)}) collective-permute-start(f32[8,2048]{1,0:T(8,128)S(1)} %get-tuple-element.28), channel_id=1, source_target_pairs={{0,3},{1,2},{2,1},{3,0},{4,7},{5,6},{6,5},{7,4},{8,11},{9,10},{10,... | collective-permute-start | bytes 196616 | tf_op jit(solution)/shard_map/ppermute | solution.py:349
  35.1 4.4 %collective-permute-start.5 = (f32[8,128]{1,0:T(8,128)S(1)}, f32[8,128]{1,0:T(8,128)S(1)}, u32[]{:S(2)}, u32[]{:S(2)}) collective-permute-start(f32[8,128]{1,0:T(8,128)S(1)} %get-tuple-element.32), channel_id=1, source_target_pairs={{0,1},{1,0},{2,3},{3,2},{4,5},{5,4},{6,7},{7,6},{8,9},{9,8},{10,11... | collective-permute-start | bytes 12296 | tf_op jit(solution)/shard_map/ppermute | solution.py:349
  35.1 4.5 %collective-permute-start.6 = (f32[8,128]{1,0:T(8,128)S(1)}, f32[8,128]{1,0:T(8,128)S(1)}, u32[]{:S(2)}, u32[]{:S(2)}) collective-permute-start(f32[8,128]{1,0:T(8,128)S(1)} %get-tuple-element.33), channel_id=1, source_target_pairs={{0,2},{1,3},{2,0},{3,1},{4,6},{5,7},{6,4},{7,5},{8,10},{9,11},{10,... | collective-permute-start | bytes 12296 | tf_op jit(solution)/shard_map/ppermute | solution.py:349
  35.5 5.6 %collective-permute-start.7 = (f32[8,128]{1,0:T(8,128)S(1)}, f32[8,128]{1,0:T(8,128)S(1)}, u32[]{:S(2)}, u32[]{:S(2)}) collective-permute-start(f32[8,128]{1,0:T(8,128)S(1)} %get-tuple-element.34), channel_id=1, source_target_pairs={{0,3},{1,2},{2,1},{3,0},{4,7},{5,6},{6,5},{7,4},{8,11},{9,10},{10,... | collective-permute-start | bytes 12296 | tf_op jit(solution)/shard_map/ppermute | solution.py:349
  41.1 0.8 copy-start.2
  162.7 4.5 %collective-permute-start.8 = (f32[8,1024]{1,0:T(8,128)S(1)}, f32[8,1024]{1,0:T(8,128)S(1)}, u32[]{:S(2)}, u32[]{:S(2)}) collective-permute-start(f32[8,1024]{1,0:T(8,128)S(1)} %get-tuple-element.37), channel_id=1, source_target_pairs={{0,1},{1,0},{2,3},{3,2},{4,5},{5,4},{6,7},{7,6},{8,9},{9,8},{10,11... | collective-permute-start | bytes 98312 | tf_op jit(solution)/shard_map/ppermute | solution.py:349
  162.8 4.9 %collective-permute-start.9 = (f32[8,1024]{1,0:T(8,128)S(1)}, f32[8,1024]{1,0:T(8,128)S(1)}, u32[]{:S(2)}, u32[]{:S(2)}) collective-permute-start(f32[8,1024]{1,0:T(8,128)S(1)} %get-tuple-element.38), channel_id=1, source_target_pairs={{0,2},{1,3},{2,0},{3,1},{4,6},{5,7},{6,4},{7,5},{8,10},{9,11},{10,... | collective-permute-start | bytes 98312 | tf_op jit(solution)/shard_map/ppermute | solution.py:349
  162.9 6.5 %collective-permute-start.10 = (f32[8,1024]{1,0:T(8,128)S(1)}, f32[8,1024]{1,0:T(8,128)S(1)}, u32[]{:S(2)}, u32[]{:S(2)}) collective-permute-start(f32[8,1024]{1,0:T(8,128)S(1)} %get-tuple-element.39), channel_id=1, source_target_pairs={{0,3},{1,2},{2,1},{3,0},{4,7},{5,6},{6,5},{7,4},{8,11},{9,10},{10,... | collective-permute-start | bytes 98312 | tf_op jit(solution)/shard_map/ppermute | solution.py:349

commit v2 on v1

v2 whole, which is shorter than its diff:
```python
import math

import jax
import jax.numpy as jnp
from jax import lax
from jax.experimental import pallas as pl
from jax.experimental.pallas import tpu as pltpu
from jax.sharding import PartitionSpec as P

BLK = 128
TOTACT = 12
KERNEL_NORM = 21.0 / (16.0 * math.pi)
FORCE_NORM = 5.0 * KERNEL_NORM * 32.0 * (2.0 / 3.0)
TINY = 1e-30
F32 = jnp.float32
I32 = jnp.int32
VMEM = pltpu.VMEM
SMEM = pltpu.SMEM
HBM = pltpu.HBM
DMA = pltpu.SemaphoreType.DMA


def call(kernel, out_shape, *args, smem=(), hbm=(), scratch=(), limit=16 << 20):
    def space(n):
        return SMEM if n in smem else HBM if n in hbm else VMEM

    return pl.pallas_call(
        kernel,
        out_shape=out_shape,
        in_specs=[pl.BlockSpec(memory_space=space(n)) for n in range(len(args))],
        out_specs=jax.tree.map(lambda _: pl.BlockSpec(memory_space=VMEM), out_shape),
        scratch_shapes=list(scratch),
        compiler_params=pltpu.CompilerParams(vmem_limit_bytes=limit),
    )(*args)


def shape(*dims, dtype=F32):
    return jax.ShapeDtypeStruct(dims, dtype)


def wide(row):
    return jnp.broadcast_to(row, (8, BLK))


def lanes(block):
    return pl.ds(pl.multiple_of(block * BLK, BLK), BLK)


def chunk(c):
    return slice(c * BLK, (c + 1) * BLK)


def take(values, index):
    return jnp.take_along_axis(values, index, axis=1)


def patch(values, code, tables):
    lane = code & (BLK - 1)
    which = code >> 7
    for n, table in enumerate(tables):
        values = jnp.where(which == n, take(table, lane), values)
    return values


def tables_of(ref, count, start=0):
    return [ref[:, chunk(start + c)] for c in range(count)]


def columns(state, slots):
    block = slots >> 7
    lane = slots & (BLK - 1)
    found = jnp.zeros((8, BLK), F32)
    for b in range(state.shape[1] // BLK):
        found = jnp.where(block == b, take(state[:, chunk(b)], lane), found)
    return found


def fetch(sources, targets, sems):
    copies = [
        pltpu.make_async_copy(a, b, sems.at[n]) for n, (a, b) in enumerate(zip(sources, targets))
    ]
    for copy in copies:
        copy.start()
    return copies


def fetch_scratch(arrays):
    return [SMEM(a.shape, I32) for a in arrays] + [DMA((len(arrays),))]


PIECES = 4


def first_kernel(particles, mig_rows, out, state, rows, sems):
    per_dev = particles.shape[1]
    size = per_dev // PIECES
    mig = mig_rows.shape[2]
    index_copy = pltpu.make_async_copy(mig_rows.at[0], rows, sems.at[PIECES])
    index_copy.start()
    copies = []
    for p in range(PIECES):
        part = slice(p * size, (p + 1) * size)
        copy = pltpu.make_async_copy(
            particles.at[:, part], state.at[pl.ds(0, 7), part], sems.at[p]
        )
        copy.start()
        copies.append(copy)
    index_copy.wait()
    slots = [wide(rows[0:1, chunk(c)]) for c in range(mig // BLK)]
    found = [jnp.zeros((8, BLK), F32) for _ in slots]
    for p, copy in enumerate(copies):
        copy.wait()
        for b in range(p * size // BLK, (p + 1) * size // BLK):
            values = state[:, chunk(b)]
            for c, s in enumerate(slots):
                picked = take(values, s & (BLK - 1))
                found[c] = jnp.where((s >> 7) == b, picked, found[c])
    for c, values in enumerate(found):
        out[:, chunk(c)] = values


def code_table(rows, counts, level, blocks):
    mig = rows.shape[1]
    slots = rows[level : level + 1, :]
    k = lax.broadcasted_iota(I32, (1, mig), 1)
    live = k < counts[0:1, level : level + 1]
    low = jnp.where(live, k & (BLK - 1), 0).astype(F32)
    high = jnp.where(live, (k >> 7) + 1, 0).astype(F32)
    in_block = lax.broadcasted_iota(I32, (blocks, mig), 0) == (slots >> 7)
    in_lane = lax.broadcasted_iota(I32, (BLK, mig), 0) == (slots & (BLK - 1))
    left = jnp.concatenate([jnp.where(in_block, low, 0.0), jnp.where(in_block, high, 0.0)], axis=0)
    right = jnp.where(in_lane, 1.0, 0.0)
    both = lax.dot_general(
        left.astype(jnp.bfloat16),
        right.astype(jnp.bfloat16),
        (((1,), (1,)), ((), ())),
        preferred_element_type=F32,
    )
    low, high = both[:blocks], both[blocks:]
    return jnp.where(high > 0.5, (high - 1.0) * BLK + low, -1.0).astype(I32)


def code_at(table, slots):
    block = slots >> 7
    lane = slots & (BLK - 1)
    row = lax.broadcasted_iota(I32, (8, BLK), 0)
    found = jnp.full((8, BLK), -1, I32)
    for v in range(table.shape[0] // 8):
        piece = take(table[8 * v : 8 * v + 8, :], lane)
        found = jnp.where(block == row + 8 * v, piece, found)
    return jnp.max(found, axis=0, keepdims=True)


def early_tables_kernel(state, rows, counts, cols, marks, codes):
    mig = rows.shape[1]
    blocks = codes.shape[1]
    for level in range(2):
        codes[level] = code_table(rows, counts, level, blocks)
    for c in range(mig // BLK):
        slots = wide(rows[1:2, chunk(c)])
        marks[0:1, chunk(c)] = code_at(codes.at[0], slots)
        cols[:, chunk(c)] = columns(state, slots)


def late_tables_kernel(state, rows, counts, codes, after, cols, marks, early, late):
    mig = rows.shape[1]
    blocks = codes.shape[1]
    code2 = code_table(rows, counts, 2, blocks)
    code3 = code_table(rows, counts, 3, blocks)
    early[...] = jnp.where(codes[1] >= 0, codes[1] + mig, codes[0])
    late[...] = jnp.where(code3 >= 0, code3 + mig, code2)
    for c in range(mig // BLK):
        two, three = (wide(rows[level : level + 1, chunk(c)]) for level in (2, 3))
        marks[1:2, chunk(c)] = code_at(early, two)
        marks[2:3, chunk(c)] = code_at(early, three)
        marks[3:4, chunk(c)] = code_at(code2, three)
        cols[0, :, chunk(c)] = columns(state, two)
        cols[1, :, chunk(c)] = columns(state, three)


def second_kernel(cols, marks, got0, out):
    count = got0.shape[1] // BLK
    tables = tables_of(got0, count)
    for c in range(count):
        out[:, chunk(c)] = patch(cols[:, chunk(c)], wide(marks[0:1, chunk(c)]), tables)


def early_block(state, early, late, tables, block):
    row = lax.broadcasted_iota(I32, (8, BLK), 0)
    patched = patch(state[:, lanes(block)], wide(early[pl.ds(block, 1), :]), tables)
    return jnp.where(row == 7, wide(late[pl.ds(block, 1), :]).astype(F32), patched)


def export_kernel(state, cols, marks, got0, got1, early, late, exports, *refs):
    outs, (exported, sems) = refs[:-2], refs[-2:]
    copies = fetch([exports], [exported], sems)
    count = got0.shape[1] // BLK
    tables = tables_of(got0, count) + tables_of(got1, count)
    row = lax.broadcasted_iota(I32, (8, BLK), 0)
    for c in range(count):
        two = patch(cols[0, :, chunk(c)], wide(marks[1:2, chunk(c)]), tables)
        three = patch(cols[1, :, chunk(c)], wide(marks[2:3, chunk(c)]), tables)
        three = jnp.where(row == 7, wide(marks[3:4, chunk(c)]).astype(F32), three)
        for out in outs:
            out[:, chunk(c)] = two
            out[:, chunk(count + c)] = three
    me = lax.axis_index("gy")
    for copy in copies:
        copy.wait()
    for q, out in enumerate(outs):
        for t in range(exported.shape[2]):
            block = exported[0, me ^ q, t]
            out[:, chunk(2 * count + t)] = early_block(state, early, late, tables, block)


def live_slot(counts, n, nact):
    second = n >= counts[0, 0]
    return jnp.where(second, 1, 0), jnp.where(second, jnp.minimum(n - counts[0, 0], nact - 1), n)


def own_kernel(state, got0, got1, early, late, ids, counts, nbrs, own, density):
    count = got0.shape[1] // BLK
    blocks = density.shape[0]
    tables = tables_of(got0, count) + tables_of(got1, count)
    last = [wide(table[6:7, :]) for table in tables]
    for b in range(blocks):
        density[b : b + 1, :] = state[6:7, chunk(b)]
    for v in range(blocks // 8):
        part = slice(8 * v, 8 * v + 8)
        density[part, :] = patch(density[part, :], early[part, :], last)
    nact = ids.shape[2]

    def pick(n, _):
        which, i = live_slot(counts, n, nact)
        wanted = [ids[0, which, i]] + [nbrs[0, which, i, t] for t in range(nbrs.shape[3])]
        for t, block in enumerate(wanted):
            own[n, t] = early_block(state, early, late, tables, block)
        return 0

    lax.fori_loop(0, counts[0, 0] + counts[0, 1], pick, 0)


def spread(rows, out):
    columns_of = jnp.transpose(jnp.concatenate((rows + rows)[:8], axis=0))
    for k in range(len(rows)):
        out[k] = jnp.broadcast_to(columns_of[:, k : k + 1], (BLK, BLK))


def in_turn(live, prepare, work, first, second):
    prepare(0, first)

    def step(p, _):
        n = 2 * p
        prepare(n + 1, second)
        work(n, first)
        prepare(jnp.minimum(n + 2, TOTACT - 1), first)
        work(n + 1, second)
        return 0

    lax.fori_loop(0, (live + 1) // 2, step, 0)


def density_sums(near, n, centre, sums):
    for g in range(BLK // 8):
        part = slice(8 * g, 8 * g + 8)
        cx, cy, cz, half = (centre[k, part, :] for k in range(4))
        total = None
        for t in range(8):
            x, y, z, m = (wide(near[n, k, t : t + 1, :]) for k in range(4))
            dx, dy, dz = cx - x, cy - y, cz - z
            square = dx * dx + dy * dy + dz * dz
            ratio = square * lax.rsqrt(jnp.maximum(square, TINY)) * half
            fall = jnp.maximum(1.0 - ratio, 0.0)
            fall = fall * fall
            term = fall * fall * (1.0 + 4.0 * ratio) * m
            total = term if total is None else total + term
        sums[n, part, :] = total


def make_density_kernel(peers, slots):
    def density_kernel(own, before, late, ids, counts, far, exports, *refs):
        sent = refs[:peers]
        near, density = refs[peers : peers + 2]
        outs = refs[peers + 2 : 2 * peers + 2]
        (late_three, ghosts, first, second, sums, fresh, *small) = refs[2 * peers + 2 :]
        copies = fetch([ids, counts, far, exports], small[:4], small[4])
        ids, counts, far, exports = small[:4]
        count = late_three.shape[2] // BLK
        blocks = density.shape[0]
        me = lax.axis_index("gy")

        for q in range(peers):
            tables = tables_of(sent[q ^ 2], count)
            for c in range(count):
                values = sent[q][:, chunk(count + c)]
                code = wide(values[7:8, :]).astype(I32)
                late_three[q, :, chunk(c)] = patch(values, code, tables)

        def settle(values, q):
            code = wide(values[7:8, :]).astype(I32)
            tables = tables_of(sent[q ^ 2], count)
            tables += [late_three[q ^ 1, :, chunk(c)] for c in range(count)]
            return patch(values, code, tables)

        for q in range(peers):
            for t in range(slots):
                ghosts[:, chunk(q * slots + t)] = settle(sent[q][:, chunk(2 * count + t)], q)

        later = [sent[2][6:7, chunk(c)] for c in range(count)]
        later = [wide(x) for x in later + [late_three[1, 6:7, chunk(c)] for c in range(count)]]
        for v in range(blocks // 8):
            part = slice(8 * v, 8 * v + 8)
            density[part, :] = patch(before[part, :], late[part, :], later)

        for copy in copies:
            copy.wait()
        live = counts[0, 0] + counts[0, 1]
        nact = ids.shape[2]
        inner = own.shape[1]

        def gather(n, _):
            which, i = live_slot(counts, n, nact)
            for t in range(inner):
                near[n, :, t, :] = settle(own[n, t], 0)
            for t in range(far.shape[3]):
                g = far[0, which, i, t] ^ (me * slots)
                near[n, :, inner + t, :] = ghosts[:, lanes(g)]
            return 0

        lax.fori_loop(0, live, gather, 0)

        def prepare(n, buffer):
            rows = [near[n, k, 0:1, :] for k in range(3)]
            spread(rows + [0.5 / near[n, 4, 0:1, :]], buffer)

        in_turn(live, prepare, lambda n, b: density_sums(near, n, b, sums), first, second)
        for n in range(TOTACT):
            h = near[n, 4, 0:1, :]
            total = jnp.sum(jnp.transpose(sums[n]), axis=0, keepdims=True)
            fresh[n : n + 1, :] = total * (KERNEL_NORM / (h * h * h))

        def place(n, _):
            which, i = live_slot(counts, n, nact)
            density[pl.ds(ids[0, which, i], 1), :] = fresh[pl.ds(n, 1), :]
            return 0

        lax.fori_loop(0, live, place, 0)
        for q in range(peers):
            for t in range(slots):
                outs[q][t : t + 1, :] = density[pl.ds(exports[0, me ^ q, t], 1), :]

    return density_kernel


def force_sums(near, press, n, centre, sums, others, tiles):
    pushed = {t: [None] * 3 for t in tiles}
    for g in range(BLK // 8):
        part = slice(8 * g, 8 * g + 8)
        cx, cy, cz, cm, ch, cp = (centre[k, part, :] for k in range(6))
        total = [None] * 3
        for t in tiles:
            x, y, z, m, h = (wide(near[n, k, t : t + 1, :]) for k in range(5))
            apart = [cx - x, cy - y, cz - z]
            square = apart[0] * apart[0] + apart[1] * apart[1] + apart[2] * apart[2]
            inverse = 1.0 / (ch + h)
            distance = square * lax.rsqrt(jnp.maximum(square, TINY))
            fall = jnp.maximum(1.0 - distance * inverse, 0.0)
            inv2 = inverse * inverse
            weight = fall * fall * fall * (inv2 * inv2 * inverse)
            weight = weight * (cp + wide(press[n, t : t + 1, :])) * (cm * m)
            for k in range(3):
                push = weight * apart[k]
                total[k] = push if total[k] is None else total[k] + push
                if t > 0:
                    pushed[t][k] = push if pushed[t][k] is None else pushed[t][k] + push
        for k in range(3):
            sums[n, k, part, :] = total[k]
    for t in tiles:
        if t > 0:
            for k in range(3):
                others[n, k, 8 * t : 8 * t + 8, :] = pushed[t][k]


def forces(near, press, live, first, second, sums, others, rows, tiles):
    def prepare(n, buffer):
        spread([near[n, k, 0:1, :] for k in range(5)] + [press[n, 0:1, :]], buffer)

    def work(n, buffer):
        force_sums(near, press, n, buffer, sums, others, tiles)

    in_turn(live, prepare, work, first, second)
    for n in range(TOTACT):
        for k in range(3):
            scale = FORCE_NORM / near[n, 3, 0:1, :]
            total = jnp.sum(jnp.transpose(sums[n, k]), axis=0, keepdims=True)
            rows[n, k, 0:1, :] = total * scale
            for t in tiles:
                if t > 0:
                    total = jnp.sum(others[n, k, 8 * t : 8 * t + 8, :], axis=0, keepdims=True)
                    scale = -FORCE_NORM / near[n, 3, t : t + 1, :]
                    rows[n, k, t : t + 1, :] = total * scale


def force_scratch():
    return [
        VMEM((6, BLK, BLK), F32),
        VMEM((6, BLK, BLK), F32),
        VMEM((TOTACT, 3, BLK, BLK), F32),
        VMEM((TOTACT, 3, 8 * 8, BLK), F32),
        VMEM((TOTACT, 8, 8, BLK), F32),
        VMEM((TOTACT, 8, BLK), F32),
        VMEM((TOTACT, 8, BLK), F32),
    ]


def inner_kernel(near, density, ids, counts, nbrs, totals, *refs):
    first, second, sums, others, rows, press, rho = refs
    totals[...] = jnp.zeros_like(totals)
    live = counts[0, 0] + counts[0, 1]
    nact = ids.shape[2]
    inner = 1 + nbrs.shape[3]

    def blocks_of(n):
        which, i = live_slot(counts, n, nact)
        return [ids[0, which, i]] + [nbrs[0, which, i, t] for t in range(nbrs.shape[3])]

    def look_up(n, _):
        for t, block in enumerate(blocks_of(n)):
            rho[n, t : t + 1, :] = density[pl.ds(block, 1), :]
        return 0

    lax.fori_loop(0, live, look_up, 0)
    for n in range(TOTACT):
        press[n] = near[n, 5] / rho[n]
    forces(near, press, live, first, second, sums, others, rows, tuple(range(inner)))

    def place(n, _):
        for t, block in enumerate(blocks_of(n)):
            totals[0:3, lanes(block)] += rows[n, 0:3, t, :]
        return 0

    lax.fori_loop(0, live, place, 0)


def make_outer_kernel(peers, slots):
    def outer_kernel(near, density, ids, counts, far, *refs):
        got = refs[:peers]
        centre = refs[peers]
        returns = refs[peers + 1 : 2 * peers + 1]
        (first, second, sums, others, rows, press, rho, far_rho, back, *small) = refs[
            2 * peers + 1 :
        ]
        copies = fetch([ids, counts, far], small[:3], small[3])
        ids, counts, far = small[:3]
        for q in range(peers):
            far_rho[q * slots : (q + 1) * slots, :] = got[q][...]
        back[...] = jnp.zeros_like(back)
        me = lax.axis_index("gy")
        nact = ids.shape[2]
        ngh = far.shape[3]
        tiles = tuple(range(8 - ngh, 8))
        for copy in copies:
            copy.wait()
        live = counts[0, 0] + counts[0, 1]

        def look_up(n, _):
            which, i = live_slot(counts, n, nact)
            rho[n, 0:1, :] = density[pl.ds(ids[0, which, i], 1), :]
            for t in range(ngh):
                g = far[0, which, i, t] ^ (me * slots)
                rho[n, 8 - ngh + t : 9 - ngh + t, :] = far_rho[pl.ds(g, 1), :]
            return 0

        lax.fori_loop(0, live, look_up, 0)
        for n in range(TOTACT):
            press[n] = near[n, 5] / rho[n]
        forces(near, press, live, first, second, sums, others, rows, tiles)

        def place(n, _):
            which, i = live_slot(counts, n, nact)
            centre[n, 0:3, :] = rows[n, 0:3, 0, :]
            for t in range(ngh):
                g = far[0, which, i, t] ^ (me * slots)
                back[0:3, lanes(g)] += rows[n, 0:3, 8 - ngh + t, :]
            return 0

        lax.fori_loop(0, live, place, 0)
        for q in range(peers):
            returns[q][...] = back[:, q * slots * BLK : (q + 1) * slots * BLK]

    return outer_kernel


def make_final_kernel(peers, slots):
    def final_kernel(totals, centre, ids, counts, exports, *refs):
        got = refs[:peers]
        out, work, *small = refs[peers:]
        copies = fetch([ids, counts, exports], small[:3], small[3])
        ids, counts, exports = small[:3]
        work[...] = totals[...]
        me = lax.axis_index("gy")
        nact = ids.shape[2]
        for copy in copies:
            copy.wait()

        def place(n, _):
            which, i = live_slot(counts, n, nact)
            work[0:3, lanes(ids[0, which, i])] += centre[n, 0:3, :]
            return 0

        lax.fori_loop(0, counts[0, 0] + counts[0, 1], place, 0)
        for q in range(peers):
            for t in range(slots):
                work[0:3, lanes(exports[0, me ^ q, t])] += got[q][0:3, chunk(t)]
        out[...] = work[0:3, :]

    return final_kernel


def crossed(block, axis, bits):
    size = lax.axis_size(axis)
    return lax.ppermute(block, axis, [(i, i ^ bits) for i in range(size) if i ^ bits < size])


def exchanged(parts):
    arrived = {q: crossed(parts[q], "gy", q) for q in range(len(parts) - 1, 0, -1)}
    return [parts[0]] + [arrived[q] for q in range(1, len(parts))]


def shards(
    particles, mig_count, mig_rows, active_ids, active_count, local_nbrs, ghost_slots, export_blocks
):
    peers = lax.axis_size("gy")
    slots = export_blocks.shape[2]
    per_dev = particles.shape[1]
    blocks = per_dev // BLK
    mig = mig_rows.shape[2]
    inner = 1 + local_nbrs.shape[3]
    wide_total = peers * slots * BLK

    sent0, state, rows = call(
        first_kernel,
        [shape(8, mig), shape(8, per_dev), shape(4, mig, dtype=I32)],
        particles,
        mig_rows,
        hbm=(0, 1),
        scratch=[DMA((PIECES + 1,))],
    )
    got0 = crossed(sent0, "gx", 2)
    cols1, marks1, codes = call(
        early_tables_kernel,
        [shape(8, mig), shape(8, mig, dtype=I32), shape(2, blocks, BLK, dtype=I32)],
        state,
        rows,
        mig_count,
    )
    sent1 = call(second_kernel, shape(8, mig), cols1, marks1, got0)
    got1 = crossed(sent1, "gx", 1)
    table = shape(blocks, BLK, dtype=I32)
    cols, marks, early, late = call(
        late_tables_kernel,
        [shape(2, 8, mig), shape(8, mig, dtype=I32), table, table],
        state,
        rows,
        mig_count,
        codes,
        sent1,
    )
    packs = call(
        export_kernel,
        [shape(8, 2 * mig + slots * BLK)] * peers,
        state,
        cols,
        marks,
        got0,
        got1,
        early,
        late,
        export_blocks,
        scratch=fetch_scratch([export_blocks]),
    )
    sent = exchanged(packs)
    own, before = call(
        own_kernel,
        [shape(TOTACT, inner, 8, BLK), shape(blocks, BLK)],
        state,
        got0,
        got1,
        early,
        late,
        active_ids,
        active_count,
        local_nbrs,
        smem=(5, 6, 7),
    )
    indices = [active_ids, active_count, ghost_slots, export_blocks]
    near, density, *exports = call(
        make_density_kernel(peers, slots),
        [shape(TOTACT, 8, 8, BLK), shape(blocks, BLK)] + [shape(slots, BLK)] * peers,
        own,
        before,
        late,
        *indices,
        *sent,
        scratch=[
            VMEM((peers, 8, mig), F32),
            VMEM((8, wide_total), F32),
            VMEM((4, BLK, BLK), F32),
            VMEM((4, BLK, BLK), F32),
            VMEM((TOTACT, BLK, BLK), F32),
            VMEM((TOTACT, BLK), F32),
        ]
        + fetch_scratch(indices),
    )
    rho = exchanged(exports)
    totals = call(
        inner_kernel,
        shape(8, per_dev),
        near,
        density,
        active_ids,
        active_count,
        local_nbrs,
        smem=(2, 3, 4),
        scratch=force_scratch(),
    )
    indices = [active_ids, active_count, ghost_slots]
    centre, *returns = call(
        make_outer_kernel(peers, slots),
        [shape(TOTACT, 8, BLK)] + [shape(8, slots * BLK)] * peers,
        near,
        density,
        *indices,
        *rho,
        scratch=force_scratch()
        + [VMEM((peers * slots, BLK), F32), VMEM((8, wide_total), F32)]
        + fetch_scratch(indices),
    )
    got = exchanged(returns)
    indices = [active_ids, active_count, export_blocks]
    accel = call(
        make_final_kernel(peers, slots),
        shape(3, per_dev),
        totals,
        centre,
        *indices,
        *got,
        scratch=[VMEM((8, per_dev), F32)] + fetch_scratch(indices),
    )
    return density.reshape(-1), accel


def solution(mesh):
    both = ("gx", "gy")
    placed = (
        P(None, both),
        P(both, None),
        P(both, None, None),
        P(both, None, None),
        P(both, None),
        P(both, None, None, None),
        P(both, None, None, None),
        P(both, None, None),
    )
    return jax.shard_map(
        shards,
        mesh=mesh,
        in_specs=placed,
        out_specs=(P(both), P(None, both)),
        check_vma=False,
    )
```

time: 173 us -> 60.4 us (0.35); the launches traced: 171 us -> 60.3 us
  Pallas kernels: 139 us -> 32.2 us
  waiting for transfers between devices: 9.78 us -> 5.26 us
    pallas_call x7 -> x10, Pallas kernels: 139 us -> 32.2 us  [call(): pl.pallas_call(kernel, out_shape=out_shape, in_specs=[pl.BlockSpec(memory...]
    ppermute x11, waiting for transfers between devices: 9.78 us -> 5.26 us  [crossed(): lax.ppermute(block, axis, [(i, i ^ bits) for i in range(size) if i ^ bits...]
    unnamed x22 -> x20, local copies, waits for them, and re-layouts: 4.6 us -> 5.27 us
  transfers between devices with their start and end apart: 11 -> 11, of which waited for: 7 -> 5; matrix products, arithmetic and copies ran while one was open for 0% -> 0% of each run, Pallas kernels for 1% -> 19%
where the time goes in v2:
time: 60.4 us; the launch traced here: 60.3 us
  Pallas kernels  32.2 us (53%)
  starting transfers between devices  16.7 us (28%)
  local copies, waits for them, and re-layouts  5.27 us (9%)
  waiting for transfers between devices  5.26 us (9%)
  between operations  0.77 us (1%)
    pallas_call x10, Pallas kernels, call(): pl.pallas_call(kernel, out_shape=out_shape, in_specs=[pl.BlockSpec(memory...  32.2 us
    ppermute x11, starting transfers between devices, crossed(): lax.ppermute(block, axis, [(i, i ^ bits) for i in range(size) if i ^ bits...  16.7 us
    unnamed x20, local copies, waits for them, and re-layouts  5.27 us
    ppermute x11, waiting for transfers between devices, crossed(): lax.ppermute(block, axis, [(i, i ^ bits) for i in range(size) if i ^ bits...  5.26 us
  transfers between devices with their start and end apart: 11, of which 5 were waited for; matrix products, arithmetic and copies ran while one was open for 0% of the time, Pallas kernels for 19%

profile of v2, /device:TPU:0, one launch (start us, length us, event | category | flops | bytes accessed | tf_op | source)
XLA Modules:
  0.0 60.3 jit_solution(13515903860446925253)
XLA Ops:
  0.6 1.0 %copy-done = f32[7,16384]{1,0:T(8,128)S(1)} copy-done((f32[7,16384]{1,0:T(8,128)S(1)}, f32[7,16384]{1,0:T(8,128)}, u32[]{:S(2)}) %copy-start) | copy-done | bytes 458776
  1.7 0.7 %copy-done.5 = s32[1,4,512]{2,1,0:T(4,128)S(1)} copy-done((s32[1,4,512]{2,1,0:T(4,128)S(1)}, s32[1,4,512]{2,1,0:T(4,128)}, u32[]{:S(2)}) %copy-start.5) | copy-done | bytes 8216
  2.4 1.8 %shard_map.95 = (f32[8,512]{1,0:T(8,128)S(1)}, f32[8,16384]{1,0:T(8,128)S(1)}, s32[4,512]{1,0:T(4,128)S(1)}) custom-call(f32[7,16384]{1,0:T(8,128)S(1)} %copy-done, s32[1,4,512]{2,1,0:T(4,128)S(1)} %copy-done.5), custom_call_target="tpu_custom_call" | custom-call | tf_op jit(solution)/shard_map/pallas_call | solution.py:27
  4.2 3.0 %collective-permute-start = (f32[8,512]{1,0:T(8,128)S(1)}, f32[8,512]{1,0:T(8,128)S(1)}, u32[]{:S(2)}, u32[]{:S(2)}) collective-permute-start(f32[8,512]{1,0:T(8,128)S(1)} %get-tuple-element.30), channel_id=1, source_target_pairs={{0,8},{4,12},{8,0},{12,4},{16,24},{20,28},{24,16},{28,20},{1,9},{5... | collective-permute-start | bytes 49160 | tf_op jit(solution)/shard_map/ppermute | solution.py:522
  7.2 0.7 %copy-done.6 = s32[1,4]{1,0:T(1,128)S(1)} copy-done((s32[1,4]{1,0:T(1,128)S(1)}, s32[1,4]{1,0:T(1,128)}, u32[]{:S(2)}) %copy-start.6) | copy-done | bytes 40
  7.8 0.8 %shard_map.96 = (f32[8,512]{1,0:T(8,128)S(1)}, s32[8,512]{1,0:T(8,128)S(1)}, s32[2,128,128]{2,1,0:T(8,128)S(1)}) custom-call(f32[8,16384]{1,0:T(8,128)S(1)} %get-tuple-element.29.state, s32[4,512]{1,0:T(4,128)S(1)} %get-tuple-element.31.rows, s32[1,4]{1,0:T(1,128)S(1)} %copy-done.6), custom_call_target="tpu_custom_call" | custom-call | tf_op jit(solution)/shard_map/pallas_call | solution.py:27
  8.6 0.3 collective-permute-done.got0
  8.9 0.1 shard_map.97.after
  9.1 1.5 %shard_map.98 = (f32[2,8,512]{2,1,0:T(8,128)S(1)}, s32[8,512]{1,0:T(8,128)S(1)}, s32[128,128]{1,0:T(8,128)S(1)}, s32[128,128]{1,0:T(8,128)S(1)}) custom-call(f32[8,16384]{1,0:T(8,128)S(1)} %get-tuple-element.29.state, s32[4,512]{1,0:T(4,128)S(1)} %get-tuple-element.31.rows, s32[1,4]{1,0:T(1,128)S(1)} %copy-done.6, ...), custom_call_target="tpu_custom_call" | custom-call | tf_op jit(solution)/shard_map/pallas_call | solution.py:27
  10.5 0.7 %copy-done.3 = s32[1,4,8]{2,1,0:T(4,128)S(1)} copy-done((s32[1,4,8]{2,1,0:T(4,128)S(1)}, s32[1,4,8]{2,1,0:T(4,128)}, u32[]{:S(2)}) %copy-start.3) | copy-done | bytes 152
  11.2 1.0 %shard_map.100 = (f32[8,2048]{1,0:T(8,128)S(1)}, f32[8,2048]{1,0:T(8,128)S(1)}, f32[8,2048]{1,0:T(8,128)S(1)}, f32[8,2048]{1,0:T(8,128)S(1)}) custom-call(f32[8,16384]{1,0:T(8,128)S(1)} %get-tuple-element.29.state, f32[2,8,512]{2,1,0:T(8,128)S(1)} %get-tuple-element.39.cols, s32[8,512]{1,0:T(8,128)S(1)} %get-tuple-element.40.marks, ...), custom_call_target="tpu_custom_call" | custom-call | tf_op jit(solution)/shard_map/pallas_call | solution.py:27
  12.3 2.2 %collective-permute-start.2 = (f32[8,2048]{1,0:T(8,128)S(1)}, f32[8,2048]{1,0:T(8,128)S(1)}, u32[]{:S(2)}, u32[]{:S(2)}) collective-permute-start(f32[8,2048]{1,0:T(8,128)S(1)} %get-tuple-element.42), channel_id=1, source_target_pairs={{0,1},{1,0},{2,3},{3,2},{4,5},{5,4},{6,7},{7,6},{8,9},{9,8},{10,11... | collective-permute-start | bytes 196616 | tf_op jit(solution)/shard_map/ppermute | solution.py:522
  14.4 2.6 %collective-permute-start.3 = (f32[8,2048]{1,0:T(8,128)S(1)}, f32[8,2048]{1,0:T(8,128)S(1)}, u32[]{:S(2)}, u32[]{:S(2)}) collective-permute-start(f32[8,2048]{1,0:T(8,128)S(1)} %get-tuple-element.43), channel_id=1, source_target_pairs={{0,2},{1,3},{2,0},{3,1},{4,6},{5,7},{6,4},{7,5},{8,10},{9,11},{10,... | collective-permute-start | bytes 196616 | tf_op jit(solution)/shard_map/ppermute | solution.py:522
  17.0 0.1 copy.10.nbrs
  17.1 0.6 copy-done.7
  17.7 0.1 copy.11.far
  17.8 0.6 copy-done.2
  18.4 2.6 %shard_map.99 = (f32[12,4,8,128]{3,2,1,0:T(8,128)S(1)}, f32[128,128]{1,0:T(8,128)S(1)}) custom-call(f32[8,16384]{1,0:T(8,128)S(1)} %get-tuple-element.29.state, f32[8,512]{1,0:T(8,128)S(1)} %collective-permute-done.got0, f32[8,512]{1,0:T(8,128)S(1)} %collective-permute-done.1.got1, s32[128,128]{1,0:T(8,128)S(1)} %get-tuple-element.35.early, ...), custom_call_target="tpu_custom_call" | custom-call | tf_op jit(solution)/shard_map/pallas_call | solution.py:27
  21.0 0.4 collective-permute-done.3.refs_2_
  21.4 1.7 %collective-permute-done.4.refs_3_ = f32[8,2048]{1,0:T(8,128)S(1)} collective-permute-done((f32[8,2048]{1,0:T(8,128)S(1)}, f32[8,2048]{1,0:T(8,128)S(1)}, u32[]{:S(2)}, u32[]{:S(2)}) %collective-permute-start.4) | collective-permute-done | bytes 65568 | tf_op jit(solution)/shard_map/ppermute | solution.py:522
  23.2 9.4 %shard_map.101 = (f32[12,8,8,128]{3,2,1,0:T(8,128)S(1)}, f32[128,128]{1,0:T(8,128)}, f32[8,128]{1,0:T(8,128)S(1)}, f32[8,128]{1,0:T(8,128)S(1)}, f32[8,128]{1,0:T(8,128)S(1)}, /*index=5*/f32[8,128]{1,0:T(8,128)S(1)}) custom-call(f32[12,4,8,128]{3,2,1,0:T(8,128)S(1)} %get-tuple-element.37.own, f32[128,128]{1,0:T(8,128)S(1)} %get-tuple-element.38.before, ...), custom_call_target="tpu_custom_call" | custom-call | tf_op jit(solution)/shard_map/pallas_call | solution.py:27
  32.5 0.1 collective-permute-start.5
  32.7 1.7 %collective-permute-start.6 = (f32[8,128]{1,0:T(8,128)S(1)}, f32[8,128]{1,0:T(8,128)S(1)}, u32[]{:S(2)}, u32[]{:S(2)}) collective-permute-start(f32[8,128]{1,0:T(8,128)S(1)} %get-tuple-element.49), channel_id=1, source_target_pairs={{0,2},{1,3},{2,0},{3,1},{4,6},{5,7},{6,4},{7,5},{8,10},{9,11},{10,... | collective-permute-start | bytes 12296 | tf_op jit(solution)/shard_map/ppermute | solution.py:522
  34.4 2.6 %collective-permute-start.7 = (f32[8,128]{1,0:T(8,128)S(1)}, f32[8,128]{1,0:T(8,128)S(1)}, u32[]{:S(2)}, u32[]{:S(2)}) collective-permute-start(f32[8,128]{1,0:T(8,128)S(1)} %get-tuple-element.50), channel_id=1, source_target_pairs={{0,3},{1,2},{2,1},{3,0},{4,7},{5,6},{6,5},{7,4},{8,11},{9,10},{10,... | collective-permute-start | bytes 12296 | tf_op jit(solution)/shard_map/ppermute | solution.py:522
  37.0 0.2 collective-permute-done.6.refs_2_
  37.2 2.6 %collective-permute-done.7.refs_3_ = f32[8,128]{1,0:T(8,128)S(1)} collective-permute-done((f32[8,128]{1,0:T(8,128)S(1)}, f32[8,128]{1,0:T(8,128)S(1)}, u32[]{:S(2)}, u32[]{:S(2)}) %collective-permute-start.7) | collective-permute-done | bytes 4128 | tf_op jit(solution)/shard_map/ppermute | solution.py:522
  39.8 0.8 %copy-done.1 = f32[128,128]{1,0:T(8,128)S(1)} copy-done((f32[128,128]{1,0:T(8,128)S(1)}, f32[128,128]{1,0:T(8,128)}, u32[]{:S(2)}) %copy-start.1) | copy-done | bytes 65560
  40.7 6.8 %shard_map.103 = (f32[12,8,128]{2,1,0:T(8,128)S(1)}, f32[8,1024]{1,0:T(8,128)S(1)}, f32[8,1024]{1,0:T(8,128)S(1)}, f32[8,1024]{1,0:T(8,128)S(1)}, f32[8,1024]{1,0:T(8,128)S(1)}) custom-call(f32[12,8,8,128]{3,2,1,0:T(8,128)S(1)} %get-tuple-element.46.near, f32[128,128]{1,0:T(8,128)S(1)} %copy-done.1, s32[1,2,8]{2,1,0:T(2,128)S(1)} %copy-done.2, ...), custom_call_target="tpu_custom_call" | custom-call | tf_op jit(solution)/shard_map/pallas_call | solution.py:27
  47.4 1.8 %collective-permute-start.10 = (f32[8,1024]{1,0:T(8,128)S(1)}, f32[8,1024]{1,0:T(8,128)S(1)}, u32[]{:S(2)}, u32[]{:S(2)}) collective-permute-start(f32[8,1024]{1,0:T(8,128)S(1)} %get-tuple-element.55), channel_id=1, source_target_pairs={{0,3},{1,2},{2,1},{3,0},{4,7},{5,6},{6,5},{7,4},{8,11},{9,10},{10,... | collective-permute-start | bytes 98312 | tf_op jit(solution)/shard_map/ppermute | solution.py:522
  49.3 2.6 %collective-permute-start.9 = (f32[8,1024]{1,0:T(8,128)S(1)}, f32[8,1024]{1,0:T(8,128)S(1)}, u32[]{:S(2)}, u32[]{:S(2)}) collective-permute-start(f32[8,1024]{1,0:T(8,128)S(1)} %get-tuple-element.54), channel_id=1, source_target_pairs={{0,2},{1,3},{2,0},{3,1},{4,6},{5,7},{6,4},{7,5},{8,10},{9,11},{10,... | collective-permute-start | bytes 98312 | tf_op jit(solution)/shard_map/ppermute | solution.py:522
  51.9 6.7 %shard_map.102.totals = f32[8,16384]{1,0:T(8,128)S(1)} custom-call(f32[12,8,8,128]{3,2,1,0:T(8,128)S(1)} %get-tuple-element.46.near, f32[128,128]{1,0:T(8,128)S(1)} %copy-done.1, s32[1,2,8]{2,1,0:T(2,128)S(1)} %copy-done.2, s32[1,2]{1,0:T(1,128)S(1)} %copy-done.4, s32[1,2,8,3]{3,2,1,0:T(8,128)S(1)} %copy.10.nbrs), custom_call_target="tpu_custom_call" | custom-call | tf_op jit(solution)/shard_map/pallas_call | solution.py:27
  58.6 1.7 %shard_map.104 = f32[3,16384]{1,0:T(4,128)} custom-call(f32[8,16384]{1,0:T(8,128)S(1)} %shard_map.102.totals, f32[12,8,128]{2,1,0:T(8,128)S(1)} %get-tuple-element.51.centre, s32[1,2,8]{2,1,0:T(2,128)S(1)} %copy-done.2, s32[1,2]{1,0:T(1,128)S(1)} %copy-done.4, s32[1,4,8]{2,1,0:T(4,128)S(1)} %copy-done.3, f32[8,1024]{1,0:T(8,128)S(1)} %get-tuple-element.52.refs_0_, ...), custom_call_target="tpu_custom_call" | custom-call | tf_op jit(solution)/shard_map/pallas_call | solution.py:27
  (20 shorter events, 0.1 us)
Async XLA Ops:
  0.6 1.0 %copy-start = (f32[7,16384]{1,0:T(8,128)S(1)}, f32[7,16384]{1,0:T(8,128)}, u32[]{:S(2)}) copy-start(f32[7,16384]{1,0:T(8,128)} %particles.1) | copy-start | bytes 1376260
  1.7 0.7 %copy-start.5 = (s32[1,4,512]{2,1,0:T(4,128)S(1)}, s32[1,4,512]{2,1,0:T(4,128)}, u32[]{:S(2)}) copy-start(s32[1,4,512]{2,1,0:T(4,128)} %mig_rows.1) | copy-start | bytes 24580
  4.2 4.7 %collective-permute-start = (f32[8,512]{1,0:T(8,128)S(1)}, f32[8,512]{1,0:T(8,128)S(1)}, u32[]{:S(2)}, u32[]{:S(2)}) collective-permute-start(f32[8,512]{1,0:T(8,128)S(1)} %get-tuple-element.30), channel_id=1, source_target_pairs={{0,8},{4,12},{8,0},{12,4},{16,24},{20,28},{24,16},{28,20},{1,9},{5... | collective-permute-start | bytes 49160 | tf_op jit(solution)/shard_map/ppermute | solution.py:522
  7.2 0.7 %copy-start.6 = (s32[1,4]{1,0:T(1,128)S(1)}, s32[1,4]{1,0:T(1,128)}, u32[]{:S(2)}) copy-start(s32[1,4]{1,0:T(1,128)} %counts.8) | copy-start | bytes 52
  9.0 1.5 %collective-permute-start.1 = (f32[8,512]{1,0:T(8,128)S(1)}, f32[8,512]{1,0:T(8,128)S(1)}, u32[]{:S(2)}, u32[]{:S(2)}) collective-permute-start(f32[8,512]{1,0:T(8,128)S(1)} %shard_map.97.after), channel_id=1, source_target_pairs={{0,4},{4,0},{8,12},{12,8},{16,20},{20,16},{24,28},{28,24},{1,5},{5... | collective-permute-start | bytes 49160 | tf_op jit(solution)/shard_map/ppermute | solution.py:522
  10.5 0.7 %copy-start.3 = (s32[1,4,8]{2,1,0:T(4,128)S(1)}, s32[1,4,8]{2,1,0:T(4,128)}, u32[]{:S(2)}) copy-start(s32[1,4,8]{2,1,0:T(4,128)} %exports.5) | copy-start | bytes 388
  12.3 4.8 %copy-start.8 = (s32[1,2,8,3]{2,1,3,0:T(2,128)S(1)}, s32[1,2,8,3]{2,1,3,0:T(2,128)}, u32[]{:S(2)}) copy-start(s32[1,2,8,3]{2,1,3,0:T(2,128)} %param.13) | copy-start | bytes 580
  12.3 8.7 %collective-permute-start.2 = (f32[8,2048]{1,0:T(8,128)S(1)}, f32[8,2048]{1,0:T(8,128)S(1)}, u32[]{:S(2)}, u32[]{:S(2)}) collective-permute-start(f32[8,2048]{1,0:T(8,128)S(1)} %get-tuple-element.42), channel_id=1, source_target_pairs={{0,1},{1,0},{2,3},{3,2},{4,5},{5,4},{6,7},{7,6},{8,9},{9,8},{10,11... | collective-permute-start | bytes 196616 | tf_op jit(solution)/shard_map/ppermute | solution.py:522
  14.4 7.0 %collective-permute-start.3 = (f32[8,2048]{1,0:T(8,128)S(1)}, f32[8,2048]{1,0:T(8,128)S(1)}, u32[]{:S(2)}, u32[]{:S(2)}) collective-permute-start(f32[8,2048]{1,0:T(8,128)S(1)} %get-tuple-element.43), channel_id=1, source_target_pairs={{0,2},{1,3},{2,0},{3,1},{4,6},{5,7},{6,4},{7,5},{8,10},{9,11},{10,... | collective-permute-start | bytes 196616 | tf_op jit(solution)/shard_map/ppermute | solution.py:522
  17.0 0.7 %copy-start.7 = (s32[1,2,8,4]{2,3,1,0:T(4,128)S(1)}, s32[1,2,8,4]{2,3,1,0:T(4,128)}, u32[]{:S(2)}) copy-start(s32[1,2,8,4]{2,3,1,0:T(4,128)} %param.14) | copy-start | bytes 772
  17.0 6.1 %collective-permute-start.4 = (f32[8,2048]{1,0:T(8,128)S(1)}, f32[8,2048]{1,0:T(8,128)S(1)}, u32[]{:S(2)}, u32[]{:S(2)}) collective-permute-start(f32[8,2048]{1,0:T(8,128)S(1)} %get-tuple-element.44), channel_id=1, source_target_pairs={{0,3},{1,2},{2,1},{3,0},{4,7},{5,6},{6,5},{7,4},{8,11},{9,10},{10,... | collective-permute-start | bytes 196616 | tf_op jit(solution)/shard_map/ppermute | solution.py:522
  17.7 0.7 %copy-start.2 = (s32[1,2,8]{2,1,0:T(2,128)S(1)}, s32[1,2,8]{2,1,0:T(2,128)}, u32[]{:S(2)}) copy-start(s32[1,2,8]{2,1,0:T(2,128)} %ids.9) | copy-start | bytes 196
  17.7 0.7 %copy-start.4 = (s32[1,2]{1,0:T(1,128)S(1)}, s32[1,2]{1,0:T(1,128)}, u32[]{:S(2)}) copy-start(s32[1,2]{1,0:T(1,128)} %counts.13) | copy-start | bytes 28
  32.5 4.5 %collective-permute-start.5 = (f32[8,128]{1,0:T(8,128)S(1)}, f32[8,128]{1,0:T(8,128)S(1)}, u32[]{:S(2)}, u32[]{:S(2)}) collective-permute-start(f32[8,128]{1,0:T(8,128)S(1)} %get-tuple-element.48), channel_id=1, source_target_pairs={{0,1},{1,0},{2,3},{3,2},{4,5},{5,4},{6,7},{7,6},{8,9},{9,8},{10,11... | collective-permute-start | bytes 12296 | tf_op jit(solution)/shard_map/ppermute | solution.py:522
  32.7 4.5 %collective-permute-start.6 = (f32[8,128]{1,0:T(8,128)S(1)}, f32[8,128]{1,0:T(8,128)S(1)}, u32[]{:S(2)}, u32[]{:S(2)}) collective-permute-start(f32[8,128]{1,0:T(8,128)S(1)} %get-tuple-element.49), channel_id=1, source_target_pairs={{0,2},{1,3},{2,0},{3,1},{4,6},{5,7},{6,4},{7,5},{8,10},{9,11},{10,... | collective-permute-start | bytes 12296 | tf_op jit(solution)/shard_map/ppermute | solution.py:522
  34.4 5.4 %collective-permute-start.7 = (f32[8,128]{1,0:T(8,128)S(1)}, f32[8,128]{1,0:T(8,128)S(1)}, u32[]{:S(2)}, u32[]{:S(2)}) collective-permute-start(f32[8,128]{1,0:T(8,128)S(1)} %get-tuple-element.50), channel_id=1, source_target_pairs={{0,3},{1,2},{2,1},{3,0},{4,7},{5,6},{6,5},{7,4},{8,11},{9,10},{10,... | collective-permute-start | bytes 12296 | tf_op jit(solution)/shard_map/ppermute | solution.py:522
  39.8 0.8 %copy-start.1 = (f32[128,128]{1,0:T(8,128)S(1)}, f32[128,128]{1,0:T(8,128)}, u32[]{:S(2)}) copy-start(f32[128,128]{1,0:T(8,128)} %get-tuple-element.45.density) | copy-start | bytes 196612
  47.4 11.1 %collective-permute-start.10 = (f32[8,1024]{1,0:T(8,128)S(1)}, f32[8,1024]{1,0:T(8,128)S(1)}, u32[]{:S(2)}, u32[]{:S(2)}) collective-permute-start(f32[8,1024]{1,0:T(8,128)S(1)} %get-tuple-element.55), channel_id=1, source_target_pairs={{0,3},{1,2},{2,1},{3,0},{4,7},{5,6},{6,5},{7,4},{8,11},{9,10},{10,... | collective-permute-start | bytes 98312 | tf_op jit(solution)/shard_map/ppermute | solution.py:522
  49.3 9.3 %collective-permute-start.8 = (f32[8,1024]{1,0:T(8,128)S(1)}, f32[8,1024]{1,0:T(8,128)S(1)}, u32[]{:S(2)}, u32[]{:S(2)}) collective-permute-start(f32[8,1024]{1,0:T(8,128)S(1)} %get-tuple-element.53), channel_id=1, source_target_pairs={{0,1},{1,0},{2,3},{3,2},{4,5},{5,4},{6,7},{7,6},{8,9},{9,8},{10,11... | collective-permute-start | bytes 98312 | tf_op jit(solution)/shard_map/ppermute | solution.py:522
  49.3 9.3 %collective-permute-start.9 = (f32[8,1024]{1,0:T(8,128)S(1)}, f32[8,1024]{1,0:T(8,128)S(1)}, u32[]{:S(2)}, u32[]{:S(2)}) collective-permute-start(f32[8,1024]{1,0:T(8,128)S(1)} %get-tuple-element.54), channel_id=1, source_target_pairs={{0,2},{1,3},{2,0},{3,1},{4,6},{5,7},{6,4},{7,5},{8,10},{9,11},{10,... | collective-permute-start | bytes 98312 | tf_op jit(solution)/shard_map/ppermute | solution.py:522

commit v3 on v2

--- a/solution.py
+++ b/solution.py
@@ -16,13 +16,12 @@
 I32 = jnp.int32
 VMEM = pltpu.VMEM
 SMEM = pltpu.SMEM
-HBM = pltpu.HBM
 DMA = pltpu.SemaphoreType.DMA
 
 
-def call(kernel, out_shape, *args, smem=(), hbm=(), scratch=(), limit=16 << 20):
+def call(kernel, out_shape, *args, smem=(), scratch=(), limit=16 << 20, cost=0):
     def space(n):
-        return SMEM if n in smem else HBM if n in hbm else VMEM
+        return SMEM if n in smem else VMEM
 
     return pl.pallas_call(
         kernel,
@@ -31,6 +30,9 @@
         out_specs=jax.tree.map(lambda _: pl.BlockSpec(memory_space=VMEM), out_shape),
         scratch_shapes=list(scratch),
         compiler_params=pltpu.CompilerParams(vmem_limit_bytes=limit),
+        cost_estimate=pl.CostEstimate(flops=0, transcendentals=0, bytes_accessed=cost)
+        if cost
+        else None,
     )(*args)
 
 
@@ -88,44 +90,18 @@
     return [SMEM(a.shape, I32) for a in arrays] + [DMA((len(arrays),))]
 
 
-PIECES = 4
-
-
-def first_kernel(particles, mig_rows, out, state, rows, sems):
-    per_dev = particles.shape[1]
-    size = per_dev // PIECES
+def first_kernel(state, mig_rows, out, rows):
+    rows[...] = mig_rows[...]
+    for c in range(mig_rows.shape[2] // BLK):
+        out[:, chunk(c)] = columns(state, wide(mig_rows[0, 0:1, chunk(c)]))
+
+
+def code_table(mig_rows, level, blocks):
     mig = mig_rows.shape[2]
-    index_copy = pltpu.make_async_copy(mig_rows.at[0], rows, sems.at[PIECES])
-    index_copy.start()
-    copies = []
-    for p in range(PIECES):
-        part = slice(p * size, (p + 1) * size)
-        copy = pltpu.make_async_copy(
-            particles.at[:, part], state.at[pl.ds(0, 7), part], sems.at[p]
-        )
-        copy.start()
-        copies.append(copy)
-    index_copy.wait()
-    slots = [wide(rows[0:1, chunk(c)]) for c in range(mig // BLK)]
-    found = [jnp.zeros((8, BLK), F32) for _ in slots]
-    for p, copy in enumerate(copies):
-        copy.wait()
-        for b in range(p * size // BLK, (p + 1) * size // BLK):
-            values = state[:, chunk(b)]
-            for c, s in enumerate(slots):
-                picked = take(values, s & (BLK - 1))
-                found[c] = jnp.where((s >> 7) == b, picked, found[c])
-    for c, values in enumerate(found):
-        out[:, chunk(c)] = values
-
-
-def code_table(rows, counts, level, blocks):
-    mig = rows.shape[1]
-    slots = rows[level : level + 1, :]
+    slots = mig_rows[0, level : level + 1, :]
     k = lax.broadcasted_iota(I32, (1, mig), 1)
-    live = k < counts[0:1, level : level + 1]
-    low = jnp.where(live, k & (BLK - 1), 0).astype(F32)
-    high = jnp.where(live, (k >> 7) + 1, 0).astype(F32)
+    low = (k & (BLK - 1)).astype(F32)
+    high = ((k >> 7) + 1).astype(F32)
     in_block = lax.broadcasted_iota(I32, (blocks, mig), 0) == (slots >> 7)
     in_lane = lax.broadcasted_iota(I32, (BLK, mig), 0) == (slots & (BLK - 1))
     left = jnp.concatenate([jnp.where(in_block, low, 0.0), jnp.where(in_block, high, 0.0)], axis=0)
@@ -140,6 +116,11 @@
     return jnp.where(high > 0.5, (high - 1.0) * BLK + low, -1.0).astype(I32)
 
 
+def codes_kernel(mig_rows, codes):
+    for level in range(4):
+        codes[level] = code_table(mig_rows, level, codes.shape[1])
+
+
 def code_at(table, slots):
     block = slots >> 7
     lane = slots & (BLK - 1)
@@ -151,31 +132,45 @@
     return jnp.max(found, axis=0, keepdims=True)
 
 
-def early_tables_kernel(state, rows, counts, cols, marks, codes):
-    mig = rows.shape[1]
-    blocks = codes.shape[1]
-    for level in range(2):
-        codes[level] = code_table(rows, counts, level, blocks)
+def early_tables_kernel(state, mig_rows, codes, counts, exports, cols, marks, tables, exports_out):
+    mig = mig_rows.shape[2]
+    exports_out[...] = exports[...]
+    valid = []
+    for level in range(4):
+        code = codes[level]
+        valid.append(jnp.where(code < counts[0:1, level : level + 1], code, -1))
+    tables[0] = jnp.where(valid[1] >= 0, valid[1] + mig, valid[0])
+    tables[1] = jnp.where(valid[3] >= 0, valid[3] + mig, valid[2])
+    tables[2] = valid[2]
+    tables[3] = valid[0]
     for c in range(mig // BLK):
-        slots = wide(rows[1:2, chunk(c)])
-        marks[0:1, chunk(c)] = code_at(codes.at[0], slots)
+        slots = wide(mig_rows[0, 1:2, chunk(c)])
+        marks[0:1, chunk(c)] = code_at(tables.at[3], slots)
         cols[:, chunk(c)] = columns(state, slots)
 
 
-def late_tables_kernel(state, rows, counts, codes, after, cols, marks, early, late):
-    mig = rows.shape[1]
-    blocks = codes.shape[1]
-    code2 = code_table(rows, counts, 2, blocks)
-    code3 = code_table(rows, counts, 3, blocks)
-    early[...] = jnp.where(codes[1] >= 0, codes[1] + mig, codes[0])
-    late[...] = jnp.where(code3 >= 0, code3 + mig, code2)
-    for c in range(mig // BLK):
-        two, three = (wide(rows[level : level + 1, chunk(c)]) for level in (2, 3))
-        marks[1:2, chunk(c)] = code_at(early, two)
-        marks[2:3, chunk(c)] = code_at(early, three)
-        marks[3:4, chunk(c)] = code_at(code2, three)
+def late_tables_kernel(
+    state, mig_rows, tables, exports, after, cols, marks, raw, code_rows, exported, sems
+):
+    copies = fetch([exports], [exported], sems)
+    for c in range(mig_rows.shape[2] // BLK):
+        two, three = (wide(mig_rows[0, level : level + 1, chunk(c)]) for level in (2, 3))
+        marks[1:2, chunk(c)] = code_at(tables.at[0], two)
+        marks[2:3, chunk(c)] = code_at(tables.at[0], three)
+        marks[3:4, chunk(c)] = code_at(tables.at[2], three)
         cols[0, :, chunk(c)] = columns(state, two)
         cols[1, :, chunk(c)] = columns(state, three)
+    for copy in copies:
+        copy.wait()
+    me = lax.axis_index("gy")
+    peers, slots = exports.shape[1:]
+    row = lax.broadcasted_iota(I32, (8, BLK), 0)
+    for q in range(peers):
+        for t in range(slots):
+            block = exported[0, me ^ q, t]
+            code = wide(tables[1, pl.ds(block, 1), :]).astype(F32)
+            raw[:, chunk(q * slots + t)] = jnp.where(row == 7, code, state[:, lanes(block)])
+            code_rows[q, t : t + 1, :] = tables[0, pl.ds(block, 1), :]
 
 
 def second_kernel(cols, marks, got0, out):
@@ -185,16 +180,15 @@
         out[:, chunk(c)] = patch(cols[:, chunk(c)], wide(marks[0:1, chunk(c)]), tables)
 
 
-def early_block(state, early, late, tables, block):
+def early_block(state, codes, tables, block):
     row = lax.broadcasted_iota(I32, (8, BLK), 0)
-    patched = patch(state[:, lanes(block)], wide(early[pl.ds(block, 1), :]), tables)
-    return jnp.where(row == 7, wide(late[pl.ds(block, 1), :]).astype(F32), patched)
-
-
-def export_kernel(state, cols, marks, got0, got1, early, late, exports, *refs):
-    outs, (exported, sems) = refs[:-2], refs[-2:]
-    copies = fetch([exports], [exported], sems)
+    patched = patch(state[:, lanes(block)], wide(codes[0, pl.ds(block, 1), :]), tables)
+    return jnp.where(row == 7, wide(codes[1, pl.ds(block, 1), :]).astype(F32), patched)
+
+
+def export_kernel(cols, marks, got0, got1, raw, code_rows, *outs):
     count = got0.shape[1] // BLK
+    slots = code_rows.shape[1]
     tables = tables_of(got0, count) + tables_of(got1, count)
     row = lax.broadcasted_iota(I32, (8, BLK), 0)
     for c in range(count):
@@ -204,13 +198,11 @@
         for out in outs:
             out[:, chunk(c)] = two
             out[:, chunk(count + c)] = three
-    me = lax.axis_index("gy")
-    for copy in copies:
-        copy.wait()
     for q, out in enumerate(outs):
-        for t in range(exported.shape[2]):
-            block = exported[0, me ^ q, t]
-            out[:, chunk(2 * count + t)] = early_block(state, early, late, tables, block)
+        for t in range(slots):
+            values = raw[:, chunk(q * slots + t)]
+            patched = patch(values, wide(code_rows[q, t : t + 1, :]), tables)
+            out[:, chunk(2 * count + t)] = jnp.where(row == 7, values, patched)
 
 
 def live_slot(counts, n, nact):
@@ -218,7 +210,7 @@
     return jnp.where(second, 1, 0), jnp.where(second, jnp.minimum(n - counts[0, 0], nact - 1), n)
 
 
-def own_kernel(state, got0, got1, early, late, ids, counts, nbrs, own, density):
+def own_kernel(state, got0, got1, codes, ids, counts, nbrs, own, density):
     count = got0.shape[1] // BLK
     blocks = density.shape[0]
     tables = tables_of(got0, count) + tables_of(got1, count)
@@ -227,17 +219,14 @@
         density[b : b + 1, :] = state[6:7, chunk(b)]
     for v in range(blocks // 8):
         part = slice(8 * v, 8 * v + 8)
-        density[part, :] = patch(density[part, :], early[part, :], last)
+        density[part, :] = patch(density[part, :], codes[0, part, :], last)
     nact = ids.shape[2]
 
-    def pick(n, _):
+    for n in range(TOTACT):
         which, i = live_slot(counts, n, nact)
         wanted = [ids[0, which, i]] + [nbrs[0, which, i, t] for t in range(nbrs.shape[3])]
         for t, block in enumerate(wanted):
-            own[n, t] = early_block(state, early, late, tables, block)
-        return 0
-
-    lax.fori_loop(0, counts[0, 0] + counts[0, 1], pick, 0)
+            own[n, t] = early_block(state, codes, tables, block)
 
 
 def spread(rows, out):
@@ -246,8 +235,8 @@
         out[k] = jnp.broadcast_to(columns_of[:, k : k + 1], (BLK, BLK))
 
 
-def in_turn(live, prepare, work, first, second):
-    prepare(0, first)
+def in_turn(live, prepare, work, first, second, start=0, stop=TOTACT):
+    prepare(start, first)
 
     def step(p, _):
         n = 2 * p
@@ -257,7 +246,7 @@
         work(n + 1, second)
         return 0
 
-    lax.fori_loop(0, (live + 1) // 2, step, 0)
+    lax.fori_loop(start // 2, (jnp.minimum(live, stop) + 1) // 2, step, 0)
 
 
 def density_sums(near, n, centre, sums):
@@ -278,8 +267,8 @@
 
 
 def make_density_kernel(peers, slots):
-    def density_kernel(own, before, late, ids, counts, far, exports, *refs):
-        sent = refs[:peers]
+    def density_kernel(own, before, codes, ids, counts, far, exports, *refs):
+        sent = by_partner(refs[:peers])
         near, density = refs[peers : peers + 2]
         outs = refs[peers + 2 : 2 * peers + 2]
         (late_three, ghosts, first, second, sums, fresh, *small) = refs[2 * peers + 2 :]
@@ -310,7 +299,7 @@
         later = [wide(x) for x in later + [late_three[1, 6:7, chunk(c)] for c in range(count)]]
         for v in range(blocks // 8):
             part = slice(8 * v, 8 * v + 8)
-            density[part, :] = patch(before[part, :], late[part, :], later)
+            density[part, :] = patch(before[part, :], codes[1, part, :], later)
 
         for copy in copies:
             copy.wait()
@@ -318,16 +307,13 @@
         nact = ids.shape[2]
         inner = own.shape[1]
 
-        def gather(n, _):
+        for n in range(TOTACT):
             which, i = live_slot(counts, n, nact)
             for t in range(inner):
                 near[n, :, t, :] = settle(own[n, t], 0)
             for t in range(far.shape[3]):
                 g = far[0, which, i, t] ^ (me * slots)
                 near[n, :, inner + t, :] = ghosts[:, lanes(g)]
-            return 0
-
-        lax.fori_loop(0, live, gather, 0)
 
         def prepare(n, buffer):
             rows = [near[n, k, 0:1, :] for k in range(3)]
@@ -381,15 +367,15 @@
                 others[n, k, 8 * t : 8 * t + 8, :] = pushed[t][k]
 
 
-def forces(near, press, live, first, second, sums, others, rows, tiles):
+def forces(near, press, live, first, second, sums, others, rows, tiles, start=0, stop=TOTACT):
     def prepare(n, buffer):
         spread([near[n, k, 0:1, :] for k in range(5)] + [press[n, 0:1, :]], buffer)
 
     def work(n, buffer):
         force_sums(near, press, n, buffer, sums, others, tiles)
 
-    in_turn(live, prepare, work, first, second)
-    for n in range(TOTACT):
+    in_turn(live, prepare, work, first, second, start, stop)
+    for n in range(start, stop):
         for k in range(3):
             scale = FORCE_NORM / near[n, 3, 0:1, :]
             total = jnp.sum(jnp.transpose(sums[n, k]), axis=0, keepdims=True)
@@ -413,9 +399,8 @@
     ]
 
 
-def inner_kernel(near, density, ids, counts, nbrs, totals, *refs):
+def inner_forces(near, density, ids, counts, nbrs, totals, refs, start, stop):
     first, second, sums, others, rows, press, rho = refs
-    totals[...] = jnp.zeros_like(totals)
     live = counts[0, 0] + counts[0, 1]
     nact = ids.shape[2]
     inner = 1 + nbrs.shape[3]
@@ -424,27 +409,46 @@
         which, i = live_slot(counts, n, nact)
         return [ids[0, which, i]] + [nbrs[0, which, i, t] for t in range(nbrs.shape[3])]
 
-    def look_up(n, _):
+    for n in range(start, stop):
         for t, block in enumerate(blocks_of(n)):
             rho[n, t : t + 1, :] = density[pl.ds(block, 1), :]
-        return 0
-
-    lax.fori_loop(0, live, look_up, 0)
-    for n in range(TOTACT):
+    for n in range(start, stop):
         press[n] = near[n, 5] / rho[n]
-    forces(near, press, live, first, second, sums, others, rows, tuple(range(inner)))
+    tiles = tuple(range(inner))
+    forces(near, press, live, first, second, sums, others, rows, tiles, start, stop)
 
     def place(n, _):
         for t, block in enumerate(blocks_of(n)):
             totals[0:3, lanes(block)] += rows[n, 0:3, t, :]
         return 0
 
-    lax.fori_loop(0, live, place, 0)
+    lax.fori_loop(start, jnp.minimum(live, stop), place, 0)
+
+
+HALF = TOTACT // 2
+
+
+def inner_kernel(near, density, ids, counts, nbrs, totals, density_out, *refs):
+    density_out[...] = density[...]
+    totals[...] = jnp.zeros_like(totals)
+    inner_forces(near, density, ids, counts, nbrs, totals, refs, 0, HALF)
+
+
+def inner_rest_kernel(near, density, ids, counts, nbrs, before, centre, totals, *refs):
+    totals[...] = before[...]
+    inner_forces(near, density, ids, counts, nbrs, totals, refs, HALF, TOTACT)
+
+    def place(n, _):
+        which, i = live_slot(counts, n, ids.shape[2])
+        totals[0:3, lanes(ids[0, which, i])] += centre[n, 0:3, :]
+        return 0
+
+    lax.fori_loop(0, counts[0, 0] + counts[0, 1], place, 0)
 
 
 def make_outer_kernel(peers, slots):
-    def outer_kernel(near, density, ids, counts, far, *refs):
-        got = refs[:peers]
+    def outer_kernel(near, density, after, ids, counts, far, *refs):
+        got = by_partner(refs[:peers])
         centre = refs[peers]
         returns = refs[peers + 1 : 2 * peers + 1]
         (first, second, sums, others, rows, press, rho, far_rho, back, *small) = refs[
@@ -463,15 +467,12 @@
             copy.wait()
         live = counts[0, 0] + counts[0, 1]
 
-        def look_up(n, _):
+        for n in range(TOTACT):
             which, i = live_slot(counts, n, nact)
             rho[n, 0:1, :] = density[pl.ds(ids[0, which, i], 1), :]
             for t in range(ngh):
                 g = far[0, which, i, t] ^ (me * slots)
                 rho[n, 8 - ngh + t : 9 - ngh + t, :] = far_rho[pl.ds(g, 1), :]
-            return 0
-
-        lax.fori_loop(0, live, look_up, 0)
         for n in range(TOTACT):
             press[n] = near[n, 5] / rho[n]
         forces(near, press, live, first, second, sums, others, rows, tiles)
@@ -492,27 +493,18 @@
 
 
 def make_final_kernel(peers, slots):
-    def final_kernel(totals, centre, ids, counts, exports, *refs):
-        got = refs[:peers]
-        out, work, *small = refs[peers:]
-        copies = fetch([ids, counts, exports], small[:3], small[3])
-        ids, counts, exports = small[:3]
-        work[...] = totals[...]
+    def final_kernel(totals, exports, *refs):
+        got = by_partner(refs[:peers])
+        out, *small = refs[peers:]
+        copies = fetch([exports], small[:1], small[1])
+        exports = small[0]
+        out[...] = totals[0:3, :]
         me = lax.axis_index("gy")
-        nact = ids.shape[2]
         for copy in copies:
             copy.wait()
-
-        def place(n, _):
-            which, i = live_slot(counts, n, nact)
-            work[0:3, lanes(ids[0, which, i])] += centre[n, 0:3, :]
-            return 0
-
-        lax.fori_loop(0, counts[0, 0] + counts[0, 1], place, 0)
         for q in range(peers):
             for t in range(slots):
-                work[0:3, lanes(exports[0, me ^ q, t])] += got[q][0:3, chunk(t)]
-        out[...] = work[0:3, :]
+                out[0:3, lanes(exports[0, me ^ q, t])] += got[q][0:3, chunk(t)]
 
     return final_kernel
 
@@ -523,8 +515,11 @@
 
 
 def exchanged(parts):
-    arrived = {q: crossed(parts[q], "gy", q) for q in range(len(parts) - 1, 0, -1)}
-    return [parts[0]] + [arrived[q] for q in range(1, len(parts))]
+    return [parts[0]] + [crossed(parts[q], "gy", q) for q in range(len(parts) - 1, 0, -1)]
+
+
+def by_partner(refs):
+    return [refs[0]] + list(refs[:0:-1])
 
 
 def shards(
@@ -538,46 +533,52 @@
     inner = 1 + local_nbrs.shape[3]
     wide_total = peers * slots * BLK
 
-    sent0, state, rows = call(
-        first_kernel,
-        [shape(8, mig), shape(8, per_dev), shape(4, mig, dtype=I32)],
-        particles,
-        mig_rows,
-        hbm=(0, 1),
-        scratch=[DMA((PIECES + 1,))],
-    )
+    state = jnp.pad(particles, ((0, 1), (0, 0)))
+    sent0, rows = call(
+        first_kernel, [shape(8, mig), shape(*mig_rows.shape, dtype=I32)], state, mig_rows
+    )
+    codes = call(codes_kernel, shape(4, blocks, BLK, dtype=I32), rows)
     got0 = crossed(sent0, "gx", 2)
-    cols1, marks1, codes = call(
+    cols1, marks1, tables, export_ids = call(
         early_tables_kernel,
-        [shape(8, mig), shape(8, mig, dtype=I32), shape(2, blocks, BLK, dtype=I32)],
+        [
+            shape(8, mig),
+            shape(8, mig, dtype=I32),
+            shape(4, blocks, BLK, dtype=I32),
+            shape(*export_blocks.shape, dtype=I32),
+        ],
         state,
         rows,
+        codes,
         mig_count,
+        export_blocks,
     )
     sent1 = call(second_kernel, shape(8, mig), cols1, marks1, got0)
     got1 = crossed(sent1, "gx", 1)
-    table = shape(blocks, BLK, dtype=I32)
-    cols, marks, early, late = call(
+    cols, marks, raw, code_rows = call(
         late_tables_kernel,
-        [shape(2, 8, mig), shape(8, mig, dtype=I32), table, table],
+        [
+            shape(2, 8, mig),
+            shape(8, mig, dtype=I32),
+            shape(8, wide_total),
+            shape(peers, slots, BLK, dtype=I32),
+        ],
         state,
         rows,
-        mig_count,
-        codes,
+        tables,
+        export_ids,
         sent1,
+        scratch=fetch_scratch([export_ids]),
     )
     packs = call(
         export_kernel,
         [shape(8, 2 * mig + slots * BLK)] * peers,
-        state,
         cols,
         marks,
         got0,
         got1,
-        early,
-        late,
-        export_blocks,
-        scratch=fetch_scratch([export_blocks]),
+        raw,
+        code_rows,
     )
     sent = exchanged(packs)
     own, before = call(
@@ -586,20 +587,19 @@
         state,
         got0,
         got1,
-        early,
-        late,
+        tables,
         active_ids,
         active_count,
         local_nbrs,
-        smem=(5, 6, 7),
-    )
-    indices = [active_ids, active_count, ghost_slots, export_blocks]
+        smem=(4, 5, 6),
+    )
+    indices = [active_ids, active_count, ghost_slots, export_ids]
     near, density, *exports = call(
         make_density_kernel(peers, slots),
         [shape(TOTACT, 8, 8, BLK), shape(blocks, BLK)] + [shape(slots, BLK)] * peers,
         own,
         before,
-        late,
+        tables,
         *indices,
         *sent,
         scratch=[
@@ -613,9 +613,9 @@
         + fetch_scratch(indices),
     )
     rho = exchanged(exports)
-    totals = call(
+    totals, density_out = call(
         inner_kernel,
-        shape(8, per_dev),
+        [shape(8, per_dev), shape(blocks, BLK)],
         near,
         density,
         active_ids,
@@ -630,6 +630,7 @@
         [shape(TOTACT, 8, BLK)] + [shape(8, slots * BLK)] * peers,
         near,
         density,
+        totals,
         *indices,
         *rho,
         scratch=force_scratch()
@@ -637,17 +638,28 @@
         + fetch_scratch(indices),
     )
     got = exchanged(returns)
-    indices = [active_ids, active_count, export_blocks]
+    totals = call(
+        inner_rest_kernel,
+        shape(8, per_dev),
+        near,
+        density,
+        active_ids,
+        active_count,
+        local_nbrs,
+        totals,
+        centre,
+        smem=(2, 3, 4),
+        scratch=force_scratch(),
+    )
     accel = call(
         make_final_kernel(peers, slots),
         shape(3, per_dev),
         totals,
-        centre,
-        *indices,
+        export_ids,
         *got,
-        scratch=[VMEM((8, per_dev), F32)] + fetch_scratch(indices),
-    )
-    return density.reshape(-1), accel
+        scratch=fetch_scratch([export_ids]),
+    )
+    return density_out.reshape(-1), accel
 
 
 def solution(mesh):

time: 60.4 us -> 52.7 us (0.87)
  local copies, waits for them, and re-layouts: 5.27 us -> 2.04 us
  Pallas kernels: 32.2 us -> 29.3 us
  waiting for transfers between devices: 5.26 us -> 3.52 us
    unnamed x20 -> x16, local copies, waits for them, and re-layouts: 5.27 us -> 0.96 us
    pallas_call x10 -> x12, Pallas kernels: 32.2 us -> 29.3 us  [call(): pl.pallas_call(kernel, out_shape=out_shape, in_specs=[pl.BlockSpec(memory...]
    ppermute x11, waiting for transfers between devices: 5.26 us -> 3.52 us  [crossed(): lax.ppermute(block, axis, [(i, i ^ bits) for i in range(size) if i ^ bits...]
    pad x0 -> x1, local copies, waits for them, and re-layouts: none -> 1.08 us  [shards(): state = jnp.pad(particles, ((0, 1), (0, 0)))]
  transfers between devices with their start and end apart: 11 -> 11, of which waited for: 5 -> 2; matrix products, arithmetic and copies ran while one was open for 0% -> 0% of each run, Pallas kernels for 19% -> 24%
where the time goes in v3:
time: 52.7 us; the launch traced here: 52.4 us
  Pallas kernels  29.3 us (56%)
  starting transfers between devices  16.8 us (32%)
  waiting for transfers between devices  3.52 us (7%)
  local copies, waits for them, and re-layouts  2.04 us (4%)
  between operations  0.78 us (1%)
    pallas_call x12, Pallas kernels, call(): pl.pallas_call(kernel, out_shape=out_shape, in_specs=[pl.BlockSpec(memory...  29.3 us
    ppermute x11, starting transfers between devices, crossed(): lax.ppermute(block, axis, [(i, i ^ bits) for i in range(size) if i ^ bits...  16.8 us
    ppermute x11, waiting for transfers between devices, crossed(): lax.ppermute(block, axis, [(i, i ^ bits) for i in range(size) if i ^ bits...  3.52 us
    pad x1, local copies, waits for them, and re-layouts, shards(): state = jnp.pad(particles, ((0, 1), (0, 0)))  1.08 us
  transfers between devices with their start and end apart: 11, of which 2 were waited for; matrix products, arithmetic and copies ran while one was open for 0% of the time, Pallas kernels for 24%

profile of v3, /device:TPU:0, one launch (start us, length us, event | category | flops | bytes accessed | tf_op | source)
XLA Modules:
  0.0 52.4 jit_solution(14017169911799188692)
XLA Ops:
  0.6 1.1 %pad.4.state = f32[8,16384]{1,0:T(8,128)S(1)} pad(f32[7,16384]{1,0:T(8,128)} %param.8, f32[]{:T(128)} %constant.2.clone.1), padding=0_1x0_0 | pad | bytes 983044 | tf_op jit(solution)/shard_map/jit(_pad)/pad | solution.py:536
  1.7 0.6 %shard_map.95 = (f32[8,512]{1,0:T(8,128)S(1)}, s32[1,4,512]{2,1,0:T(4,128)S(1)}) custom-call(f32[8,16384]{1,0:T(8,128)S(1)} %pad.4.state, s32[1,4,512]{2,1,0:T(4,128)S(1)} %copy-done.2), custom_call_target="tpu_custom_call" | custom-call | tf_op jit(solution)/shard_map/pallas_call | solution.py:26
  2.4 3.0 %collective-permute-start = (f32[8,512]{1,0:T(8,128)S(1)}, f32[8,512]{1,0:T(8,128)S(1)}, u32[]{:S(2)}, u32[]{:S(2)}) collective-permute-start(f32[8,512]{1,0:T(8,128)S(1)} %get-tuple-element.31), channel_id=1, source_target_pairs={{0,8},{4,12},{8,0},{12,4},{16,24},{20,28},{24,16},{28,20},{1,9},{5... | collective-permute-start | bytes 49160 | tf_op jit(solution)/shard_map/ppermute | solution.py:514
  5.4 0.5 shard_map.96.codes
  5.9 0.2 copy-done.3
  6.0 0.7 %shard_map.97 = (f32[8,512]{1,0:T(8,128)S(1)}, s32[8,512]{1,0:T(8,128)S(1)}, s32[4,128,128]{2,1,0:T(8,128)S(1)}, s32[1,4,8]{2,1,0:T(4,128)S(1)}) custom-call(f32[8,16384]{1,0:T(8,128)S(1)} %pad.4.state, s32[1,4,512]{2,1,0:T(4,128)S(1)} %get-tuple-element.32.mig_rows, s32[4,128,128]{2,1,0:T(8,128)S(1)} %shard_map.96.codes, s32[1,4]{1,0:T(1,128)S(1)} %copy-done.4, ...), custom_call_target="tpu_custom_call" | custom-call | tf_op jit(solution)/shard_map/pallas_call | solution.py:26
  6.8 0.3 collective-permute-done.got0
  7.1 0.1 shard_map.98.after
  7.2 0.1 collective-permute-start.1
  7.3 1.5 %shard_map.100 = (f32[2,8,512]{2,1,0:T(8,128)S(1)}, s32[8,512]{1,0:T(8,128)S(1)}, f32[8,4096]{1,0:T(8,128)S(1)}, s32[4,8,128]{2,1,0:T(8,128)S(1)}) custom-call(f32[8,16384]{1,0:T(8,128)S(1)} %pad.4.state, s32[1,4,512]{2,1,0:T(4,128)S(1)} %get-tuple-element.32.mig_rows, s32[4,128,128]{2,1,0:T(8,128)S(1)} %get-tuple-element.35.codes.tables, ...), custom_call_target="tpu_custom_call" | custom-call | tf_op jit(solution)/shard_map/pallas_call | solution.py:26
  8.8 0.5 %shard_map.101 = (f32[8,2048]{1,0:T(8,128)S(1)}, f32[8,2048]{1,0:T(8,128)S(1)}, f32[8,2048]{1,0:T(8,128)S(1)}, f32[8,2048]{1,0:T(8,128)S(1)}) custom-call(f32[2,8,512]{2,1,0:T(8,128)S(1)} %get-tuple-element.39.cols, s32[8,512]{1,0:T(8,128)S(1)} %get-tuple-element.40.marks, f32[8,512]{1,0:T(8,128)S(1)} %collective-permute-done.got0, ...), custom_call_target="tpu_custom_call" | custom-call | tf_op jit(solution)/shard_map/pallas_call | solution.py:26
  9.3 4.2 %collective-permute-start.2 = (f32[8,2048]{1,0:T(8,128)S(1)}, f32[8,2048]{1,0:T(8,128)S(1)}, u32[]{:S(2)}, u32[]{:S(2)}) collective-permute-start(f32[8,2048]{1,0:T(8,128)S(1)} %get-tuple-element.44), channel_id=1, source_target_pairs={{0,3},{1,2},{2,1},{3,0},{4,7},{5,6},{6,5},{7,4},{8,11},{9,10},{10,... | collective-permute-start | bytes 196616 | tf_op jit(solution)/shard_map/ppermute | solution.py:514
  13.5 0.0 collective-permute-start.3
  13.5 0.6 %collective-permute-start.4 = (f32[8,2048]{1,0:T(8,128)S(1)}, f32[8,2048]{1,0:T(8,128)S(1)}, u32[]{:S(2)}, u32[]{:S(2)}) collective-permute-start(f32[8,2048]{1,0:T(8,128)S(1)} %get-tuple-element.46), channel_id=1, source_target_pairs={{0,1},{1,0},{2,3},{3,2},{4,5},{5,4},{6,7},{7,6},{8,9},{9,8},{10,11... | collective-permute-start | bytes 196616 | tf_op jit(solution)/shard_map/ppermute | solution.py:514
  14.2 0.1 copy.10.nbrs
  14.3 0.1 copy.11.far
  14.4 0.6 %copy-done = s32[1,2,8]{2,1,0:T(2,128)S(1)} copy-done((s32[1,2,8]{2,1,0:T(2,128)S(1)}, s32[1,2,8]{2,1,0:T(2,128)}, u32[]{:S(2)}) %copy-start) | copy-done | bytes 88
  14.9 1.5 %shard_map.99 = (f32[12,4,8,128]{3,2,1,0:T(8,128)S(1)}, f32[128,128]{1,0:T(8,128)S(1)}) custom-call(f32[8,16384]{1,0:T(8,128)S(1)} %pad.4.state, f32[8,512]{1,0:T(8,128)S(1)} %collective-permute-done.got0, f32[8,512]{1,0:T(8,128)S(1)} %collective-permute-done.1.got1, s32[4,128,128]{2,1,0:T(8,128)S(1)} %get-tuple-element.35.codes.tables, ...), custom_call_target="tpu_custom_call" | custom-call | tf_op jit(solution)/shard_map/pallas_call | solution.py:26
  16.5 3.2 %collective-permute-done.3.refs_2_ = f32[8,2048]{1,0:T(8,128)S(1)} collective-permute-done((f32[8,2048]{1,0:T(8,128)S(1)}, f32[8,2048]{1,0:T(8,128)S(1)}, u32[]{:S(2)}, u32[]{:S(2)}) %collective-permute-start.3) | collective-permute-done | bytes 65568 | tf_op jit(solution)/shard_map/ppermute | solution.py:514
  19.6 7.5 %shard_map.102 = (f32[12,8,8,128]{3,2,1,0:T(8,128)S(1)}, f32[128,128]{1,0:T(8,128)S(1)}, f32[8,128]{1,0:T(8,128)S(1)}, f32[8,128]{1,0:T(8,128)S(1)}, f32[8,128]{1,0:T(8,128)S(1)}, /*index=5*/f32[8,128]{1,0:T(8,128)S(1)}) custom-call(f32[12,4,8,128]{3,2,1,0:T(8,128)S(1)} %get-tuple-element.36.own, f32[128,128]{1,0:T(8,128)S(1)} %get-tuple-element.37.before, ...), custom_call_target="tpu_custom_call" | custom-call | tf_op jit(solution)/shard_map/pallas_call | solution.py:26
  27.1 2.5 %collective-permute-start.5 = (f32[8,128]{1,0:T(8,128)S(1)}, f32[8,128]{1,0:T(8,128)S(1)}, u32[]{:S(2)}, u32[]{:S(2)}) collective-permute-start(f32[8,128]{1,0:T(8,128)S(1)} %get-tuple-element.52), channel_id=1, source_target_pairs={{0,3},{1,2},{2,1},{3,0},{4,7},{5,6},{6,5},{7,4},{8,11},{9,10},{10,... | collective-permute-start | bytes 12296 | tf_op jit(solution)/shard_map/ppermute | solution.py:514
  29.7 0.0 collective-permute-start.6
  29.7 1.9 %collective-permute-start.7 = (f32[8,128]{1,0:T(8,128)S(1)}, f32[8,128]{1,0:T(8,128)S(1)}, u32[]{:S(2)}, u32[]{:S(2)}) collective-permute-start(f32[8,128]{1,0:T(8,128)S(1)} %get-tuple-element.54), channel_id=1, source_target_pairs={{0,1},{1,0},{2,3},{3,2},{4,5},{5,4},{6,7},{7,6},{8,9},{9,8},{10,11... | collective-permute-start | bytes 12296 | tf_op jit(solution)/shard_map/ppermute | solution.py:514
  31.6 4.4 %shard_map.103 = (f32[8,16384]{1,0:T(8,128)S(1)}, f32[128,128]{1,0:T(8,128)}) custom-call(f32[12,8,8,128]{3,2,1,0:T(8,128)S(1)} %get-tuple-element.47.near, f32[128,128]{1,0:T(8,128)S(1)} %get-tuple-element.48.density, s32[1,2,8]{2,1,0:T(2,128)S(1)} %copy-done, s32[1,2]{1,0:T(1,128)S(1)} %copy-done.1, s32[1,2,8,3]{3,2,1,0:T(8,128)S(1)} %copy.10.nbrs), custom_call_target="tpu_custom_call" | custom-call | tf_op jit(solution)/shard_map/pallas_call | solution.py:26
  36.0 0.0 collective-permute-done.5.refs_1_
  36.0 0.0 collective-permute-done.6.refs_2_
  36.0 6.6 %shard_map.104 = (f32[12,8,128]{2,1,0:T(8,128)S(1)}, f32[8,1024]{1,0:T(8,128)S(1)}, f32[8,1024]{1,0:T(8,128)S(1)}, f32[8,1024]{1,0:T(8,128)S(1)}, f32[8,1024]{1,0:T(8,128)S(1)}) custom-call(f32[12,8,8,128]{3,2,1,0:T(8,128)S(1)} %get-tuple-element.47.near, f32[128,128]{1,0:T(8,128)S(1)} %get-tuple-element.48.density, ...), custom_call_target="tpu_custom_call" | custom-call | tf_op jit(solution)/shard_map/pallas_call | solution.py:26
  42.6 2.5 %collective-permute-start.8 = (f32[8,1024]{1,0:T(8,128)S(1)}, f32[8,1024]{1,0:T(8,128)S(1)}, u32[]{:S(2)}, u32[]{:S(2)}) collective-permute-start(f32[8,1024]{1,0:T(8,128)S(1)} %get-tuple-element.57), channel_id=1, source_target_pairs={{0,3},{1,2},{2,1},{3,0},{4,7},{5,6},{6,5},{7,4},{8,11},{9,10},{10,... | collective-permute-start | bytes 98312 | tf_op jit(solution)/shard_map/ppermute | solution.py:514
  45.1 1.9 %collective-permute-start.10 = (f32[8,1024]{1,0:T(8,128)S(1)}, f32[8,1024]{1,0:T(8,128)S(1)}, u32[]{:S(2)}, u32[]{:S(2)}) collective-permute-start(f32[8,1024]{1,0:T(8,128)S(1)} %get-tuple-element.59), channel_id=1, source_target_pairs={{0,1},{1,0},{2,3},{3,2},{4,5},{5,4},{6,7},{7,6},{8,9},{9,8},{10,11... | collective-permute-start | bytes 98312 | tf_op jit(solution)/shard_map/ppermute | solution.py:514
  47.0 3.9 %shard_map.105.totals = f32[8,16384]{1,0:T(8,128)S(1)} custom-call(f32[12,8,8,128]{3,2,1,0:T(8,128)S(1)} %get-tuple-element.47.near, f32[128,128]{1,0:T(8,128)S(1)} %get-tuple-element.48.density, s32[1,2,8]{2,1,0:T(2,128)S(1)} %copy-done, s32[1,2]{1,0:T(1,128)S(1)} %copy-done.1, s32[1,2,8,3]{3,2,1,0:T(8,128)S(1)} %copy.10.nbrs, ...), custom_call_target="tpu_custom_call" | custom-call | tf_op jit(solution)/shard_map/pallas_call | solution.py:26
  51.0 0.0 collective-permute-done.9.refs_2_
  51.0 1.4 %shard_map.106 = f32[3,16384]{1,0:T(4,128)} custom-call(f32[8,16384]{1,0:T(8,128)S(1)} %shard_map.105.totals, s32[1,4,8]{2,1,0:T(4,128)S(1)} %get-tuple-element.38.exports, f32[8,1024]{1,0:T(8,128)S(1)} %get-tuple-element.56.refs_0_, f32[8,1024]{1,0:T(8,128)S(1)} %collective-permute-done.8.refs_1_, f32[8,1024]{1,0:T(8,128)S(1)} %collective-permute-done.9.refs_2_, ...), custom_call_target="tpu_custom_call" | custom-call | tf_op jit(solution)/shard_map/pallas_call | solution.py:26
  (19 shorter events, 0.0 us)
Async XLA Ops:
  0.6 1.1 %copy-start.2 = (s32[1,4,512]{2,1,0:T(4,128)S(1)}, s32[1,4,512]{2,1,0:T(4,128)}, u32[]{:S(2)}) copy-start(s32[1,4,512]{2,1,0:T(4,128)} %mig_rows.1) | copy-start | bytes 24580
  2.4 4.7 %collective-permute-start = (f32[8,512]{1,0:T(8,128)S(1)}, f32[8,512]{1,0:T(8,128)S(1)}, u32[]{:S(2)}, u32[]{:S(2)}) collective-permute-start(f32[8,512]{1,0:T(8,128)S(1)} %get-tuple-element.31), channel_id=1, source_target_pairs={{0,8},{4,12},{8,0},{12,4},{16,24},{20,28},{24,16},{28,20},{1,9},{5... | collective-permute-start | bytes 49160 | tf_op jit(solution)/shard_map/ppermute | solution.py:514
  5.4 0.7 %copy-start.3 = (s32[1,4,8]{2,1,0:T(4,128)S(1)}, s32[1,4,8]{2,1,0:T(4,128)}, u32[]{:S(2)}) copy-start(s32[1,4,8]{2,1,0:T(4,128)} %exports.1) | copy-start | bytes 388
  5.4 0.7 %copy-start.4 = (s32[1,4]{1,0:T(1,128)S(1)}, s32[1,4]{1,0:T(1,128)}, u32[]{:S(2)}) copy-start(s32[1,4]{1,0:T(1,128)} %counts.6) | copy-start | bytes 52
  7.2 1.6 %collective-permute-start.1 = (f32[8,512]{1,0:T(8,128)S(1)}, f32[8,512]{1,0:T(8,128)S(1)}, u32[]{:S(2)}, u32[]{:S(2)}) collective-permute-start(f32[8,512]{1,0:T(8,128)S(1)} %shard_map.98.after), channel_id=1, source_target_pairs={{0,4},{4,0},{8,12},{12,8},{16,20},{20,16},{24,28},{28,24},{1,5},{5... | collective-permute-start | bytes 49160 | tf_op jit(solution)/shard_map/ppermute | solution.py:514
  9.3 4.9 %copy-start.6 = (s32[1,2,8,3]{2,1,3,0:T(2,128)S(1)}, s32[1,2,8,3]{2,1,3,0:T(2,128)}, u32[]{:S(2)}) copy-start(s32[1,2,8,3]{2,1,3,0:T(2,128)} %param.13) | copy-start | bytes 580
  9.3 7.1 %collective-permute-start.2 = (f32[8,2048]{1,0:T(8,128)S(1)}, f32[8,2048]{1,0:T(8,128)S(1)}, u32[]{:S(2)}, u32[]{:S(2)}) collective-permute-start(f32[8,2048]{1,0:T(8,128)S(1)} %get-tuple-element.44), channel_id=1, source_target_pairs={{0,3},{1,2},{2,1},{3,0},{4,7},{5,6},{6,5},{7,4},{8,11},{9,10},{10,... | collective-permute-start | bytes 196616 | tf_op jit(solution)/shard_map/ppermute | solution.py:514
  13.5 6.1 %collective-permute-start.3 = (f32[8,2048]{1,0:T(8,128)S(1)}, f32[8,2048]{1,0:T(8,128)S(1)}, u32[]{:S(2)}, u32[]{:S(2)}) collective-permute-start(f32[8,2048]{1,0:T(8,128)S(1)} %get-tuple-element.45), channel_id=1, source_target_pairs={{0,2},{1,3},{2,0},{3,1},{4,6},{5,7},{6,4},{7,5},{8,10},{9,11},{10,... | collective-permute-start | bytes 196616 | tf_op jit(solution)/shard_map/ppermute | solution.py:514
  13.5 0.7 %copy-start.5 = (s32[1,2,8,4]{2,3,1,0:T(4,128)S(1)}, s32[1,2,8,4]{2,3,1,0:T(4,128)}, u32[]{:S(2)}) copy-start(s32[1,2,8,4]{2,3,1,0:T(4,128)} %param.14) | copy-start | bytes 772
  13.5 6.1 %collective-permute-start.4 = (f32[8,2048]{1,0:T(8,128)S(1)}, f32[8,2048]{1,0:T(8,128)S(1)}, u32[]{:S(2)}, u32[]{:S(2)}) collective-permute-start(f32[8,2048]{1,0:T(8,128)S(1)} %get-tuple-element.46), channel_id=1, source_target_pairs={{0,1},{1,0},{2,3},{3,2},{4,5},{5,4},{6,7},{7,6},{8,9},{9,8},{10,11... | collective-permute-start | bytes 196616 | tf_op jit(solution)/shard_map/ppermute | solution.py:514
  14.3 0.7 %copy-start = (s32[1,2,8]{2,1,0:T(2,128)S(1)}, s32[1,2,8]{2,1,0:T(2,128)}, u32[]{:S(2)}) copy-start(s32[1,2,8]{2,1,0:T(2,128)} %ids.9) | copy-start | bytes 196
  14.3 0.7 %copy-start.1 = (s32[1,2]{1,0:T(1,128)S(1)}, s32[1,2]{1,0:T(1,128)}, u32[]{:S(2)}) copy-start(s32[1,2]{1,0:T(1,128)} %counts.11) | copy-start | bytes 28
  27.1 8.8 %collective-permute-start.5 = (f32[8,128]{1,0:T(8,128)S(1)}, f32[8,128]{1,0:T(8,128)S(1)}, u32[]{:S(2)}, u32[]{:S(2)}) collective-permute-start(f32[8,128]{1,0:T(8,128)S(1)} %get-tuple-element.52), channel_id=1, source_target_pairs={{0,3},{1,2},{2,1},{3,0},{4,7},{5,6},{6,5},{7,4},{8,11},{9,10},{10,... | collective-permute-start | bytes 12296 | tf_op jit(solution)/shard_map/ppermute | solution.py:514
  29.7 6.3 %collective-permute-start.6 = (f32[8,128]{1,0:T(8,128)S(1)}, f32[8,128]{1,0:T(8,128)S(1)}, u32[]{:S(2)}, u32[]{:S(2)}) collective-permute-start(f32[8,128]{1,0:T(8,128)S(1)} %get-tuple-element.53), channel_id=1, source_target_pairs={{0,2},{1,3},{2,0},{3,1},{4,6},{5,7},{6,4},{7,5},{8,10},{9,11},{10,... | collective-permute-start | bytes 12296 | tf_op jit(solution)/shard_map/ppermute | solution.py:514
  29.7 6.3 %collective-permute-start.7 = (f32[8,128]{1,0:T(8,128)S(1)}, f32[8,128]{1,0:T(8,128)S(1)}, u32[]{:S(2)}, u32[]{:S(2)}) collective-permute-start(f32[8,128]{1,0:T(8,128)S(1)} %get-tuple-element.54), channel_id=1, source_target_pairs={{0,1},{1,0},{2,3},{3,2},{4,5},{5,4},{6,7},{7,6},{8,9},{9,8},{10,11... | collective-permute-start | bytes 12296 | tf_op jit(solution)/shard_map/ppermute | solution.py:514
  42.6 8.4 %collective-permute-start.8 = (f32[8,1024]{1,0:T(8,128)S(1)}, f32[8,1024]{1,0:T(8,128)S(1)}, u32[]{:S(2)}, u32[]{:S(2)}) collective-permute-start(f32[8,1024]{1,0:T(8,128)S(1)} %get-tuple-element.57), channel_id=1, source_target_pairs={{0,3},{1,2},{2,1},{3,0},{4,7},{5,6},{6,5},{7,4},{8,11},{9,10},{10,... | collective-permute-start | bytes 98312 | tf_op jit(solution)/shard_map/ppermute | solution.py:514
  45.1 5.9 %collective-permute-start.9 = (f32[8,1024]{1,0:T(8,128)S(1)}, f32[8,1024]{1,0:T(8,128)S(1)}, u32[]{:S(2)}, u32[]{:S(2)}) collective-permute-start(f32[8,1024]{1,0:T(8,128)S(1)} %get-tuple-element.58), channel_id=1, source_target_pairs={{0,2},{1,3},{2,0},{3,1},{4,6},{5,7},{6,4},{7,5},{8,10},{9,11},{10,... | collective-permute-start | bytes 98312 | tf_op jit(solution)/shard_map/ppermute | solution.py:514
  45.1 5.9 %collective-permute-start.10 = (f32[8,1024]{1,0:T(8,128)S(1)}, f32[8,1024]{1,0:T(8,128)S(1)}, u32[]{:S(2)}, u32[]{:S(2)}) collective-permute-start(f32[8,1024]{1,0:T(8,128)S(1)} %get-tuple-element.59), channel_id=1, source_target_pairs={{0,1},{1,0},{2,3},{3,2},{4,5},{5,4},{6,7},{7,6},{8,9},{9,8},{10,11... | collective-permute-start | bytes 98312 | tf_op jit(solution)/shard_map/ppermute | solution.py:514

commit v4 on v3

v4 whole, which is shorter than its diff:
```python
import math

import jax
import jax.numpy as jnp
from jax import lax
from jax.experimental import pallas as pl
from jax.experimental.pallas import tpu as pltpu
from jax.sharding import PartitionSpec as P

BLK = 128
TOTACT = 12
KERNEL_NORM = 21.0 / (16.0 * math.pi)
FORCE_NORM = 5.0 * KERNEL_NORM * 32.0 * (2.0 / 3.0)
TINY = 1e-30
F32 = jnp.float32
I32 = jnp.int32
VMEM = pltpu.VMEM
SMEM = pltpu.SMEM
DMA = pltpu.SemaphoreType.DMA


def call(kernel, out_shape, *args, smem=(), scratch=(), limit=16 << 20, cost=0):
    def space(n):
        return SMEM if n in smem else VMEM

    return pl.pallas_call(
        kernel,
        out_shape=out_shape,
        in_specs=[pl.BlockSpec(memory_space=space(n)) for n in range(len(args))],
        out_specs=jax.tree.map(lambda _: pl.BlockSpec(memory_space=VMEM), out_shape),
        scratch_shapes=list(scratch),
        compiler_params=pltpu.CompilerParams(vmem_limit_bytes=limit),
        cost_estimate=pl.CostEstimate(flops=0, transcendentals=0, bytes_accessed=cost)
        if cost
        else None,
    )(*args)


def shape(*dims, dtype=F32):
    return jax.ShapeDtypeStruct(dims, dtype)


def wide(row):
    return jnp.broadcast_to(row, (8, BLK))


def lanes(block):
    return pl.ds(pl.multiple_of(block * BLK, BLK), BLK)


def chunk(c):
    return slice(c * BLK, (c + 1) * BLK)


def take(values, index):
    return jnp.take_along_axis(values, index, axis=1)


def patch(values, code, tables):
    lane = code & (BLK - 1)
    which = code >> 7
    for n, table in enumerate(tables):
        values = jnp.where(which == n, take(table, lane), values)
    return values


def tables_of(ref, count, start=0):
    return [ref[:, chunk(start + c)] for c in range(count)]


def columns(state, slots):
    block = slots >> 7
    lane = slots & (BLK - 1)
    found = jnp.zeros((8, BLK), F32)
    for b in range(state.shape[1] // BLK):
        found = jnp.where(block == b, take(state[:, chunk(b)], lane), found)
    return found


def fetch(sources, targets, sems):
    copies = [
        pltpu.make_async_copy(a, b, sems.at[n]) for n, (a, b) in enumerate(zip(sources, targets))
    ]
    for copy in copies:
        copy.start()
    return copies


def fetch_scratch(arrays):
    return [SMEM(a.shape, I32) for a in arrays] + [DMA((len(arrays),))]


def first_kernel(particles, ints, out, state):
    state[0:7, :] = particles[...]
    state[7:8, :] = jnp.zeros((1, state.shape[1]), F32)
    for c in range(ints.shape[1] // BLK):
        out[:, chunk(c)] = columns(state, wide(ints[0:1, chunk(c)]))


def code_table(ints, level, blocks):
    mig = ints.shape[1]
    slots = ints[level : level + 1, :]
    k = lax.broadcasted_iota(I32, (1, mig), 1)
    low = (k & (BLK - 1)).astype(F32)
    high = ((k >> 7) + 1).astype(F32)
    in_block = lax.broadcasted_iota(I32, (blocks, mig), 0) == (slots >> 7)
    in_lane = lax.broadcasted_iota(I32, (BLK, mig), 0) == (slots & (BLK - 1))
    left = jnp.concatenate([jnp.where(in_block, low, 0.0), jnp.where(in_block, high, 0.0)], axis=0)
    right = jnp.where(in_lane, 1.0, 0.0)
    both = lax.dot_general(
        left.astype(jnp.bfloat16),
        right.astype(jnp.bfloat16),
        (((1,), (1,)), ((), ())),
        preferred_element_type=F32,
    )
    low, high = both[:blocks], both[blocks:]
    return jnp.where(high > 0.5, (high - 1.0) * BLK + low, -1.0).astype(I32)


def codes_kernel(ints, codes):
    for level in range(4):
        codes[level] = code_table(ints, level, codes.shape[1])


def code_at(table, slots):
    block = slots >> 7
    lane = slots & (BLK - 1)
    row = lax.broadcasted_iota(I32, (8, BLK), 0)
    found = jnp.full((8, BLK), -1, I32)
    for v in range(table.shape[0] // 8):
        piece = take(table[8 * v : 8 * v + 8, :], lane)
        found = jnp.where(block == row + 8 * v, piece, found)
    return jnp.max(found, axis=0, keepdims=True)


def early_tables_kernel(state, ints, codes, cols, marks, tables):
    mig = ints.shape[1]
    valid = []
    for level in range(4):
        code = codes[level]
        valid.append(jnp.where(code < ints[4:5, level : level + 1], code, -1))
    tables[0] = jnp.where(valid[1] >= 0, valid[1] + mig, valid[0])
    tables[1] = jnp.where(valid[3] >= 0, valid[3] + mig, valid[2])
    tables[2] = valid[2]
    tables[3] = valid[0]
    for c in range(mig // BLK):
        slots = wide(ints[1:2, chunk(c)])
        marks[0:1, chunk(c)] = code_at(tables.at[3], slots)
        cols[:, chunk(c)] = columns(state, slots)


def late_tables_kernel(
    state, ints, tables, after, cols, marks, raw, code_rows, exported, sems
):
    peers, slots, _ = code_rows.shape
    copies = fetch([ints.at[pl.ds(8, peers), pl.ds(0, BLK)]], [exported], sems)
    for c in range(ints.shape[1] // BLK):
        two, three = (wide(ints[level : level + 1, chunk(c)]) for level in (2, 3))
        marks[1:2, chunk(c)] = code_at(tables.at[0], two)
        marks[2:3, chunk(c)] = code_at(tables.at[0], three)
        marks[3:4, chunk(c)] = code_at(tables.at[2], three)
        cols[0, :, chunk(c)] = columns(state, two)
        cols[1, :, chunk(c)] = columns(state, three)
    for copy in copies:
        copy.wait()
    me = lax.axis_index("gy")
    row = lax.broadcasted_iota(I32, (8, BLK), 0)
    for q in range(peers):
        for t in range(slots):
            block = exported[me ^ q, t]
            code = wide(tables[1, pl.ds(block, 1), :]).astype(F32)
            raw[:, chunk(q * slots + t)] = jnp.where(row == 7, code, state[:, lanes(block)])
            code_rows[q, t : t + 1, :] = tables[0, pl.ds(block, 1), :]


def second_kernel(cols, marks, got0, out):
    count = got0.shape[1] // BLK
    tables = tables_of(got0, count)
    for c in range(count):
        out[:, chunk(c)] = patch(cols[:, chunk(c)], wide(marks[0:1, chunk(c)]), tables)


def early_block(state, codes, tables, block):
    row = lax.broadcasted_iota(I32, (8, BLK), 0)
    patched = patch(state[:, lanes(block)], wide(codes[0, pl.ds(block, 1), :]), tables)
    return jnp.where(row == 7, wide(codes[1, pl.ds(block, 1), :]).astype(F32), patched)


def export_kernel(cols, marks, got0, got1, raw, code_rows, *outs):
    count = got0.shape[1] // BLK
    slots = code_rows.shape[1]
    tables = tables_of(got0, count) + tables_of(got1, count)
    row = lax.broadcasted_iota(I32, (8, BLK), 0)
    for c in range(count):
        two = patch(cols[0, :, chunk(c)], wide(marks[1:2, chunk(c)]), tables)
        three = patch(cols[1, :, chunk(c)], wide(marks[2:3, chunk(c)]), tables)
        three = jnp.where(row == 7, wide(marks[3:4, chunk(c)]).astype(F32), three)
        for out in outs:
            out[:, chunk(c)] = two
            out[:, chunk(count + c)] = three
    for q, out in enumerate(outs):
        for t in range(slots):
            values = raw[:, chunk(q * slots + t)]
            patched = patch(values, wide(code_rows[q, t : t + 1, :]), tables)
            out[:, chunk(2 * count + t)] = jnp.where(row == 7, values, patched)


def live_slot(counts, n, nact):
    second = n >= counts[0, 0]
    return jnp.where(second, 1, 0), jnp.where(second, jnp.minimum(n - counts[0, 0], nact - 1), n)


def own_kernel(state, got0, got1, codes, ids, counts, nbrs, own, density):
    count = got0.shape[1] // BLK
    blocks = density.shape[0]
    tables = tables_of(got0, count) + tables_of(got1, count)
    last = [wide(table[6:7, :]) for table in tables]
    for b in range(blocks):
        density[b : b + 1, :] = state[6:7, chunk(b)]
    for v in range(blocks // 8):
        part = slice(8 * v, 8 * v + 8)
        density[part, :] = patch(density[part, :], codes[0, part, :], last)
    nact = ids.shape[2]

    for n in range(TOTACT):
        which, i = live_slot(counts, n, nact)
        wanted = [ids[0, which, i]] + [nbrs[0, which, i, t] for t in range(nbrs.shape[3])]
        for t, block in enumerate(wanted):
            own[n, t] = early_block(state, codes, tables, block)


def spread(rows, *outs):
    columns_of = jnp.transpose(jnp.concatenate((rows + rows)[:8], axis=0))
    for k in range(len(rows)):
        values = jnp.broadcast_to(columns_of[:, k : k + 1], (BLK, BLK))
        for out in outs:
            out[k] = values


def pair_sums(near, n, centre, sums, inside, outside):
    local = inside.shape[1] // BLK
    for g in range(BLK // 8):
        part = slice(8 * g, 8 * g + 8)
        cx, cy, cz, cm, ch = (centre[k, part, :] for k in range(5))
        half = 0.5 / ch
        total = None
        for t in range(8):
            x, y, z, m, h = (wide(near[n, k, t : t + 1, :]) for k in range(5))
            dx, dy, dz = cx - x, cy - y, cz - z
            square = dx * dx + dy * dy + dz * dz
            distance = square * lax.rsqrt(jnp.maximum(square, TINY))
            fall = jnp.maximum(1.0 - distance * half, 0.0)
            fall2 = fall * fall
            term = fall2 * fall2 * (1.25 - fall) * m
            total = term if total is None else total + term
            inverse = 1.0 / (ch + h)
            inv2 = inverse * inverse
            slope = jnp.maximum(inverse - distance * inv2, 0.0)
            weight = slope * slope * slope * inv2 * (cm * m)
            if t < local:
                row = 8 * (g * local + t)
                inside[n, row : row + 8, :] = weight
            else:
                row = 8 * (g * (8 - local) + t - local)
                outside[n, row : row + 8, :] = weight
        sums[n, part, :] = total


def back_sums(near, n, centre, press, outside, others):
    far = outside.shape[1] // BLK
    first = 8 - far
    ghost = [[wide(near[n, k, t : t + 1, :]) for k in range(3)] for t in range(first, 8)]
    sums = [[None] * 6 for _ in range(far)]
    for g in range(BLK // 8):
        part = slice(8 * g, 8 * g + 8)
        here = [centre[n, k, part, :] for k in range(3)]
        cp = press[n, part, :]
        for t in range(far):
            row = 8 * (g * far + t)
            weight = outside[n, row : row + 8, :]
            for k in range(3):
                push = weight * (here[k] - ghost[t][k])
                for place, value in ((k, push * cp), (3 + k, push)):
                    old = sums[t][place]
                    sums[t][place] = value if old is None else old + value
    for t in range(far):
        for k in range(6):
            row = 8 * (k * far + t)
            others[n, row : row + 8, :] = sums[t][k]


def make_density_kernel(peers, slots):
    def density_kernel(own, before, codes, ids, counts, far, exports, *refs):
        sent = by_partner(refs[:peers])
        near, density, centre, press, inside, outside = refs[peers : peers + 6]
        outs = refs[peers + 6 : 2 * peers + 6]
        (late_three, ghosts, first, second, sums, fresh, others, rows, back, *small) = refs[
            2 * peers + 6 :
        ]
        copies = fetch([ids, counts, far, exports], small[:4], small[4])
        ids, counts, far, exports = small[:4]
        count = late_three.shape[2] // BLK
        blocks = density.shape[0]
        me = lax.axis_index("gy")

        for q in range(peers):
            tables = tables_of(sent[q ^ 2], count)
            for c in range(count):
                values = sent[q][:, chunk(count + c)]
                code = wide(values[7:8, :]).astype(I32)
                late_three[q, :, chunk(c)] = patch(values, code, tables)

        def settle(values, q):
            code = wide(values[7:8, :]).astype(I32)
            tables = tables_of(sent[q ^ 2], count)
            tables += [late_three[q ^ 1, :, chunk(c)] for c in range(count)]
            return patch(values, code, tables)

        for q in range(peers):
            for t in range(slots):
                ghosts[:, chunk(q * slots + t)] = settle(sent[q][:, chunk(2 * count + t)], q)

        later = [sent[2][6:7, chunk(c)] for c in range(count)]
        later = [wide(x) for x in later + [late_three[1, 6:7, chunk(c)] for c in range(count)]]
        for v in range(blocks // 8):
            part = slice(8 * v, 8 * v + 8)
            density[part, :] = patch(before[part, :], codes[1, part, :], later)
        back[...] = jnp.zeros_like(back)

        for copy in copies:
            copy.wait()
        live = counts[0, 0] + counts[0, 1]
        nact = ids.shape[2]
        inner = own.shape[1]
        ngh = far.shape[3]

        def far_of(n):
            which, i = live_slot(counts, n, nact)
            return [far[0, which, i, t] ^ (me * slots) for t in range(ngh)]

        for n in range(TOTACT):
            for t in range(inner):
                near[n, :, t, :] = settle(own[n, t], 0)
            for t, g in enumerate(far_of(n)):
                near[n, :, inner + t, :] = ghosts[:, lanes(g)]

        def prepare(n, buffer):
            spread([near[n, k, 0:1, :] for k in range(5)], buffer, centre.at[n])

        prepare(0, first)

        def step(p, _):
            n = 2 * p
            prepare(n + 1, second)
            pair_sums(near, n, first, sums, inside, outside)
            prepare(jnp.minimum(n + 2, TOTACT - 1), first)
            pair_sums(near, n + 1, second, sums, inside, outside)
            return 0

        lax.fori_loop(0, (live + 1) // 2, step, 0)
        for n in range(TOTACT):
            h = near[n, 4, 0:1, :]
            total = jnp.sum(jnp.transpose(sums[n]), axis=0, keepdims=True)
            fresh[n : n + 1, :] = total * (4.0 * KERNEL_NORM / (h * h * h))
        pressures = [near[n, 5, 0:1, :] / fresh[n : n + 1, :] for n in range(TOTACT)]
        pressures = jnp.concatenate(pressures + pressures[: 16 - TOTACT], axis=0)
        pressures = jnp.transpose(pressures)
        for n in range(TOTACT):
            press[n] = jnp.broadcast_to(pressures[:, n : n + 1], (BLK, BLK))

        def back_step(n, _):
            back_sums(near, n, centre, press, outside, others)
            which, i = live_slot(counts, n, nact)
            density[pl.ds(ids[0, which, i], 1), :] = fresh[pl.ds(n, 1), :]
            return 0

        lax.fori_loop(0, live, back_step, 0)
        for n in range(TOTACT):
            for t in range(ngh):
                m = near[n, 3, inner + t : inner + t + 1, :]
                u = near[n, 5, inner + t : inner + t + 1, :]
                scale = -FORCE_NORM / m
                for k in range(6):
                    row = 8 * (k * ngh + t)
                    total = jnp.sum(others[n, row : row + 8, :], axis=0, keepdims=True)
                    rows[n, k, t : t + 1, :] = total * (scale if k < 3 else scale * u)

        def place(n, _):
            for t, g in enumerate(far_of(n)):
                back[0:6, lanes(g)] += rows[n, 0:6, t, :]
            return 0

        lax.fori_loop(0, live, place, 0)
        for q in range(peers):
            outs[q][...] = back[:, q * slots * BLK : (q + 1) * slots * BLK]
            for t in range(slots):
                rho = density[pl.ds(exports[0, me ^ q, t], 1), :]
                outs[q][6:7, chunk(t)] = rho

    return density_kernel


def inner_sums(near, n, centre, press, others_press, inside, sums, others):
    local = inside.shape[1] // BLK
    tile = [[wide(near[n, k, t : t + 1, :]) for k in range(3)] for t in range(local)]
    theirs = [wide(others_press[n, t : t + 1, :]) for t in range(local)]
    pushed = [[None] * 3 for _ in range(local)]
    for g in range(BLK // 8):
        part = slice(8 * g, 8 * g + 8)
        here = [centre[n, k, part, :] for k in range(3)]
        cp = press[n, part, :]
        total = [None] * 3
        for t in range(local):
            row = 8 * (g * local + t)
            weight = inside[n, row : row + 8, :] * (cp + theirs[t])
            for k in range(3):
                push = weight * (here[k] - tile[t][k])
                total[k] = push if total[k] is None else total[k] + push
                if t > 0:
                    old = pushed[t][k]
                    pushed[t][k] = push if old is None else old + push
        for k in range(3):
            sums[n, k, part, :] = total[k]
    for t in range(1, local):
        for k in range(3):
            row = 8 * (k * local + t)
            others[n, row : row + 8, :] = pushed[t][k]


def inner_kernel(
    near, density, centre, press, inside, ids, counts, nbrs, totals, sums, density_out, *refs
):
    rho, others_press, others, rows = refs
    density_out[...] = density[...]
    totals[...] = jnp.zeros_like(totals)
    live = counts[0, 0] + counts[0, 1]
    nact = ids.shape[2]
    inner = 1 + nbrs.shape[3]

    def blocks_of(n):
        which, i = live_slot(counts, n, nact)
        return [ids[0, which, i]] + [nbrs[0, which, i, t] for t in range(nbrs.shape[3])]

    for n in range(TOTACT):
        for t, block in enumerate(blocks_of(n)):
            rho[n, t : t + 1, :] = density[pl.ds(block, 1), :]
    for n in range(TOTACT):
        others_press[n] = near[n, 5] / rho[n]

    def step(n, _):
        inner_sums(near, n, centre, press, others_press, inside, sums, others)
        return 0

    lax.fori_loop(0, live, step, 0)
    for n in range(TOTACT):
        for t in range(1, inner):
            scale = -FORCE_NORM / near[n, 3, t : t + 1, :]
            for k in range(3):
                row = 8 * (k * inner + t)
                total = jnp.sum(others[n, row : row + 8, :], axis=0, keepdims=True)
                rows[n, k, t : t + 1, :] = total * scale

    def place(n, _):
        for t, block in enumerate(blocks_of(n)):
            if t > 0:
                totals[0:3, lanes(block)] += rows[n, 0:3, t, :]
        return 0

    lax.fori_loop(0, live, place, 0)


def outer_sums(near, n, centre, press, others_press, outside, before, sums):
    far = outside.shape[1] // BLK
    first = 8 - far
    tile = [[wide(near[n, k, t : t + 1, :]) for k in range(3)] for t in range(first, 8)]
    theirs = [wide(others_press[n, t : t + 1, :]) for t in range(first, 8)]
    for g in range(BLK // 8):
        part = slice(8 * g, 8 * g + 8)
        here = [centre[n, k, part, :] for k in range(3)]
        cp = press[n, part, :]
        total = [before[n, k, part, :] for k in range(3)]
        for t in range(far):
            row = 8 * (g * far + t)
            weight = outside[n, row : row + 8, :] * (cp + theirs[t])
            for k in range(3):
                total[k] = total[k] + weight * (here[k] - tile[t][k])
        for k in range(3):
            sums[n, k, part, :] = total[k]


def make_outer_kernel(peers, slots):
    def outer_kernel(
        near, density, centre, press, outside, totals, before, ids, counts, far, exports, *refs
    ):
        got = by_partner(refs[:peers])
        out, far_rho, rho, others_press, sums, rows, *small = refs[peers:]
        copies = fetch([ids, counts, far, exports], small[:4], small[4])
        ids, counts, far, exports = small[:4]
        for q in range(peers):
            for t in range(slots):
                g = q * slots + t
                far_rho[g : g + 1, :] = got[q][6:7, chunk(t)]
        out[...] = totals[0:3, :]
        me = lax.axis_index("gy")
        nact = ids.shape[2]
        ngh = far.shape[3]
        for copy in copies:
            copy.wait()
        live = counts[0, 0] + counts[0, 1]
        for n in range(TOTACT):
            which, i = live_slot(counts, n, nact)
            for t in range(ngh):
                g = far[0, which, i, t] ^ (me * slots)
                rho[n, 8 - ngh + t : 9 - ngh + t, :] = far_rho[pl.ds(g, 1), :]
        for n in range(TOTACT):
            others_press[n] = near[n, 5] / rho[n]

        def step(n, _):
            outer_sums(near, n, centre, press, others_press, outside, before, sums)
            return 0

        lax.fori_loop(0, live, step, 0)
        for n in range(TOTACT):
            scale = FORCE_NORM / near[n, 3, 0:1, :]
            for k in range(3):
                total = jnp.sum(jnp.transpose(sums[n, k]), axis=0, keepdims=True)
                rows[n, k : k + 1, :] = total * scale
        for q in range(peers):
            for t in range(slots):
                b = exports[0, me ^ q, t]
                own_rho = density[pl.ds(b, 1), :]
                value = got[q][0:3, chunk(t)] + got[q][3:6, chunk(t)] / own_rho
                out[0:3, lanes(b)] += value

        def place(n, _):
            which, i = live_slot(counts, n, nact)
            out[0:3, lanes(ids[0, which, i])] += rows[n, 0:3, :]
            return 0

        lax.fori_loop(0, live, place, 0)

    return outer_kernel


def crossed(block, axis, bits):
    size = lax.axis_size(axis)
    return lax.ppermute(block, axis, [(i, i ^ bits) for i in range(size) if i ^ bits < size])


def exchanged(parts):
    return [parts[0]] + [crossed(parts[q], "gy", q) for q in range(len(parts) - 1, 0, -1)]


def by_partner(refs):
    return [refs[0]] + list(refs[:0:-1])


def shards(
    particles, mig_count, mig_rows, active_ids, active_count, local_nbrs, ghost_slots, export_blocks
):
    peers = lax.axis_size("gy")
    slots = export_blocks.shape[2]
    per_dev = particles.shape[1]
    blocks = per_dev // BLK
    mig = mig_rows.shape[2]
    inner = 1 + local_nbrs.shape[3]
    wide_total = peers * slots * BLK

    ints = jnp.concatenate(
        [
            mig_rows[0],
            jnp.pad(mig_count, ((0, 3), (0, mig - 4))),
            jnp.pad(export_blocks[0], ((0, 0), (0, mig - slots))),
        ],
        axis=0,
    )
    sent0, state = call(first_kernel, [shape(8, mig), shape(8, per_dev)], particles, ints)
    codes = call(codes_kernel, shape(4, blocks, BLK, dtype=I32), ints)
    got0 = crossed(sent0, "gx", 2)
    cols1, marks1, tables = call(
        early_tables_kernel,
        [shape(8, mig), shape(8, mig, dtype=I32), shape(4, blocks, BLK, dtype=I32)],
        state,
        ints,
        codes,
    )
    sent1 = call(second_kernel, shape(8, mig), cols1, marks1, got0)
    got1 = crossed(sent1, "gx", 1)
    cols, marks, raw, code_rows = call(
        late_tables_kernel,
        [
            shape(2, 8, mig),
            shape(8, mig, dtype=I32),
            shape(8, wide_total),
            shape(peers, slots, BLK, dtype=I32),
        ],
        state,
        ints,
        tables,
        sent1,
        scratch=[SMEM((peers, BLK), I32), DMA((1,))],
    )
    packs = call(
        export_kernel,
        [shape(8, 2 * mig + slots * BLK)] * peers,
        cols,
        marks,
        got0,
        got1,
        raw,
        code_rows,
    )
    sent = exchanged(packs)
    own, before = call(
        own_kernel,
        [shape(TOTACT, inner, 8, BLK), shape(blocks, BLK)],
        state,
        got0,
        got1,
        tables,
        active_ids,
        active_count,
        local_nbrs,
        smem=(4, 5, 6),
    )
    indices = [active_ids, active_count, ghost_slots, export_blocks]
    local = shape(TOTACT, inner * BLK, BLK)
    remote = shape(TOTACT, (8 - inner) * BLK, BLK)
    near, density, centre, press, inside, outside, *returns = call(
        make_density_kernel(peers, slots),
        [
            shape(TOTACT, 8, 8, BLK),
            shape(blocks, BLK),
            shape(TOTACT, 5, BLK, BLK),
            shape(TOTACT, BLK, BLK),
            local,
            remote,
        ]
        + [shape(8, slots * BLK)] * peers,
        own,
        before,
        tables,
        *indices,
        *sent,
        scratch=[
            VMEM((peers, 8, mig), F32),
            VMEM((8, wide_total), F32),
            VMEM((5, BLK, BLK), F32),
            VMEM((5, BLK, BLK), F32),
            VMEM((TOTACT, BLK, BLK), F32),
            VMEM((TOTACT, BLK), F32),
            VMEM((TOTACT, 6 * (8 - inner) * 8, BLK), F32),
            VMEM((TOTACT, 8, 8, BLK), F32),
            VMEM((8, wide_total), F32),
        ]
        + fetch_scratch(indices),
    )
    got = exchanged(returns)
    totals, sums, density_out = call(
        inner_kernel,
        [shape(8, per_dev), shape(TOTACT, 3, BLK, BLK), shape(blocks, BLK)],
        near,
        density,
        centre,
        press,
        inside,
        active_ids,
        active_count,
        local_nbrs,
        smem=(5, 6, 7),
        scratch=[
            VMEM((TOTACT, 8, BLK), F32),
            VMEM((TOTACT, 8, BLK), F32),
            VMEM((TOTACT, 3 * inner * 8, BLK), F32),
            VMEM((TOTACT, 8, 8, BLK), F32),
        ],
    )
    accel = call(
        make_outer_kernel(peers, slots),
        shape(3, per_dev),
        near,
        density,
        centre,
        press,
        outside,
        totals,
        sums,
        *indices,
        *got,
        scratch=[
            VMEM((peers * slots, BLK), F32),
            VMEM((TOTACT, 8, BLK), F32),
            VMEM((TOTACT, 8, BLK), F32),
            VMEM((TOTACT, 3, BLK, BLK), F32),
            VMEM((TOTACT, 8, BLK), F32),
        ]
        + fetch_scratch(indices),
    )
    return density_out.reshape(-1), accel


def solution(mesh):
    both = ("gx", "gy")
    placed = (
        P(None, both),
        P(both, None),
        P(both, None, None),
        P(both, None, None),
        P(both, None),
        P(both, None, None, None),
        P(both, None, None, None),
        P(both, None, None),
    )
    return jax.shard_map(
        shards,
        mesh=mesh,
        in_specs=placed,
        out_specs=(P(both), P(None, both)),
        check_vma=False,
    )
```

time: 52.7 us -> 44.4 us (0.84)
  Pallas kernels: 29.3 us -> 24.8 us
  starting transfers between devices: 16.8 us -> 12.4 us
  waiting for transfers between devices: 3.52 us -> 1.6 us
  local copies, waits for them, and re-layouts: 2.04 us -> 3.91 us
  other arithmetic: 0 us -> 0.76 us
    pallas_call x12 -> x10, Pallas kernels: 29.3 us -> 24.8 us  [call(): pl.pallas_call(kernel, out_shape=out_shape, in_specs=[pl.BlockSpec(memory...]
    ppermute x11 -> x8, starting transfers between devices: 16.8 us -> 12.4 us  [crossed(): lax.ppermute(block, axis, [(i, i ^ bits) for i in range(size) if i ^ bits...]
    unnamed x16 -> x10, local copies, waits for them, and re-layouts: 0.96 us -> 3.91 us
    ppermute x11 -> x8, waiting for transfers between devices: 3.52 us -> 1.6 us  [crossed(): lax.ppermute(block, axis, [(i, i ^ bits) for i in range(size) if i ^ bits...]
    pad x1 -> x0, local copies, waits for them, and re-layouts: 1.08 us -> none  [shards(): state = jnp.pad(particles, ((0, 1), (0, 0)))]
    concatenate x0 -> x1, other arithmetic: none -> 0.76 us  [shards(): jnp.concatenate([mig_rows[0], jnp.pad(mig_count, ((0, 3), (0, mig - 4))),...]
  transfers between devices with their start and end apart: 11 -> 8, of which waited for: 2 -> 2; matrix products, arithmetic and copies ran while one was open for 0% -> 3% of each run, Pallas kernels for 24% -> 17%
where the time goes in v4:
time: 44.4 us; the launch traced here: 44.1 us
  Pallas kernels  24.8 us (56%)
  starting transfers between devices  12.4 us (28%)
  local copies, waits for them, and re-layouts  3.91 us (9%)
  waiting for transfers between devices  1.6 us (4%)
  other arithmetic  0.76 us (2%)
  between operations  0.72 us (2%)
    pallas_call x10, Pallas kernels, call(): pl.pallas_call(kernel, out_shape=out_shape, in_specs=[pl.BlockSpec(memory...  24.8 us
    ppermute x8, starting transfers between devices, crossed(): lax.ppermute(block, axis, [(i, i ^ bits) for i in range(size) if i ^ bits...  12.4 us
    unnamed x10, local copies, waits for them, and re-layouts  3.91 us
    ppermute x8, waiting for transfers between devices, crossed(): lax.ppermute(block, axis, [(i, i ^ bits) for i in range(size) if i ^ bits...  1.6 us
  transfers between devices with their start and end apart: 8, of which 2 were waited for; matrix products, arithmetic and copies ran while one was open for 3% of the time, Pallas kernels for 17%

profile of v4, /device:TPU:0, one launch (start us, length us, event | category | flops | bytes accessed | tf_op | source)
XLA Modules:
  0.0 44.1 jit_solution(3477621998900305255)
XLA Ops:
  0.6 0.8 %pad_add_fusion.ints = s32[12,512]{1,0:T(8,128)S(1)} fusion(s32[4,8]{1,0:T(4,128)} %bitcast.3, s32[1,4]{1,0:T(1,128)} %param.9, s32[4,512]{1,0:T(4,128)} %bitcast.4), kind=kLoop, calls=%fused_computation | loop fusion | flops 12288 | bytes 32912 | tf_op jit(solution)/shard_map/concatenate | solution.py:569
  1.4 1.0 %copy-done = f32[7,16384]{1,0:T(8,128)S(1)} copy-done((f32[7,16384]{1,0:T(8,128)S(1)}, f32[7,16384]{1,0:T(8,128)}, u32[]{:S(2)}) %copy-start) | copy-done | bytes 458776
  2.4 0.6 %shard_map.95 = (f32[8,512]{1,0:T(8,128)S(1)}, f32[8,16384]{1,0:T(8,128)S(1)}) custom-call(f32[7,16384]{1,0:T(8,128)S(1)} %copy-done, s32[12,512]{1,0:T(8,128)S(1)} %pad_add_fusion.ints), custom_call_target="tpu_custom_call" | custom-call | tf_op jit(solution)/shard_map/pallas_call | solution.py:26
  3.1 3.0 %collective-permute-start = (f32[8,512]{1,0:T(8,128)S(1)}, f32[8,512]{1,0:T(8,128)S(1)}, u32[]{:S(2)}, u32[]{:S(2)}) collective-permute-start(f32[8,512]{1,0:T(8,128)S(1)} %get-tuple-element.31), channel_id=1, source_target_pairs={{0,8},{4,12},{8,0},{12,4},{16,24},{20,28},{24,16},{28,20},{1,9},{5... | collective-permute-start | bytes 49160 | tf_op jit(solution)/shard_map/ppermute | solution.py:547
  6.1 0.5 %shard_map.96.codes = s32[4,128,128]{2,1,0:T(8,128)S(1)} custom-call(s32[12,512]{1,0:T(8,128)S(1)} %pad_add_fusion.ints), custom_call_target="tpu_custom_call" | custom-call | tf_op jit(solution)/shard_map/pallas_call | solution.py:26
  6.6 0.7 %shard_map.97 = (f32[8,512]{1,0:T(8,128)S(1)}, s32[8,512]{1,0:T(8,128)S(1)}, s32[4,128,128]{2,1,0:T(8,128)S(1)}) custom-call(f32[8,16384]{1,0:T(8,128)S(1)} %get-tuple-element.30.state, s32[12,512]{1,0:T(8,128)S(1)} %pad_add_fusion.ints, s32[4,128,128]{2,1,0:T(8,128)S(1)} %shard_map.96.codes), custom_call_target="tpu_custom_call" | custom-call | tf_op jit(solution)/shard_map/pallas_call | solution.py:26
  7.3 0.5 %collective-permute-done.got0 = f32[8,512]{1,0:T(8,128)S(1)} collective-permute-done((f32[8,512]{1,0:T(8,128)S(1)}, f32[8,512]{1,0:T(8,128)S(1)}, u32[]{:S(2)}, u32[]{:S(2)}) %collective-permute-start) | collective-permute-done | bytes 16416 | tf_op jit(solution)/shard_map/ppermute | solution.py:547
  7.8 0.1 shard_map.98.after
  7.9 0.1 collective-permute-start.1
  8.0 1.5 %shard_map.100 = (f32[2,8,512]{2,1,0:T(8,128)S(1)}, s32[8,512]{1,0:T(8,128)S(1)}, f32[8,4096]{1,0:T(8,128)S(1)}, s32[4,8,128]{2,1,0:T(8,128)S(1)}) custom-call(f32[8,16384]{1,0:T(8,128)S(1)} %get-tuple-element.30.state, s32[12,512]{1,0:T(8,128)S(1)} %pad_add_fusion.ints, s32[4,128,128]{2,1,0:T(8,128)S(1)} %get-tuple-element.34.codes.tables, ...), custom_call_target="tpu_custom_call" | custom-call | tf_op jit(solution)/shard_map/pallas_call | solution.py:26
  9.5 0.0 collective-permute-done.1.got1
  9.5 0.5 %shard_map.101 = (f32[8,2048]{1,0:T(8,128)S(1)}, f32[8,2048]{1,0:T(8,128)S(1)}, f32[8,2048]{1,0:T(8,128)S(1)}, f32[8,2048]{1,0:T(8,128)S(1)}) custom-call(f32[2,8,512]{2,1,0:T(8,128)S(1)} %get-tuple-element.37.cols, s32[8,512]{1,0:T(8,128)S(1)} %get-tuple-element.38.marks, f32[8,512]{1,0:T(8,128)S(1)} %collective-permute-done.got0, ...), custom_call_target="tpu_custom_call" | custom-call | tf_op jit(solution)/shard_map/pallas_call | solution.py:26
  10.0 4.2 %collective-permute-start.2 = (f32[8,2048]{1,0:T(8,128)S(1)}, f32[8,2048]{1,0:T(8,128)S(1)}, u32[]{:S(2)}, u32[]{:S(2)}) collective-permute-start(f32[8,2048]{1,0:T(8,128)S(1)} %get-tuple-element.42), channel_id=1, source_target_pairs={{0,3},{1,2},{2,1},{3,0},{4,7},{5,6},{6,5},{7,4},{8,11},{9,10},{10,... | collective-permute-start | bytes 196616 | tf_op jit(solution)/shard_map/ppermute | solution.py:547
  14.2 0.0 collective-permute-start.3
  14.2 0.6 %collective-permute-start.4 = (f32[8,2048]{1,0:T(8,128)S(1)}, f32[8,2048]{1,0:T(8,128)S(1)}, u32[]{:S(2)}, u32[]{:S(2)}) collective-permute-start(f32[8,2048]{1,0:T(8,128)S(1)} %get-tuple-element.44), channel_id=1, source_target_pairs={{0,1},{1,0},{2,3},{3,2},{4,5},{5,4},{6,7},{7,6},{8,9},{9,8},{10,11... | collective-permute-start | bytes 196616 | tf_op jit(solution)/shard_map/ppermute | solution.py:547
  14.9 0.8 %copy.10.nbrs = s32[1,2,8,3]{3,2,1,0:T(8,128)S(1)} copy(s32[1,2,8,3]{2,1,3,0:T(2,128)} %param.13) | data formatting | bytes 384 | tf_op args[5]
  15.6 0.8 %copy.11.far = s32[1,2,8,4]{3,2,1,0:T(8,128)S(1)} copy(s32[1,2,8,4]{2,3,1,0:T(4,128)} %param.14) | data formatting | bytes 512 | tf_op args[6]
  16.4 0.7 %copy-done.2 = s32[1,2,8]{2,1,0:T(2,128)S(1)} copy-done((s32[1,2,8]{2,1,0:T(2,128)S(1)}, s32[1,2,8]{2,1,0:T(2,128)}, u32[]{:S(2)}) %copy-start.2) | copy-done | bytes 88
  17.1 0.7 %copy-done.3 = s32[1,2]{1,0:T(1,128)S(1)} copy-done((s32[1,2]{1,0:T(1,128)S(1)}, s32[1,2]{1,0:T(1,128)}, u32[]{:S(2)}) %copy-start.3) | copy-done | bytes 32
  17.7 1.5 %shard_map.99 = (f32[12,4,8,128]{3,2,1,0:T(8,128)S(1)}, f32[128,128]{1,0:T(8,128)S(1)}) custom-call(f32[8,16384]{1,0:T(8,128)S(1)} %get-tuple-element.30.state, f32[8,512]{1,0:T(8,128)S(1)} %collective-permute-done.got0, f32[8,512]{1,0:T(8,128)S(1)} %collective-permute-done.1.got1, s32[4,128,128]{2,1,0:T(8,128)S(1)} %get-tuple-element.34.codes.tables, ...), custom_call_target="tpu_custom_call" | custom-call | tf_op jit(solution)/shard_map/pallas_call | solution.py:26
  19.2 0.0 collective-permute-done.2.refs_1_
  19.3 1.1 %collective-permute-done.3.refs_2_ = f32[8,2048]{1,0:T(8,128)S(1)} collective-permute-done((f32[8,2048]{1,0:T(8,128)S(1)}, f32[8,2048]{1,0:T(8,128)S(1)}, u32[]{:S(2)}, u32[]{:S(2)}) %collective-permute-start.3) | collective-permute-done | bytes 65568 | tf_op jit(solution)/shard_map/ppermute | solution.py:547
  20.3 0.0 collective-permute-done.4.refs_3_
  20.3 12.5 %shard_map.102 = (f32[12,8,8,128]{3,2,1,0:T(8,128)S(1)}, f32[128,128]{1,0:T(8,128)S(1)}, f32[12,5,128,128]{3,2,1,0:T(8,128)S(1)}, f32[12,128,128]{2,1,0:T(8,128)...) custom-call(f32[12,4,8,128]{3,2,1,0:T(8,128)S(1)} %get-tuple-element, ...), custom_call_target="tpu_custom_call" | custom-call | tf_op jit(solution)/shard_map/pallas_call | solution.py:26
  32.9 2.8 %collective-permute-start.5 = (f32[8,1024]{1,0:T(8,128)S(1)}, f32[8,1024]{1,0:T(8,128)S(1)}, u32[]{:S(2)}, u32[]{:S(2)}) collective-permute-start(f32[8,1024]{1,0:T(8,128)S(1)} %get-tuple-element.55), channel_id=1, source_target_pairs={{0,3},{1,2},{2,1},{3,0},{4,7},{5,6},{6,5},{7,4},{8,11},{9,10},{10,... | collective-permute-start | bytes 98312 | tf_op jit(solution)/shard_map/ppermute | solution.py:547
  35.6 0.0 collective-permute-start.6
  35.6 1.7 %collective-permute-start.7 = (f32[8,1024]{1,0:T(8,128)S(1)}, f32[8,1024]{1,0:T(8,128)S(1)}, u32[]{:S(2)}, u32[]{:S(2)}) collective-permute-start(f32[8,1024]{1,0:T(8,128)S(1)} %get-tuple-element.57), channel_id=1, source_target_pairs={{0,1},{1,0},{2,3},{3,2},{4,5},{5,4},{6,7},{7,6},{8,9},{9,8},{10,11... | collective-permute-start | bytes 98312 | tf_op jit(solution)/shard_map/ppermute | solution.py:547
  37.3 3.1 %shard_map.103 = (f32[8,16384]{1,0:T(8,128)S(1)}, f32[12,3,128,128]{3,2,1,0:T(8,128)S(1)}, f32[128,128]{1,0:T(8,128)}) custom-call(f32[12,8,8,128]{3,2,1,0:T(8,128)S(1)} %get-tuple-element.45.near, f32[128,128]{1,0:T(8,128)S(1)} %get-tuple-element.46.density, f32[12,5,128,128]{3,2,1,0:T(8,128)S(1)} %get-tuple-element.47.centre, ...), custom_call_target="tpu_custom_call" | custom-call | tf_op jit(solution)/shard_map/pallas_call | solution.py:26
  40.4 0.0 collective-permute-done.5.refs_1_
  40.4 0.0 collective-permute-done.6.refs_2_
  40.4 0.0 collective-permute-done.7.refs_3_
  40.5 3.7 %shard_map.104 = f32[3,16384]{1,0:T(4,128)} custom-call(f32[12,8,8,128]{3,2,1,0:T(8,128)S(1)} %get-tuple-element.45.near, f32[128,128]{1,0:T(8,128)S(1)} %get-tuple-element.46.density, f32[12,5,128,128]{3,2,1,0:T(8,128)S(1)} %get-tuple-element.47.centre, f32[12,128,128]{2,1,0:T(8,128)S(1)} %get-tuple-element.48.press, ...), custom_call_target="tpu_custom_call" | custom-call | tf_op jit(solution)/shard_map/pallas_call | solution.py:26
  (5 shorter events, 0.0 us)
Async XLA Ops:
  0.6 19.7 %copy-start.1 = (s32[1,4,8]{2,1,0:T(4,128)S(1)}, s32[1,4,8]{2,1,0:T(4,128)}, u32[]{:S(2)}) copy-start(s32[1,4,8]{2,1,0:T(4,128)} %exports.3) | copy-start | bytes 388
  1.4 1.0 %copy-start = (f32[7,16384]{1,0:T(8,128)S(1)}, f32[7,16384]{1,0:T(8,128)}, u32[]{:S(2)}) copy-start(f32[7,16384]{1,0:T(8,128)} %particles.1) | copy-start | bytes 1376260
  3.1 4.7 %collective-permute-start = (f32[8,512]{1,0:T(8,128)S(1)}, f32[8,512]{1,0:T(8,128)S(1)}, u32[]{:S(2)}, u32[]{:S(2)}) collective-permute-start(f32[8,512]{1,0:T(8,128)S(1)} %get-tuple-element.31), channel_id=1, source_target_pairs={{0,8},{4,12},{8,0},{12,4},{16,24},{20,28},{24,16},{28,20},{1,9},{5... | collective-permute-start | bytes 49160 | tf_op jit(solution)/shard_map/ppermute | solution.py:547
  7.9 1.6 %collective-permute-start.1 = (f32[8,512]{1,0:T(8,128)S(1)}, f32[8,512]{1,0:T(8,128)S(1)}, u32[]{:S(2)}, u32[]{:S(2)}) collective-permute-start(f32[8,512]{1,0:T(8,128)S(1)} %shard_map.98.after), channel_id=1, source_target_pairs={{0,4},{4,0},{8,12},{12,8},{16,20},{20,16},{24,28},{28,24},{1,5},{5... | collective-permute-start | bytes 49160 | tf_op jit(solution)/shard_map/ppermute | solution.py:547
  10.0 9.2 %collective-permute-start.2 = (f32[8,2048]{1,0:T(8,128)S(1)}, f32[8,2048]{1,0:T(8,128)S(1)}, u32[]{:S(2)}, u32[]{:S(2)}) collective-permute-start(f32[8,2048]{1,0:T(8,128)S(1)} %get-tuple-element.42), channel_id=1, source_target_pairs={{0,3},{1,2},{2,1},{3,0},{4,7},{5,6},{6,5},{7,4},{8,11},{9,10},{10,... | collective-permute-start | bytes 196616 | tf_op jit(solution)/shard_map/ppermute | solution.py:547
  14.2 6.1 %collective-permute-start.3 = (f32[8,2048]{1,0:T(8,128)S(1)}, f32[8,2048]{1,0:T(8,128)S(1)}, u32[]{:S(2)}, u32[]{:S(2)}) collective-permute-start(f32[8,2048]{1,0:T(8,128)S(1)} %get-tuple-element.43), channel_id=1, source_target_pairs={{0,2},{1,3},{2,0},{3,1},{4,6},{5,7},{6,4},{7,5},{8,10},{9,11},{10,... | collective-permute-start | bytes 196616 | tf_op jit(solution)/shard_map/ppermute | solution.py:547
  14.2 6.1 %collective-permute-start.4 = (f32[8,2048]{1,0:T(8,128)S(1)}, f32[8,2048]{1,0:T(8,128)S(1)}, u32[]{:S(2)}, u32[]{:S(2)}) collective-permute-start(f32[8,2048]{1,0:T(8,128)S(1)} %get-tuple-element.44), channel_id=1, source_target_pairs={{0,1},{1,0},{2,3},{3,2},{4,5},{5,4},{6,7},{7,6},{8,9},{9,8},{10,11... | collective-permute-start | bytes 196616 | tf_op jit(solution)/shard_map/ppermute | solution.py:547
  16.4 0.7 %copy-start.2 = (s32[1,2,8]{2,1,0:T(2,128)S(1)}, s32[1,2,8]{2,1,0:T(2,128)}, u32[]{:S(2)}) copy-start(s32[1,2,8]{2,1,0:T(2,128)} %ids.7) | copy-start | bytes 196
  17.1 0.7 %copy-start.3 = (s32[1,2]{1,0:T(1,128)S(1)}, s32[1,2]{1,0:T(1,128)}, u32[]{:S(2)}) copy-start(s32[1,2]{1,0:T(1,128)} %counts.7) | copy-start | bytes 28
  32.9 7.6 %collective-permute-start.5 = (f32[8,1024]{1,0:T(8,128)S(1)}, f32[8,1024]{1,0:T(8,128)S(1)}, u32[]{:S(2)}, u32[]{:S(2)}) collective-permute-start(f32[8,1024]{1,0:T(8,128)S(1)} %get-tuple-element.55), channel_id=1, source_target_pairs={{0,3},{1,2},{2,1},{3,0},{4,7},{5,6},{6,5},{7,4},{8,11},{9,10},{10,... | collective-permute-start | bytes 98312 | tf_op jit(solution)/shard_map/ppermute | solution.py:547
  35.6 4.8 %collective-permute-start.6 = (f32[8,1024]{1,0:T(8,128)S(1)}, f32[8,1024]{1,0:T(8,128)S(1)}, u32[]{:S(2)}, u32[]{:S(2)}) collective-permute-start(f32[8,1024]{1,0:T(8,128)S(1)} %get-tuple-element.56), channel_id=1, source_target_pairs={{0,2},{1,3},{2,0},{3,1},{4,6},{5,7},{6,4},{7,5},{8,10},{9,11},{10,... | collective-permute-start | bytes 98312 | tf_op jit(solution)/shard_map/ppermute | solution.py:547
  35.6 4.8 %collective-permute-start.7 = (f32[8,1024]{1,0:T(8,128)S(1)}, f32[8,1024]{1,0:T(8,128)S(1)}, u32[]{:S(2)}, u32[]{:S(2)}) collective-permute-start(f32[8,1024]{1,0:T(8,128)S(1)} %get-tuple-element.57), channel_id=1, source_target_pairs={{0,1},{1,0},{2,3},{3,2},{4,5},{5,4},{6,7},{7,6},{8,9},{9,8},{10,11... | collective-permute-start | bytes 98312 | tf_op jit(solution)/shard_map/ppermute | solution.py:547

commit v5 on v4

--- a/solution.py
+++ b/solution.py
@@ -12,6 +12,8 @@
 KERNEL_NORM = 21.0 / (16.0 * math.pi)
 FORCE_NORM = 5.0 * KERNEL_NORM * 32.0 * (2.0 / 3.0)
 TINY = 1e-30
+BLOCK_ORDER = (3, 1, 2)
+RETURN_ORDER = (2, 3, 1)
 F32 = jnp.float32
 I32 = jnp.int32
 VMEM = pltpu.VMEM
@@ -210,7 +212,32 @@
     return jnp.where(second, 1, 0), jnp.where(second, jnp.minimum(n - counts[0, 0], nact - 1), n)
 
 
-def own_kernel(state, got0, got1, codes, ids, counts, nbrs, own, density):
+def picked_rows(chosen, table):
+    high = table.astype(jnp.bfloat16)
+    rest = table - high.astype(F32)
+    middle = rest.astype(jnp.bfloat16)
+    low = (rest - middle.astype(F32)).astype(jnp.bfloat16)
+    chosen = chosen.astype(jnp.bfloat16)
+    return jnp.dot(
+        jnp.concatenate([chosen] * 3, axis=1),
+        jnp.concatenate([high, middle, low], axis=0),
+        preferred_element_type=F32,
+    )
+
+
+def own_kernel(state, got0, got1, codes, ids, counts, nbrs, far, exports, *refs):
+    own, density, near_pick, far_pick = refs[:4]
+    copied, small = refs[4:9], refs[9:]
+    for source, target in zip((ids, counts, nbrs, far, exports), copied):
+        target[...] = source[...]
+    copies = fetch([ids, counts, nbrs, far], small[:4], small[4])
+    ids, counts, nbrs, far = small[:4]
+    me = lax.axis_index("gy")
+    slots = 8
+    near_pick[...] = jnp.zeros_like(near_pick)
+    far_pick[...] = jnp.zeros_like(far_pick)
+    near_lane = lax.broadcasted_iota(I32, (1, near_pick.shape[1]), 1)
+    far_lane = lax.broadcasted_iota(I32, (1, far_pick.shape[1]), 1)
     count = got0.shape[1] // BLK
     blocks = density.shape[0]
     tables = tables_of(got0, count) + tables_of(got1, count)
@@ -222,79 +249,104 @@
         density[part, :] = patch(density[part, :], codes[0, part, :], last)
     nact = ids.shape[2]
 
+    for copy in copies:
+        copy.wait()
     for n in range(TOTACT):
         which, i = live_slot(counts, n, nact)
         wanted = [ids[0, which, i]] + [nbrs[0, which, i, t] for t in range(nbrs.shape[3])]
         for t, block in enumerate(wanted):
             own[n, t] = early_block(state, codes, tables, block)
-
-
-def spread(rows, *outs):
+            near_pick[8 * n + t : 8 * n + t + 1, :] = jnp.where(near_lane == block, 1.0, 0.0)
+        for t in range(far.shape[3]):
+            g = far[0, which, i, t] ^ (me * slots)
+            at = 8 * n + len(wanted) + t
+            far_pick[at : at + 1, :] = jnp.where(far_lane == g, 1.0, 0.0)
+
+
+def spread(rows, out, kept):
     columns_of = jnp.transpose(jnp.concatenate((rows + rows)[:8], axis=0))
     for k in range(len(rows)):
         values = jnp.broadcast_to(columns_of[:, k : k + 1], (BLK, BLK))
-        for out in outs:
-            out[k] = values
-
-
-def pair_sums(near, n, centre, sums, inside, outside):
+        out[k] = values
+        if k < 5:
+            kept[k] = values
+
+
+def added(old, value):
+    return value if old is None else old + value
+
+
+def pair_weight(distance, h1, h2, m1, m2):
+    inverse = 1.0 / (h1 + h2)
+    inv2 = inverse * inverse
+    slope = jnp.maximum(inverse - distance * inv2, 0.0)
+    return slope * slope * slope * inv2 * (m1 * m2)
+
+
+def pair_sums(near, n, centre, inside, outside, press, fresh, others):
     local = inside.shape[1] // BLK
+    far = 8 - local
+    row = lax.broadcasted_iota(I32, (8, BLK), 0)
+    lane = lax.broadcasted_iota(I32, (8, BLK), 1)
+    plain = [[None] * 3 for _ in range(far)]
+    pressed = [[None] * 3 for _ in range(far)]
+    own = None
+    waiting = None
+
+    def settle_pushes(pushes, pressure):
+        for t in range(far):
+            for k in range(3):
+                pressed[t][k] = added(pressed[t][k], pushes[t][k] * pressure)
+
     for g in range(BLK // 8):
         part = slice(8 * g, 8 * g + 8)
-        cx, cy, cz, cm, ch = (centre[k, part, :] for k in range(5))
+        cx, cy, cz, cm, ch, cu = (centre[k, part, :] for k in range(6))
         half = 0.5 / ch
         total = None
+        pushes = []
         for t in range(8):
             x, y, z, m, h = (wide(near[n, k, t : t + 1, :]) for k in range(5))
-            dx, dy, dz = cx - x, cy - y, cz - z
-            square = dx * dx + dy * dy + dz * dz
+            apart = (cx - x, cy - y, cz - z)
+            square = apart[0] * apart[0] + apart[1] * apart[1] + apart[2] * apart[2]
             distance = square * lax.rsqrt(jnp.maximum(square, TINY))
             fall = jnp.maximum(1.0 - distance * half, 0.0)
             fall2 = fall * fall
-            term = fall2 * fall2 * (1.25 - fall) * m
-            total = term if total is None else total + term
-            inverse = 1.0 / (ch + h)
-            inv2 = inverse * inverse
-            slope = jnp.maximum(inverse - distance * inv2, 0.0)
-            weight = slope * slope * slope * inv2 * (cm * m)
+            total = added(total, fall2 * fall2 * (1.25 - fall) * m)
             if t < local:
-                row = 8 * (g * local + t)
-                inside[n, row : row + 8, :] = weight
+                at = 8 * (g * local + t)
+                inside[n, at : at + 8, :] = distance
             else:
-                row = 8 * (g * (8 - local) + t - local)
-                outside[n, row : row + 8, :] = weight
-        sums[n, part, :] = total
-
-
-def back_sums(near, n, centre, press, outside, others):
-    far = outside.shape[1] // BLK
-    first = 8 - far
-    ghost = [[wide(near[n, k, t : t + 1, :]) for k in range(3)] for t in range(first, 8)]
-    sums = [[None] * 6 for _ in range(far)]
-    for g in range(BLK // 8):
-        part = slice(8 * g, 8 * g + 8)
-        here = [centre[n, k, part, :] for k in range(3)]
-        cp = press[n, part, :]
-        for t in range(far):
-            row = 8 * (g * far + t)
-            weight = outside[n, row : row + 8, :]
-            for k in range(3):
-                push = weight * (here[k] - ghost[t][k])
-                for place, value in ((k, push * cp), (3 + k, push)):
-                    old = sums[t][place]
-                    sums[t][place] = value if old is None else old + value
+                weight = pair_weight(distance, ch, h, cm, m)
+                at = 8 * (g * far + t - local)
+                push = [weight * apart[k] for k in range(3)]
+                for k in range(3):
+                    outside[n, k, at : at + 8, :] = push[k]
+                    plain[t - local][k] = added(plain[t - local][k], push[k])
+                pushes.append(push)
+        total = jnp.broadcast_to(jnp.sum(total, axis=1, keepdims=True), (8, BLK))
+        rho = total * (4.0 * KERNEL_NORM / (ch * ch * ch))
+        pressure = cu / rho
+        press[n, part, :] = pressure
+        own = added(own, jnp.where(row + 8 * g == lane, rho, 0.0))
+        if waiting is not None:
+            settle_pushes(*waiting)
+        waiting = (pushes, pressure)
+    settle_pushes(*waiting)
+    fresh[pl.ds(n, 1), :] = jnp.sum(own, axis=0, keepdims=True)
     for t in range(far):
-        for k in range(6):
-            row = 8 * (k * far + t)
-            others[n, row : row + 8, :] = sums[t][k]
+        for k in range(3):
+            at = 8 * (k * far + t)
+            others[n, at : at + 8, :] = pressed[t][k]
+            at = 8 * ((3 + k) * far + t)
+            others[n, at : at + 8, :] = plain[t][k]
 
 
 def make_density_kernel(peers, slots):
     def density_kernel(own, before, codes, ids, counts, far, exports, *refs):
-        sent = by_partner(refs[:peers])
+        sent = by_partner(refs[:peers], BLOCK_ORDER)
         near, density, centre, press, inside, outside = refs[peers : peers + 6]
         outs = refs[peers + 6 : 2 * peers + 6]
-        (late_three, ghosts, first, second, sums, fresh, others, rows, back, *small) = refs[
+        (late_three, ghosts, first, second, fresh, others, rows, back, *small) = refs[
             2 * peers + 6 :
         ]
         copies = fetch([ids, counts, far, exports], small[:4], small[4])
@@ -345,36 +397,22 @@
                 near[n, :, inner + t, :] = ghosts[:, lanes(g)]
 
         def prepare(n, buffer):
-            spread([near[n, k, 0:1, :] for k in range(5)], buffer, centre.at[n])
+            spread([near[n, k, 0:1, :] for k in range(6)], buffer, centre.at[n])
+
+        def work(n, buffer):
+            pair_sums(near, n, buffer, inside, outside, press, fresh, others)
 
         prepare(0, first)
 
         def step(p, _):
             n = 2 * p
             prepare(n + 1, second)
-            pair_sums(near, n, first, sums, inside, outside)
+            work(n, first)
             prepare(jnp.minimum(n + 2, TOTACT - 1), first)
-            pair_sums(near, n + 1, second, sums, inside, outside)
+            work(n + 1, second)
             return 0
 
         lax.fori_loop(0, (live + 1) // 2, step, 0)
-        for n in range(TOTACT):
-            h = near[n, 4, 0:1, :]
-            total = jnp.sum(jnp.transpose(sums[n]), axis=0, keepdims=True)
-            fresh[n : n + 1, :] = total * (4.0 * KERNEL_NORM / (h * h * h))
-        pressures = [near[n, 5, 0:1, :] / fresh[n : n + 1, :] for n in range(TOTACT)]
-        pressures = jnp.concatenate(pressures + pressures[: 16 - TOTACT], axis=0)
-        pressures = jnp.transpose(pressures)
-        for n in range(TOTACT):
-            press[n] = jnp.broadcast_to(pressures[:, n : n + 1], (BLK, BLK))
-
-        def back_step(n, _):
-            back_sums(near, n, centre, press, outside, others)
-            which, i = live_slot(counts, n, nact)
-            density[pl.ds(ids[0, which, i], 1), :] = fresh[pl.ds(n, 1), :]
-            return 0
-
-        lax.fori_loop(0, live, back_step, 0)
         for n in range(TOTACT):
             for t in range(ngh):
                 m = near[n, 3, inner + t : inner + t + 1, :]
@@ -385,9 +423,13 @@
                     total = jnp.sum(others[n, row : row + 8, :], axis=0, keepdims=True)
                     rows[n, k, t : t + 1, :] = total * (scale if k < 3 else scale * u)
 
+        for n in range(TOTACT):
+            for t, g in enumerate(far_of(n)):
+                back[0:6, lanes(g)] += jnp.where(n < live, rows[n, 0:6, t, :], 0.0)
+
         def place(n, _):
-            for t, g in enumerate(far_of(n)):
-                back[0:6, lanes(g)] += rows[n, 0:6, t, :]
+            which, i = live_slot(counts, n, nact)
+            density[pl.ds(ids[0, which, i], 1), :] = fresh[pl.ds(n, 1), :]
             return 0
 
         lax.fori_loop(0, live, place, 0)
@@ -402,19 +444,19 @@
 
 def inner_sums(near, n, centre, press, others_press, inside, sums, others):
     local = inside.shape[1] // BLK
-    tile = [[wide(near[n, k, t : t + 1, :]) for k in range(3)] for t in range(local)]
-    theirs = [wide(others_press[n, t : t + 1, :]) for t in range(local)]
     pushed = [[None] * 3 for _ in range(local)]
     for g in range(BLK // 8):
         part = slice(8 * g, 8 * g + 8)
-        here = [centre[n, k, part, :] for k in range(3)]
+        *here, cm, ch = (centre[n, k, part, :] for k in range(5))
         cp = press[n, part, :]
         total = [None] * 3
         for t in range(local):
+            *tile, m, h = (wide(near[n, k, t : t + 1, :]) for k in range(5))
             row = 8 * (g * local + t)
-            weight = inside[n, row : row + 8, :] * (cp + theirs[t])
+            weight = pair_weight(inside[n, row : row + 8, :], ch, h, cm, m)
+            weight = weight * (cp + wide(others_press[n, t : t + 1, :]))
             for k in range(3):
-                push = weight * (here[k] - tile[t][k])
+                push = weight * (here[k] - tile[k])
                 total[k] = push if total[k] is None else total[k] + push
                 if t > 0:
                     old = pushed[t][k]
@@ -428,116 +470,97 @@
 
 
 def inner_kernel(
-    near, density, centre, press, inside, ids, counts, nbrs, totals, sums, density_out, *refs
+    near, density, centre, press, inside, near_pick, ids, counts, nbrs, totals, sums, *refs
 ):
-    rho, others_press, others, rows = refs
-    density_out[...] = density[...]
+    others_press, others, rows, *small = refs
+    copies = fetch([ids, counts, nbrs], small[:3], small[3])
+    ids, counts, nbrs = small[:3]
     totals[...] = jnp.zeros_like(totals)
-    live = counts[0, 0] + counts[0, 1]
-    nact = ids.shape[2]
-    inner = 1 + nbrs.shape[3]
-
-    def blocks_of(n):
-        which, i = live_slot(counts, n, nact)
-        return [ids[0, which, i]] + [nbrs[0, which, i, t] for t in range(nbrs.shape[3])]
-
+    rho = picked_rows(near_pick[...], density[...])
     for n in range(TOTACT):
-        for t, block in enumerate(blocks_of(n)):
-            rho[n, t : t + 1, :] = density[pl.ds(block, 1), :]
-    for n in range(TOTACT):
-        others_press[n] = near[n, 5] / rho[n]
+        others_press[n] = near[n, 5] / rho[8 * n : 8 * n + 8]
 
     def step(n, _):
         inner_sums(near, n, centre, press, others_press, inside, sums, others)
         return 0
 
-    lax.fori_loop(0, live, step, 0)
+    lax.fori_loop(0, TOTACT, step, 0)
+    for copy in copies:
+        copy.wait()
+    live = counts[0, 0] + counts[0, 1]
+    inner = 1 + nbrs.shape[3]
     for n in range(TOTACT):
+        which, i = live_slot(counts, n, ids.shape[2])
         for t in range(1, inner):
             scale = -FORCE_NORM / near[n, 3, t : t + 1, :]
             for k in range(3):
                 row = 8 * (k * inner + t)
                 total = jnp.sum(others[n, row : row + 8, :], axis=0, keepdims=True)
                 rows[n, k, t : t + 1, :] = total * scale
-
-    def place(n, _):
-        for t, block in enumerate(blocks_of(n)):
-            if t > 0:
-                totals[0:3, lanes(block)] += rows[n, 0:3, t, :]
-        return 0
-
-    lax.fori_loop(0, live, place, 0)
-
-
-def outer_sums(near, n, centre, press, others_press, outside, before, sums):
-    far = outside.shape[1] // BLK
-    first = 8 - far
-    tile = [[wide(near[n, k, t : t + 1, :]) for k in range(3)] for t in range(first, 8)]
-    theirs = [wide(others_press[n, t : t + 1, :]) for t in range(first, 8)]
+            block = nbrs[0, which, i, t - 1]
+            totals[0:3, lanes(block)] += jnp.where(n < live, rows[n, 0:3, t, :], 0.0)
+
+
+def outer_sums(near, n, press, others_press, outside, before, rows):
+    far = outside.shape[2] // BLK
+    theirs = [wide(others_press[n, t : t + 1, :]) for t in range(8 - far, 8)]
+    row = lax.broadcasted_iota(I32, (8, BLK), 0)
+    lane = lax.broadcasted_iota(I32, (8, BLK), 1)
+    own = [None] * 3
     for g in range(BLK // 8):
         part = slice(8 * g, 8 * g + 8)
-        here = [centre[n, k, part, :] for k in range(3)]
         cp = press[n, part, :]
         total = [before[n, k, part, :] for k in range(3)]
         for t in range(far):
-            row = 8 * (g * far + t)
-            weight = outside[n, row : row + 8, :] * (cp + theirs[t])
+            at = 8 * (g * far + t)
+            both = cp + theirs[t]
             for k in range(3):
-                total[k] = total[k] + weight * (here[k] - tile[t][k])
+                total[k] = total[k] + both * outside[n, k, at : at + 8, :]
         for k in range(3):
-            sums[n, k, part, :] = total[k]
+            value = jnp.broadcast_to(jnp.sum(total[k], axis=1, keepdims=True), (8, BLK))
+            own[k] = added(own[k], jnp.where(row + 8 * g == lane, value, 0.0))
+    scale = FORCE_NORM / near[n, 3, 0:1, :]
+    for k in range(3):
+        rows[n, k : k + 1, :] = jnp.sum(own[k], axis=0, keepdims=True) * scale
 
 
 def make_outer_kernel(peers, slots):
     def outer_kernel(
-        near, density, centre, press, outside, totals, before, ids, counts, far, exports, *refs
+        near, density, press, outside, totals, before, far_pick, ids, counts, exports, *refs
     ):
-        got = by_partner(refs[:peers])
-        out, far_rho, rho, others_press, sums, rows, *small = refs[peers:]
-        copies = fetch([ids, counts, far, exports], small[:4], small[4])
-        ids, counts, far, exports = small[:4]
+        sent = refs[:peers]
+        got = by_partner(refs[peers : 2 * peers], RETURN_ORDER)
+        out, density_out, far_rho, others_press, rows, *small = refs[2 * peers :]
+        copies = fetch([ids, counts, exports], small[:3], small[3])
+        ids, counts, exports = small[:3]
+        density_out[...] = density[...]
+        far_rho[...] = jnp.zeros_like(far_rho)
         for q in range(peers):
             for t in range(slots):
                 g = q * slots + t
                 far_rho[g : g + 1, :] = got[q][6:7, chunk(t)]
         out[...] = totals[0:3, :]
-        me = lax.axis_index("gy")
-        nact = ids.shape[2]
-        ngh = far.shape[3]
+        rho = picked_rows(far_pick[...], far_rho[...])
+        for n in range(TOTACT):
+            others_press[n] = near[n, 5] / rho[8 * n : 8 * n + 8]
+
+        def step(n, _):
+            outer_sums(near, n, press, others_press, outside, before, rows)
+            return 0
+
+        lax.fori_loop(0, TOTACT, step, 0)
         for copy in copies:
             copy.wait()
+        me = lax.axis_index("gy")
         live = counts[0, 0] + counts[0, 1]
-        for n in range(TOTACT):
-            which, i = live_slot(counts, n, nact)
-            for t in range(ngh):
-                g = far[0, which, i, t] ^ (me * slots)
-                rho[n, 8 - ngh + t : 9 - ngh + t, :] = far_rho[pl.ds(g, 1), :]
-        for n in range(TOTACT):
-            others_press[n] = near[n, 5] / rho[n]
-
-        def step(n, _):
-            outer_sums(near, n, centre, press, others_press, outside, before, sums)
-            return 0
-
-        lax.fori_loop(0, live, step, 0)
-        for n in range(TOTACT):
-            scale = FORCE_NORM / near[n, 3, 0:1, :]
-            for k in range(3):
-                total = jnp.sum(jnp.transpose(sums[n, k]), axis=0, keepdims=True)
-                rows[n, k : k + 1, :] = total * scale
         for q in range(peers):
             for t in range(slots):
-                b = exports[0, me ^ q, t]
-                own_rho = density[pl.ds(b, 1), :]
+                own_rho = sent[q][6:7, chunk(t)]
                 value = got[q][0:3, chunk(t)] + got[q][3:6, chunk(t)] / own_rho
-                out[0:3, lanes(b)] += value
-
-        def place(n, _):
-            which, i = live_slot(counts, n, nact)
-            out[0:3, lanes(ids[0, which, i])] += rows[n, 0:3, :]
-            return 0
-
-        lax.fori_loop(0, live, place, 0)
+                out[0:3, lanes(exports[0, me ^ q, t])] += value
+        for n in range(TOTACT):
+            which, i = live_slot(counts, n, ids.shape[2])
+            out[0:3, lanes(ids[0, which, i])] += jnp.where(n < live, rows[n, 0:3, :], 0.0)
 
     return outer_kernel
 
@@ -547,12 +570,17 @@
     return lax.ppermute(block, axis, [(i, i ^ bits) for i in range(size) if i ^ bits < size])
 
 
-def exchanged(parts):
-    return [parts[0]] + [crossed(parts[q], "gy", q) for q in range(len(parts) - 1, 0, -1)]
-
-
-def by_partner(refs):
-    return [refs[0]] + list(refs[:0:-1])
+def first_steps(peers, first):
+    return list(first) + [q for q in range(peers - 1, 0, -1) if q not in first]
+
+
+def exchanged(parts, first):
+    return [parts[0]] + [crossed(parts[q], "gy", q) for q in first_steps(len(parts), first)]
+
+
+def by_partner(refs, first):
+    steps = [0] + first_steps(len(refs), first)
+    return [refs[steps.index(q)] for q in range(len(refs))]
 
 
 def shards(
@@ -610,22 +638,28 @@
         raw,
         code_rows,
     )
-    sent = exchanged(packs)
-    own, before = call(
+    sent = exchanged(packs, BLOCK_ORDER)
+    small = [active_ids, active_count, local_nbrs, ghost_slots]
+    own, before, near_pick, far_pick, ids, counts, nbrs, far, export_ids = call(
         own_kernel,
-        [shape(TOTACT, inner, 8, BLK), shape(blocks, BLK)],
+        [
+            shape(TOTACT, inner, 8, BLK),
+            shape(blocks, BLK),
+            shape(TOTACT * 8, blocks),
+            shape(TOTACT * 8, max(BLK, peers * slots)),
+        ]
+        + [shape(*a.shape, dtype=I32) for a in small + [export_blocks]],
         state,
         got0,
         got1,
         tables,
-        active_ids,
-        active_count,
-        local_nbrs,
-        smem=(4, 5, 6),
-    )
-    indices = [active_ids, active_count, ghost_slots, export_blocks]
+        *small,
+        export_blocks,
+        scratch=fetch_scratch(small),
+    )
+    indices = [ids, counts, far, export_ids]
     local = shape(TOTACT, inner * BLK, BLK)
-    remote = shape(TOTACT, (8 - inner) * BLK, BLK)
+    remote = shape(TOTACT, 3, (8 - inner) * BLK, BLK)
     near, density, centre, press, inside, outside, *returns = call(
         make_density_kernel(peers, slots),
         [
@@ -645,9 +679,8 @@
         scratch=[
             VMEM((peers, 8, mig), F32),
             VMEM((8, wide_total), F32),
-            VMEM((5, BLK, BLK), F32),
-            VMEM((5, BLK, BLK), F32),
-            VMEM((TOTACT, BLK, BLK), F32),
+            VMEM((6, BLK, BLK), F32),
+            VMEM((6, BLK, BLK), F32),
             VMEM((TOTACT, BLK), F32),
             VMEM((TOTACT, 6 * (8 - inner) * 8, BLK), F32),
             VMEM((TOTACT, 8, 8, BLK), F32),
@@ -655,46 +688,45 @@
         ]
         + fetch_scratch(indices),
     )
-    got = exchanged(returns)
-    totals, sums, density_out = call(
+    got = exchanged(returns, RETURN_ORDER)
+    small = [ids, counts, nbrs]
+    totals, sums = call(
         inner_kernel,
-        [shape(8, per_dev), shape(TOTACT, 3, BLK, BLK), shape(blocks, BLK)],
+        [shape(8, per_dev), shape(TOTACT, 3, BLK, BLK)],
         near,
         density,
         centre,
         press,
         inside,
-        active_ids,
-        active_count,
-        local_nbrs,
-        smem=(5, 6, 7),
+        near_pick,
+        *small,
         scratch=[
-            VMEM((TOTACT, 8, BLK), F32),
             VMEM((TOTACT, 8, BLK), F32),
             VMEM((TOTACT, 3 * inner * 8, BLK), F32),
             VMEM((TOTACT, 8, 8, BLK), F32),
-        ],
-    )
-    accel = call(
+        ]
+        + fetch_scratch(small),
+    )
+    small = [ids, counts, export_ids]
+    accel, density_out = call(
         make_outer_kernel(peers, slots),
-        shape(3, per_dev),
+        [shape(3, per_dev), shape(blocks, BLK)],
         near,
         density,
-        centre,
         press,
         outside,
         totals,
         sums,
-        *indices,
+        far_pick,
+        *small,
+        *returns,
         *got,
         scratch=[
-            VMEM((peers * slots, BLK), F32),
+            VMEM((max(BLK, peers * slots), BLK), F32),
             VMEM((TOTACT, 8, BLK), F32),
             VMEM((TOTACT, 8, BLK), F32),
-            VMEM((TOTACT, 3, BLK, BLK), F32),
-            VMEM((TOTACT, 8, BLK), F32),
         ]
-        + fetch_scratch(indices),
+        + fetch_scratch(small),
     )
     return density_out.reshape(-1), accel
 

time: 44.4 us -> 41.4 us (0.932)
  Pallas kernels: 24.8 us -> 21.9 us
  starting transfers between devices: 12.4 us -> 11.7 us
  local copies, waits for them, and re-layouts: 3.91 us -> 4.58 us
    pallas_call x10, Pallas kernels: 24.8 us -> 21.9 us  [call(): pl.pallas_call(kernel, out_shape=out_shape, in_specs=[pl.BlockSpec(memory...]
    unnamed x10, local copies, waits for them, and re-layouts: 3.91 us -> 4.58 us
    ppermute x8, starting transfers between devices: 12.4 us -> 11.7 us  [crossed(): lax.ppermute(block, axis, [(i, i ^ bits) for i in range(size) if i ^ bits...]
  transfers between devices with their start and end apart: 8 -> 8, of which waited for: 2 -> 2; matrix products, arithmetic and copies ran while one was open for 3% -> 4% of each run, Pallas kernels for 17% -> 18%
where the time goes in v5:
time: 41.4 us; the launch traced here: 41.1 us
  Pallas kernels  21.9 us (53%)
  starting transfers between devices  11.7 us (28%)
  local copies, waits for them, and re-layouts  4.58 us (11%)
  waiting for transfers between devices  1.37 us (3%)
  between operations  0.76 us (2%)
  other arithmetic  0.74 us (2%)
    pallas_call x10, Pallas kernels, call(): pl.pallas_call(kernel, out_shape=out_shape, in_specs=[pl.BlockSpec(memory...  21.9 us
    ppermute x8, starting transfers between devices, crossed(): lax.ppermute(block, axis, [(i, i ^ bits) for i in range(size) if i ^ bits...  11.7 us
    unnamed x10, local copies, waits for them, and re-layouts  4.58 us
    ppermute x8, waiting for transfers between devices, crossed(): lax.ppermute(block, axis, [(i, i ^ bits) for i in range(size) if i ^ bits...  1.37 us
  transfers between devices with their start and end apart: 8, of which 2 were waited for; matrix products, arithmetic and copies ran while one was open for 4% of the time, Pallas kernels for 18%

profile of v5, /device:TPU:0, one launch (start us, length us, event | category | flops | bytes accessed | tf_op | source)
XLA Modules:
  0.0 41.1 jit_solution(16575572528082858178)
XLA Ops:
  0.6 0.7 %pad_add_fusion.ints = s32[12,512]{1,0:T(8,128)S(1)} fusion(s32[4,8]{1,0:T(4,128)} %bitcast.3, s32[1,4]{1,0:T(1,128)} %param.9, s32[4,512]{1,0:T(4,128)} %bitcast.4), kind=kLoop, calls=%fused_computation | loop fusion | flops 12288 | bytes 32912 | tf_op jit(solution)/shard_map/concatenate | solution.py:597
  1.4 1.0 %copy-done = f32[7,16384]{1,0:T(8,128)S(1)} copy-done((f32[7,16384]{1,0:T(8,128)S(1)}, f32[7,16384]{1,0:T(8,128)}, u32[]{:S(2)}) %copy-start) | copy-done | bytes 458776
  2.4 0.6 %shard_map.95 = (f32[8,512]{1,0:T(8,128)S(1)}, f32[8,16384]{1,0:T(8,128)S(1)}) custom-call(f32[7,16384]{1,0:T(8,128)S(1)} %copy-done, s32[12,512]{1,0:T(8,128)S(1)} %pad_add_fusion.ints), custom_call_target="tpu_custom_call" | custom-call | tf_op jit(solution)/shard_map/pallas_call | solution.py:28
  3.0 3.0 %collective-permute-start = (f32[8,512]{1,0:T(8,128)S(1)}, f32[8,512]{1,0:T(8,128)S(1)}, u32[]{:S(2)}, u32[]{:S(2)}) collective-permute-start(f32[8,512]{1,0:T(8,128)S(1)} %get-tuple-element.39), channel_id=1, source_target_pairs={{0,8},{4,12},{8,0},{12,4},{16,24},{20,28},{24,16},{28,20},{1,9},{5... | collective-permute-start | bytes 49160 | tf_op jit(solution)/shard_map/ppermute | solution.py:570
  6.1 0.5 %shard_map.96.codes = s32[4,128,128]{2,1,0:T(8,128)S(1)} custom-call(s32[12,512]{1,0:T(8,128)S(1)} %pad_add_fusion.ints), custom_call_target="tpu_custom_call" | custom-call | tf_op jit(solution)/shard_map/pallas_call | solution.py:28
  6.6 0.7 %shard_map.97 = (f32[8,512]{1,0:T(8,128)S(1)}, s32[8,512]{1,0:T(8,128)S(1)}, s32[4,128,128]{2,1,0:T(8,128)S(1)}) custom-call(f32[8,16384]{1,0:T(8,128)S(1)} %get-tuple-element.38.state, s32[12,512]{1,0:T(8,128)S(1)} %pad_add_fusion.ints, s32[4,128,128]{2,1,0:T(8,128)S(1)} %shard_map.96.codes), custom_call_target="tpu_custom_call" | custom-call | tf_op jit(solution)/shard_map/pallas_call | solution.py:28
  7.3 0.5 %collective-permute-done.got0 = f32[8,512]{1,0:T(8,128)S(1)} collective-permute-done((f32[8,512]{1,0:T(8,128)S(1)}, f32[8,512]{1,0:T(8,128)S(1)}, u32[]{:S(2)}, u32[]{:S(2)}) %collective-permute-start) | collective-permute-done | bytes 16416 | tf_op jit(solution)/shard_map/ppermute | solution.py:570
  7.8 0.1 shard_map.98.after
  7.9 0.1 collective-permute-start.1
  8.0 1.5 %shard_map.100 = (f32[2,8,512]{2,1,0:T(8,128)S(1)}, s32[8,512]{1,0:T(8,128)S(1)}, f32[8,4096]{1,0:T(8,128)S(1)}, s32[4,8,128]{2,1,0:T(8,128)S(1)}) custom-call(f32[8,16384]{1,0:T(8,128)S(1)} %get-tuple-element.38.state, s32[12,512]{1,0:T(8,128)S(1)} %pad_add_fusion.ints, s32[4,128,128]{2,1,0:T(8,128)S(1)} %get-tuple-element.42.codes.tables, ...), custom_call_target="tpu_custom_call" | custom-call | tf_op jit(solution)/shard_map/pallas_call | solution.py:28
  9.5 0.0 collective-permute-done.1.got1
  9.5 0.5 %shard_map.101 = (f32[8,2048]{1,0:T(8,128)S(1)}, f32[8,2048]{1,0:T(8,128)S(1)}, f32[8,2048]{1,0:T(8,128)S(1)}, f32[8,2048]{1,0:T(8,128)S(1)}) custom-call(f32[2,8,512]{2,1,0:T(8,128)S(1)} %get-tuple-element.49.cols, s32[8,512]{1,0:T(8,128)S(1)} %get-tuple-element.50.marks, f32[8,512]{1,0:T(8,128)S(1)} %collective-permute-done.got0, ...), custom_call_target="tpu_custom_call" | custom-call | tf_op jit(solution)/shard_map/pallas_call | solution.py:28
  10.0 4.2 %collective-permute-start.2 = (f32[8,2048]{1,0:T(8,128)S(1)}, f32[8,2048]{1,0:T(8,128)S(1)}, u32[]{:S(2)}, u32[]{:S(2)}) collective-permute-start(f32[8,2048]{1,0:T(8,128)S(1)} %get-tuple-element.54), channel_id=1, source_target_pairs={{0,3},{1,2},{2,1},{3,0},{4,7},{5,6},{6,5},{7,4},{8,11},{9,10},{10,... | collective-permute-start | bytes 196616 | tf_op jit(solution)/shard_map/ppermute | solution.py:570
  14.2 0.0 collective-permute-start.3
  14.2 0.6 %collective-permute-start.4 = (f32[8,2048]{1,0:T(8,128)S(1)}, f32[8,2048]{1,0:T(8,128)S(1)}, u32[]{:S(2)}, u32[]{:S(2)}) collective-permute-start(f32[8,2048]{1,0:T(8,128)S(1)} %get-tuple-element.56), channel_id=1, source_target_pairs={{0,2},{1,3},{2,0},{3,1},{4,6},{5,7},{6,4},{7,5},{8,10},{9,11},{10,... | collective-permute-start | bytes 196616 | tf_op jit(solution)/shard_map/ppermute | solution.py:570
  14.8 0.8 %copy.10.nbrs = s32[1,2,8,3]{3,2,1,0:T(8,128)S(1)} copy(s32[1,2,8,3]{2,1,3,0:T(2,128)} %param.13) | data formatting | bytes 384 | tf_op args[5]
  15.6 0.8 %copy.11.far = s32[1,2,8,4]{3,2,1,0:T(8,128)S(1)} copy(s32[1,2,8,4]{2,3,1,0:T(4,128)} %param.14) | data formatting | bytes 512 | tf_op args[6]
  16.4 0.7 %copy-done.1 = s32[1,4,8]{2,1,0:T(4,128)S(1)} copy-done((s32[1,4,8]{2,1,0:T(4,128)S(1)}, s32[1,4,8]{2,1,0:T(4,128)}, u32[]{:S(2)}) %copy-start.1) | copy-done | bytes 152
  17.1 0.7 %copy-done.2 = s32[1,2,8]{2,1,0:T(2,128)S(1)} copy-done((s32[1,2,8]{2,1,0:T(2,128)S(1)}, s32[1,2,8]{2,1,0:T(2,128)}, u32[]{:S(2)}) %copy-start.2) | copy-done | bytes 88
  17.7 0.7 %copy-done.3 = s32[1,2]{1,0:T(1,128)S(1)} copy-done((s32[1,2]{1,0:T(1,128)S(1)}, s32[1,2]{1,0:T(1,128)}, u32[]{:S(2)}) %copy-start.3) | copy-done | bytes 32
  18.4 1.7 %shard_map.99 = (f32[12,4,8,128]{3,2,1,0:T(8,128)S(1)}, f32[128,128]{1,0:T(8,128)S(1)}, f32[96,128]{1,0:T(8,128)S(1)}, f32[96,128]{1,0:T(8,128)S(1)}, s32[1,2,8]...) custom-call(f32[8,16384]{1,0:T(8,128)S(1)} %get-tuple-element.38.sta, ...), custom_call_target="tpu_custom_call" | custom-call | tf_op jit(solution)/shard_map/pallas_call | solution.py:28
  20.1 0.0 collective-permute-done.2.refs_1_
  20.1 0.0 collective-permute-done.3.refs_2_
  20.1 0.0 collective-permute-done.4.refs_3_
  20.1 10.1 %shard_map.102 = (f32[12,8,8,128]{3,2,1,0:T(8,128)S(1)}, f32[128,128]{1,0:T(8,128)S(1)}, f32[12,5,128,128]{3,2,1,0:T(8,128)S(1)}, f32[12,128,128]{2,1,0:T(8,128)...) custom-call(f32[12,4,8,128]{3,2,1,0:T(8,128)S(1)} %get-tuple-element, ...), custom_call_target="tpu_custom_call" | custom-call | tf_op jit(solution)/shard_map/pallas_call | solution.py:28
  30.3 1.0 %collective-permute-start.5 = (f32[8,1024]{1,0:T(8,128)S(1)}, f32[8,1024]{1,0:T(8,128)S(1)}, u32[]{:S(2)}, u32[]{:S(2)}) collective-permute-start(f32[8,1024]{1,0:T(8,128)S(1)} %get-tuple-element.70.refs_2_), channel_id=1, source_target_pairs={{0,2},{1,3},{2,0},{3,1},{4,6},{5,7},{6,4},{7,5},{8,10},{9,11},{10,... | collective-permute-start | bytes 98312 | tf_op jit(solution)/shard_map/ppermute | solution.py:570
  31.3 2.8 %collective-permute-start.6 = (f32[8,1024]{1,0:T(8,128)S(1)}, f32[8,1024]{1,0:T(8,128)S(1)}, u32[]{:S(2)}, u32[]{:S(2)}) collective-permute-start(f32[8,1024]{1,0:T(8,128)S(1)} %get-tuple-element.71.refs_3_), channel_id=1, source_target_pairs={{0,3},{1,2},{2,1},{3,0},{4,7},{5,6},{6,5},{7,4},{8,11},{9,10},{10,... | collective-permute-start | bytes 98312 | tf_op jit(solution)/shard_map/ppermute | solution.py:570
  34.1 0.0 collective-permute-start.7
  34.1 3.0 %shard_map.103 = (f32[8,16384]{1,0:T(8,128)S(1)}, f32[12,3,128,128]{3,2,1,0:T(8,128)S(1)}) custom-call(f32[12,8,8,128]{3,2,1,0:T(8,128)S(1)} %get-tuple-element.57.near, f32[128,128]{1,0:T(8,128)S(1)} %get-tuple-element.58.density, f32[12,5,128,128]{3,2,1,0:T(8,128)S(1)} %get-tuple-element.61.centre, f32[12,128,128]{2,1,0:T(8,128)S(1)} %get-tuple-element.59.press, ...), custom_call_target="tpu_custom_call" | custom-call | tf_op jit(solution)/shard_map/pallas_call | solution.py:28
  37.1 0.0 collective-permute-done.6.refs_6_
  37.1 0.9 %collective-permute-done.7.refs_7_ = f32[8,1024]{1,0:T(8,128)S(1)} collective-permute-done((f32[8,1024]{1,0:T(8,128)S(1)}, f32[8,1024]{1,0:T(8,128)S(1)}, u32[]{:S(2)}, u32[]{:S(2)}) %collective-permute-start.7) | collective-permute-done | bytes 32800 | tf_op jit(solution)/shard_map/ppermute | solution.py:570
  38.0 3.1 %shard_map.104 = (f32[3,16384]{1,0:T(4,128)}, f32[128,128]{1,0:T(8,128)}) custom-call(f32[12,8,8,128]{3,2,1,0:T(8,128)S(1)} %get-tuple-element.57.near, f32[128,128]{1,0:T(8,128)S(1)} %get-tuple-element.58.density, f32[12,128,128]{2,1,0:T(8,128)S(1)} %get-tuple-element.59.press, f32[12,3,512,128]{3,2,1,0:T(8,128)S(1)} %get-tuple-element.60.outside, ...), custom_call_target="tpu_custom_call" | custom-call | tf_op jit(solution)/shard_map/pallas_call | solution.py:28
  (5 shorter events, 0.0 us)
Async XLA Ops:
  1.4 1.0 %copy-start = (f32[7,16384]{1,0:T(8,128)S(1)}, f32[7,16384]{1,0:T(8,128)}, u32[]{:S(2)}) copy-start(f32[7,16384]{1,0:T(8,128)} %particles.1) | copy-start | bytes 1376260
  3.0 4.7 %collective-permute-start = (f32[8,512]{1,0:T(8,128)S(1)}, f32[8,512]{1,0:T(8,128)S(1)}, u32[]{:S(2)}, u32[]{:S(2)}) collective-permute-start(f32[8,512]{1,0:T(8,128)S(1)} %get-tuple-element.39), channel_id=1, source_target_pairs={{0,8},{4,12},{8,0},{12,4},{16,24},{20,28},{24,16},{28,20},{1,9},{5... | collective-permute-start | bytes 49160 | tf_op jit(solution)/shard_map/ppermute | solution.py:570
  7.9 1.6 %collective-permute-start.1 = (f32[8,512]{1,0:T(8,128)S(1)}, f32[8,512]{1,0:T(8,128)S(1)}, u32[]{:S(2)}, u32[]{:S(2)}) collective-permute-start(f32[8,512]{1,0:T(8,128)S(1)} %shard_map.98.after), channel_id=1, source_target_pairs={{0,4},{4,0},{8,12},{12,8},{16,20},{20,16},{24,28},{28,24},{1,5},{5... | collective-permute-start | bytes 49160 | tf_op jit(solution)/shard_map/ppermute | solution.py:570
  10.0 10.1 %collective-permute-start.2 = (f32[8,2048]{1,0:T(8,128)S(1)}, f32[8,2048]{1,0:T(8,128)S(1)}, u32[]{:S(2)}, u32[]{:S(2)}) collective-permute-start(f32[8,2048]{1,0:T(8,128)S(1)} %get-tuple-element.54), channel_id=1, source_target_pairs={{0,3},{1,2},{2,1},{3,0},{4,7},{5,6},{6,5},{7,4},{8,11},{9,10},{10,... | collective-permute-start | bytes 196616 | tf_op jit(solution)/shard_map/ppermute | solution.py:570
  14.2 5.9 %collective-permute-start.3 = (f32[8,2048]{1,0:T(8,128)S(1)}, f32[8,2048]{1,0:T(8,128)S(1)}, u32[]{:S(2)}, u32[]{:S(2)}) collective-permute-start(f32[8,2048]{1,0:T(8,128)S(1)} %get-tuple-element.55), channel_id=1, source_target_pairs={{0,1},{1,0},{2,3},{3,2},{4,5},{5,4},{6,7},{7,6},{8,9},{9,8},{10,11... | collective-permute-start | bytes 196616 | tf_op jit(solution)/shard_map/ppermute | solution.py:570
  14.2 5.9 %collective-permute-start.4 = (f32[8,2048]{1,0:T(8,128)S(1)}, f32[8,2048]{1,0:T(8,128)S(1)}, u32[]{:S(2)}, u32[]{:S(2)}) collective-permute-start(f32[8,2048]{1,0:T(8,128)S(1)} %get-tuple-element.56), channel_id=1, source_target_pairs={{0,2},{1,3},{2,0},{3,1},{4,6},{5,7},{6,4},{7,5},{8,10},{9,11},{10,... | collective-permute-start | bytes 196616 | tf_op jit(solution)/shard_map/ppermute | solution.py:570
  16.4 0.7 %copy-start.1 = (s32[1,4,8]{2,1,0:T(4,128)S(1)}, s32[1,4,8]{2,1,0:T(4,128)}, u32[]{:S(2)}) copy-start(s32[1,4,8]{2,1,0:T(4,128)} %exports.1) | copy-start | bytes 388
  17.1 0.7 %copy-start.2 = (s32[1,2,8]{2,1,0:T(2,128)S(1)}, s32[1,2,8]{2,1,0:T(2,128)}, u32[]{:S(2)}) copy-start(s32[1,2,8]{2,1,0:T(2,128)} %ids.1) | copy-start | bytes 196
  17.7 0.7 %copy-start.3 = (s32[1,2]{1,0:T(1,128)S(1)}, s32[1,2]{1,0:T(1,128)}, u32[]{:S(2)}) copy-start(s32[1,2]{1,0:T(1,128)} %counts.1) | copy-start | bytes 28
  30.3 6.8 %collective-permute-start.5 = (f32[8,1024]{1,0:T(8,128)S(1)}, f32[8,1024]{1,0:T(8,128)S(1)}, u32[]{:S(2)}, u32[]{:S(2)}) collective-permute-start(f32[8,1024]{1,0:T(8,128)S(1)} %get-tuple-element.70.refs_2_), channel_id=1, source_target_pairs={{0,2},{1,3},{2,0},{3,1},{4,6},{5,7},{6,4},{7,5},{8,10},{9,11},{10,... | collective-permute-start | bytes 98312 | tf_op jit(solution)/shard_map/ppermute | solution.py:570
  31.3 5.8 %collective-permute-start.6 = (f32[8,1024]{1,0:T(8,128)S(1)}, f32[8,1024]{1,0:T(8,128)S(1)}, u32[]{:S(2)}, u32[]{:S(2)}) collective-permute-start(f32[8,1024]{1,0:T(8,128)S(1)} %get-tuple-element.71.refs_3_), channel_id=1, source_target_pairs={{0,3},{1,2},{2,1},{3,0},{4,7},{5,6},{6,5},{7,4},{8,11},{9,10},{10,... | collective-permute-start | bytes 98312 | tf_op jit(solution)/shard_map/ppermute | solution.py:570
  34.1 3.9 %collective-permute-start.7 = (f32[8,1024]{1,0:T(8,128)S(1)}, f32[8,1024]{1,0:T(8,128)S(1)}, u32[]{:S(2)}, u32[]{:S(2)}) collective-permute-start(f32[8,1024]{1,0:T(8,128)S(1)} %get-tuple-element.69.refs_1_), channel_id=1, source_target_pairs={{0,1},{1,0},{2,3},{3,2},{4,5},{5,4},{6,7},{7,6},{8,9},{9,8},{10,11... | collective-permute-start | bytes 98312 | tf_op jit(solution)/shard_map/ppermute | solution.py:570

commit v6 on v5

--- a/solution.py
+++ b/solution.py
@@ -12,8 +12,9 @@
 KERNEL_NORM = 21.0 / (16.0 * math.pi)
 FORCE_NORM = 5.0 * KERNEL_NORM * 32.0 * (2.0 / 3.0)
 TINY = 1e-30
-BLOCK_ORDER = (3, 1, 2)
+BLOCK_ORDER = (2, 3, 1)
 RETURN_ORDER = (2, 3, 1)
+PIECES = 4
 F32 = jnp.float32
 I32 = jnp.int32
 VMEM = pltpu.VMEM
@@ -21,7 +22,7 @@
 DMA = pltpu.SemaphoreType.DMA
 
 
-def call(kernel, out_shape, *args, smem=(), scratch=(), limit=16 << 20, cost=0):
+def call(kernel, out_shape, *args, smem=(), scratch=(), limit=16 << 20, out_any=False):
     def space(n):
         return SMEM if n in smem else VMEM
 
@@ -29,12 +30,11 @@
         kernel,
         out_shape=out_shape,
         in_specs=[pl.BlockSpec(memory_space=space(n)) for n in range(len(args))],
-        out_specs=jax.tree.map(lambda _: pl.BlockSpec(memory_space=VMEM), out_shape),
+        out_specs=jax.tree.map(
+            lambda _: pl.BlockSpec(memory_space=pl.ANY if out_any else VMEM), out_shape
+        ),
         scratch_shapes=list(scratch),
         compiler_params=pltpu.CompilerParams(vmem_limit_bytes=limit),
-        cost_estimate=pl.CostEstimate(flops=0, transcendentals=0, bytes_accessed=cost)
-        if cost
-        else None,
     )(*args)
 
 
@@ -92,9 +92,7 @@
     return [SMEM(a.shape, I32) for a in arrays] + [DMA((len(arrays),))]
 
 
-def first_kernel(particles, ints, out, state):
-    state[0:7, :] = particles[...]
-    state[7:8, :] = jnp.zeros((1, state.shape[1]), F32)
+def first_kernel(state, ints, out):
     for c in range(ints.shape[1] // BLK):
         out[:, chunk(c)] = columns(state, wide(ints[0:1, chunk(c)]))
 
@@ -147,20 +145,21 @@
     tables[3] = valid[0]
     for c in range(mig // BLK):
         slots = wide(ints[1:2, chunk(c)])
+        two, three = (wide(ints[level : level + 1, chunk(c)]) for level in (2, 3))
         marks[0:1, chunk(c)] = code_at(tables.at[3], slots)
+        marks[1:2, chunk(c)] = code_at(tables.at[0], two)
+        marks[2:3, chunk(c)] = code_at(tables.at[0], three)
+        marks[3:4, chunk(c)] = code_at(tables.at[2], three)
         cols[:, chunk(c)] = columns(state, slots)
 
 
 def late_tables_kernel(
-    state, ints, tables, after, cols, marks, raw, code_rows, exported, sems
+    state, ints, tables, after, cols, raw, code_rows, exported, sems
 ):
     peers, slots, _ = code_rows.shape
     copies = fetch([ints.at[pl.ds(8, peers), pl.ds(0, BLK)]], [exported], sems)
     for c in range(ints.shape[1] // BLK):
         two, three = (wide(ints[level : level + 1, chunk(c)]) for level in (2, 3))
-        marks[1:2, chunk(c)] = code_at(tables.at[0], two)
-        marks[2:3, chunk(c)] = code_at(tables.at[0], three)
-        marks[3:4, chunk(c)] = code_at(tables.at[2], three)
         cols[0, :, chunk(c)] = columns(state, two)
         cols[1, :, chunk(c)] = columns(state, three)
     for copy in copies:
@@ -188,28 +187,91 @@
     return jnp.where(row == 7, wide(codes[1, pl.ds(block, 1), :]).astype(F32), patched)
 
 
+def packed_width(mig, slots):
+    total = mig * 2 // BLK + slots
+    return total - total // 8
+
+
 def export_kernel(cols, marks, got0, got1, raw, code_rows, *outs):
     count = got0.shape[1] // BLK
     slots = code_rows.shape[1]
     tables = tables_of(got0, count) + tables_of(got1, count)
     row = lax.broadcasted_iota(I32, (8, BLK), 0)
+    twos, threes = [], []
     for c in range(count):
-        two = patch(cols[0, :, chunk(c)], wide(marks[1:2, chunk(c)]), tables)
+        twos.append(patch(cols[0, :, chunk(c)], wide(marks[1:2, chunk(c)]), tables))
         three = patch(cols[1, :, chunk(c)], wide(marks[2:3, chunk(c)]), tables)
-        three = jnp.where(row == 7, wide(marks[3:4, chunk(c)]).astype(F32), three)
-        for out in outs:
-            out[:, chunk(c)] = two
-            out[:, chunk(count + c)] = three
+        threes.append((three, wide(marks[3:4, chunk(c)]).astype(F32)))
     for q, out in enumerate(outs):
+        coded = list(threes)
         for t in range(slots):
             values = raw[:, chunk(q * slots + t)]
             patched = patch(values, wide(code_rows[q, t : t + 1, :]), tables)
-            out[:, chunk(2 * count + t)] = jnp.where(row == 7, values, patched)
-
-
-def live_slot(counts, n, nact):
-    second = n >= counts[0, 0]
-    return jnp.where(second, 1, 0), jnp.where(second, jnp.minimum(n - counts[0, 0], nact - 1), n)
+            coded.append((patched, wide(values[7:8, :])))
+        code_row = 7 if q == 0 else 6
+        items = list(twos)
+        if q == 1:
+            for c in range(count):
+                items[c] = jnp.where(row == 6, wide(threes[c][0][6:7, :]), twos[c])
+        items += [jnp.where(row == code_row, code, v) for v, code in coded]
+        kept = out.shape[1] // BLK
+        for i in range(kept):
+            item = items[i]
+            if kept < len(items):
+                item = jnp.where(row == 7, wide(items[kept + i // 7][i % 7 : i % 7 + 1, :]), item)
+            out[:, chunk(i)] = item
+
+
+def unpacked(ref, total):
+    kept = ref.shape[1] // BLK
+    items = [ref[:, chunk(i)] for i in range(kept)]
+    for extra in range(total - kept):
+        rows = [ref[7:8, chunk(7 * extra + r)] for r in range(7)]
+        items.append(jnp.concatenate(rows + rows[:1], axis=0))
+    return items, 7 if kept == total else 6
+
+
+class Indices:
+    def __init__(self, ref, near, far):
+        self.ref, self.near, self.far = ref, near, far
+        self.counts = 2 + 2 * (near + far)
+
+    def live(self):
+        return self.ref[self.counts, 0] + self.ref[self.counts, 1]
+
+    def slot(self, n):
+        first = self.ref[self.counts, 0]
+        second = n >= first
+        last = self.ref.shape[1] - 1
+        return jnp.where(second, 1, 0), jnp.where(second, jnp.minimum(n - first, last), n)
+
+    def active(self, n):
+        which, i = self.slot(n)
+        return self.ref[which, i]
+
+    def near_blocks(self, n):
+        which, i = self.slot(n)
+        return [self.ref[2 + 2 * t + which, i] for t in range(self.near)]
+
+    def ghosts(self, n, mine):
+        which, i = self.slot(n)
+        start = 2 + 2 * self.near + which * self.far
+        return [self.ref[start + t, i] ^ mine for t in range(self.far)]
+
+    def exported(self, place, t):
+        return self.ref[self.counts + 1 + place, t]
+
+
+def pack_indices(packed, ids, counts, nbrs, far, exports):
+    packed[...] = jnp.zeros_like(packed)
+    packed[0:2, :] = ids[0]
+    at = 2
+    for part in (nbrs, far):
+        for k in range(part.shape[1]):
+            packed[at : at + part.shape[2], :] = part[0, k]
+            at += part.shape[2]
+    packed[at : at + 1, 0:2] = counts[...]
+    packed[at + 1 : at + 1 + exports.shape[1], :] = exports[0]
 
 
 def picked_rows(chosen, table):
@@ -225,15 +287,16 @@
     )
 
 
-def own_kernel(state, got0, got1, codes, ids, counts, nbrs, far, exports, *refs):
-    own, density, near_pick, far_pick = refs[:4]
-    copied, small = refs[4:9], refs[9:]
-    for source, target in zip((ids, counts, nbrs, far, exports), copied):
-        target[...] = source[...]
-    copies = fetch([ids, counts, nbrs, far], small[:4], small[4])
-    ids, counts, nbrs, far = small[:4]
+def own_kernel(
+    state, got0, got1, codes, ids, counts, nbrs, far, exports, own, density, near_pick, far_pick,
+    packed, *small
+):
+    pack_indices(packed, ids, counts, nbrs, far, exports)
+    copies = fetch([packed], [small[0]], small[1])
+    inner = own.shape[1]
+    indices = Indices(small[0], inner - 1, 8 - inner)
     me = lax.axis_index("gy")
-    slots = 8
+    slots = packed.shape[1]
     near_pick[...] = jnp.zeros_like(near_pick)
     far_pick[...] = jnp.zeros_like(far_pick)
     near_lane = lax.broadcasted_iota(I32, (1, near_pick.shape[1]), 1)
@@ -247,19 +310,16 @@
     for v in range(blocks // 8):
         part = slice(8 * v, 8 * v + 8)
         density[part, :] = patch(density[part, :], codes[0, part, :], last)
-    nact = ids.shape[2]
 
     for copy in copies:
         copy.wait()
     for n in range(TOTACT):
-        which, i = live_slot(counts, n, nact)
-        wanted = [ids[0, which, i]] + [nbrs[0, which, i, t] for t in range(nbrs.shape[3])]
+        wanted = [indices.active(n)] + indices.near_blocks(n)
         for t, block in enumerate(wanted):
             own[n, t] = early_block(state, codes, tables, block)
             near_pick[8 * n + t : 8 * n + t + 1, :] = jnp.where(near_lane == block, 1.0, 0.0)
-        for t in range(far.shape[3]):
-            g = far[0, which, i, t] ^ (me * slots)
-            at = 8 * n + len(wanted) + t
+        for t, g in enumerate(indices.ghosts(n, me * slots)):
+            at = 8 * n + inner + t
             far_pick[at : at + 1, :] = jnp.where(far_lane == g, 1.0, 0.0)
 
 
@@ -342,35 +402,42 @@
 
 
 def make_density_kernel(peers, slots):
-    def density_kernel(own, before, codes, ids, counts, far, exports, *refs):
+    def density_kernel(own, before, codes, packed, *refs):
         sent = by_partner(refs[:peers], BLOCK_ORDER)
         near, density, centre, press, inside, outside = refs[peers : peers + 6]
         outs = refs[peers + 6 : 2 * peers + 6]
         (late_three, ghosts, first, second, fresh, others, rows, back, *small) = refs[
             2 * peers + 6 :
         ]
-        copies = fetch([ids, counts, far, exports], small[:4], small[4])
-        ids, counts, far, exports = small[:4]
+        copies = fetch([packed], [small[0]], small[1])
+        inner = own.shape[1]
+        ngh = 8 - inner
+        indices = Indices(small[0], inner - 1, ngh)
         count = late_three.shape[2] // BLK
         blocks = density.shape[0]
+        row = lax.broadcasted_iota(I32, (8, BLK), 0)
         me = lax.axis_index("gy")
 
         for q in range(peers):
+            items, code_row = unpacked(sent[q], 2 * count + slots)
             tables = tables_of(sent[q ^ 2], count)
             for c in range(count):
-                values = sent[q][:, chunk(count + c)]
-                code = wide(values[7:8, :]).astype(I32)
+                values = items[count + c]
+                code = wide(values[code_row : code_row + 1, :]).astype(I32)
+                if q == 1:
+                    values = jnp.where(row == 6, wide(items[c][6:7, :]), values)
                 late_three[q, :, chunk(c)] = patch(values, code, tables)
 
-        def settle(values, q):
-            code = wide(values[7:8, :]).astype(I32)
+        def settle(values, q, code_row=7):
+            code = wide(values[code_row : code_row + 1, :]).astype(I32)
             tables = tables_of(sent[q ^ 2], count)
             tables += [late_three[q ^ 1, :, chunk(c)] for c in range(count)]
             return patch(values, code, tables)
 
         for q in range(peers):
+            items, code_row = unpacked(sent[q], 2 * count + slots)
             for t in range(slots):
-                ghosts[:, chunk(q * slots + t)] = settle(sent[q][:, chunk(2 * count + t)], q)
+                ghosts[:, chunk(q * slots + t)] = settle(items[2 * count + t], q, code_row)
 
         later = [sent[2][6:7, chunk(c)] for c in range(count)]
         later = [wide(x) for x in later + [late_three[1, 6:7, chunk(c)] for c in range(count)]]
@@ -381,19 +448,12 @@
 
         for copy in copies:
             copy.wait()
-        live = counts[0, 0] + counts[0, 1]
-        nact = ids.shape[2]
-        inner = own.shape[1]
-        ngh = far.shape[3]
-
-        def far_of(n):
-            which, i = live_slot(counts, n, nact)
-            return [far[0, which, i, t] ^ (me * slots) for t in range(ngh)]
+        live = indices.live()
 
         for n in range(TOTACT):
             for t in range(inner):
                 near[n, :, t, :] = settle(own[n, t], 0)
-            for t, g in enumerate(far_of(n)):
+            for t, g in enumerate(indices.ghosts(n, me * slots)):
                 near[n, :, inner + t, :] = ghosts[:, lanes(g)]
 
         def prepare(n, buffer):
@@ -424,19 +484,18 @@
                     rows[n, k, t : t + 1, :] = total * (scale if k < 3 else scale * u)
 
         for n in range(TOTACT):
-            for t, g in enumerate(far_of(n)):
+            for t, g in enumerate(indices.ghosts(n, me * slots)):
                 back[0:6, lanes(g)] += jnp.where(n < live, rows[n, 0:6, t, :], 0.0)
 
         def place(n, _):
-            which, i = live_slot(counts, n, nact)
-            density[pl.ds(ids[0, which, i], 1), :] = fresh[pl.ds(n, 1), :]
+            density[pl.ds(indices.active(n), 1), :] = fresh[pl.ds(n, 1), :]
             return 0
 
         lax.fori_loop(0, live, place, 0)
         for q in range(peers):
             outs[q][...] = back[:, q * slots * BLK : (q + 1) * slots * BLK]
             for t in range(slots):
-                rho = density[pl.ds(exports[0, me ^ q, t], 1), :]
+                rho = density[pl.ds(indices.exported(me ^ q, t), 1), :]
                 outs[q][6:7, chunk(t)] = rho
 
     return density_kernel
@@ -470,11 +529,12 @@
 
 
 def inner_kernel(
-    near, density, centre, press, inside, near_pick, ids, counts, nbrs, totals, sums, *refs
+    near, density, centre, press, inside, near_pick, packed, totals, sums, *refs
 ):
     others_press, others, rows, *small = refs
-    copies = fetch([ids, counts, nbrs], small[:3], small[3])
-    ids, counts, nbrs = small[:3]
+    copies = fetch([packed], [small[0]], small[1])
+    inner = inside.shape[1] // BLK
+    indices = Indices(small[0], inner - 1, 8 - inner)
     totals[...] = jnp.zeros_like(totals)
     rho = picked_rows(near_pick[...], density[...])
     for n in range(TOTACT):
@@ -487,18 +547,16 @@
     lax.fori_loop(0, TOTACT, step, 0)
     for copy in copies:
         copy.wait()
-    live = counts[0, 0] + counts[0, 1]
-    inner = 1 + nbrs.shape[3]
+    live = indices.live()
     for n in range(TOTACT):
-        which, i = live_slot(counts, n, ids.shape[2])
+        blocks = indices.near_blocks(n)
         for t in range(1, inner):
             scale = -FORCE_NORM / near[n, 3, t : t + 1, :]
             for k in range(3):
                 row = 8 * (k * inner + t)
                 total = jnp.sum(others[n, row : row + 8, :], axis=0, keepdims=True)
                 rows[n, k, t : t + 1, :] = total * scale
-            block = nbrs[0, which, i, t - 1]
-            totals[0:3, lanes(block)] += jnp.where(n < live, rows[n, 0:3, t, :], 0.0)
+            totals[0:3, lanes(blocks[t - 1])] += jnp.where(n < live, rows[n, 0:3, t, :], 0.0)
 
 
 def outer_sums(near, n, press, others_press, outside, before, rows):
@@ -526,14 +584,16 @@
 
 def make_outer_kernel(peers, slots):
     def outer_kernel(
-        near, density, press, outside, totals, before, far_pick, ids, counts, exports, *refs
+        near, density, press, outside, totals, before, far_pick, packed, *refs
     ):
         sent = refs[:peers]
         got = by_partner(refs[peers : 2 * peers], RETURN_ORDER)
-        out, density_out, far_rho, others_press, rows, *small = refs[2 * peers :]
-        copies = fetch([ids, counts, exports], small[:3], small[3])
-        ids, counts, exports = small[:3]
-        density_out[...] = density[...]
+        accel, density_out, out, far_rho, others_press, rows, sems, *small = refs[2 * peers :]
+        density_copy = pltpu.make_async_copy(density, density_out, sems.at[PIECES])
+        density_copy.start()
+        copies = fetch([packed], [small[0]], small[1])
+        ngh = outside.shape[2] // BLK
+        indices = Indices(small[0], 7 - ngh, ngh)
         far_rho[...] = jnp.zeros_like(far_rho)
         for q in range(peers):
             for t in range(slots):
@@ -545,22 +605,31 @@
             others_press[n] = near[n, 5] / rho[8 * n : 8 * n + 8]
 
         def step(n, _):
-            outer_sums(near, n, press, others_press, outside, before, rows)
+            outer_sums(near, 2 * n, press, others_press, outside, before, rows)
+            outer_sums(near, 2 * n + 1, press, others_press, outside, before, rows)
             return 0
 
-        lax.fori_loop(0, TOTACT, step, 0)
+        lax.fori_loop(0, TOTACT // 2, step, 0)
         for copy in copies:
             copy.wait()
         me = lax.axis_index("gy")
-        live = counts[0, 0] + counts[0, 1]
+        live = indices.live()
         for q in range(peers):
             for t in range(slots):
                 own_rho = sent[q][6:7, chunk(t)]
                 value = got[q][0:3, chunk(t)] + got[q][3:6, chunk(t)] / own_rho
-                out[0:3, lanes(exports[0, me ^ q, t])] += value
+                out[0:3, lanes(indices.exported(me ^ q, t))] += value
         for n in range(TOTACT):
-            which, i = live_slot(counts, n, ids.shape[2])
-            out[0:3, lanes(ids[0, which, i])] += jnp.where(n < live, rows[n, 0:3, :], 0.0)
+            out[0:3, lanes(indices.active(n))] += jnp.where(n < live, rows[n, 0:3, :], 0.0)
+        size = out.shape[1] // PIECES
+        copies = [density_copy]
+        for p in range(PIECES):
+            part = slice(p * size, (p + 1) * size)
+            copy = pltpu.make_async_copy(out.at[:, part], accel.at[:, part], sems.at[p])
+            copy.start()
+            copies.append(copy)
+        for copy in copies:
+            copy.wait()
 
     return outer_kernel
 
@@ -602,7 +671,8 @@
         ],
         axis=0,
     )
-    sent0, state = call(first_kernel, [shape(8, mig), shape(8, per_dev)], particles, ints)
+    state = jnp.pad(particles, ((0, 1), (0, 0)))
+    sent0 = call(first_kernel, shape(8, mig), state, ints)
     codes = call(codes_kernel, shape(4, blocks, BLK, dtype=I32), ints)
     got0 = crossed(sent0, "gx", 2)
     cols1, marks1, tables = call(
@@ -614,11 +684,10 @@
     )
     sent1 = call(second_kernel, shape(8, mig), cols1, marks1, got0)
     got1 = crossed(sent1, "gx", 1)
-    cols, marks, raw, code_rows = call(
+    cols, raw, code_rows = call(
         late_tables_kernel,
         [
             shape(2, 8, mig),
-            shape(8, mig, dtype=I32),
             shape(8, wide_total),
             shape(peers, slots, BLK, dtype=I32),
         ],
@@ -630,34 +699,39 @@
     )
     packs = call(
         export_kernel,
-        [shape(8, 2 * mig + slots * BLK)] * peers,
+        [
+            shape(8, 2 * mig + slots * BLK if q == 0 else packed_width(mig, slots) * BLK)
+            for q in range(peers)
+        ],
         cols,
-        marks,
+        marks1,
         got0,
         got1,
         raw,
         code_rows,
     )
     sent = exchanged(packs, BLOCK_ORDER)
-    small = [active_ids, active_count, local_nbrs, ghost_slots]
-    own, before, near_pick, far_pick, ids, counts, nbrs, far, export_ids = call(
+    packed = shape(3 + 2 * 7 + peers, active_ids.shape[2], dtype=I32)
+    own, before, near_pick, far_pick, packed = call(
         own_kernel,
         [
             shape(TOTACT, inner, 8, BLK),
             shape(blocks, BLK),
             shape(TOTACT * 8, blocks),
             shape(TOTACT * 8, max(BLK, peers * slots)),
-        ]
-        + [shape(*a.shape, dtype=I32) for a in small + [export_blocks]],
+            packed,
+        ],
         state,
         got0,
         got1,
         tables,
-        *small,
+        active_ids,
+        active_count,
+        jnp.transpose(local_nbrs, (0, 3, 1, 2)),
+        jnp.transpose(ghost_slots, (0, 1, 3, 2)),
         export_blocks,
-        scratch=fetch_scratch(small),
-    )
-    indices = [ids, counts, far, export_ids]
+        scratch=fetch_scratch([packed]),
+    )
     local = shape(TOTACT, inner * BLK, BLK)
     remote = shape(TOTACT, 3, (8 - inner) * BLK, BLK)
     near, density, centre, press, inside, outside, *returns = call(
@@ -674,7 +748,7 @@
         own,
         before,
         tables,
-        *indices,
+        packed,
         *sent,
         scratch=[
             VMEM((peers, 8, mig), F32),
@@ -686,10 +760,9 @@
             VMEM((TOTACT, 8, 8, BLK), F32),
             VMEM((8, wide_total), F32),
         ]
-        + fetch_scratch(indices),
+        + fetch_scratch([packed]),
     )
     got = exchanged(returns, RETURN_ORDER)
-    small = [ids, counts, nbrs]
     totals, sums = call(
         inner_kernel,
         [shape(8, per_dev), shape(TOTACT, 3, BLK, BLK)],
@@ -699,15 +772,14 @@
         press,
         inside,
         near_pick,
-        *small,
+        packed,
         scratch=[
             VMEM((TOTACT, 8, BLK), F32),
             VMEM((TOTACT, 3 * inner * 8, BLK), F32),
             VMEM((TOTACT, 8, 8, BLK), F32),
         ]
-        + fetch_scratch(small),
-    )
-    small = [ids, counts, export_ids]
+        + fetch_scratch([packed]),
+    )
     accel, density_out = call(
         make_outer_kernel(peers, slots),
         [shape(3, per_dev), shape(blocks, BLK)],
@@ -718,15 +790,18 @@
         totals,
         sums,
         far_pick,
-        *small,
+        packed,
         *returns,
         *got,
+        out_any=True,
         scratch=[
+            VMEM((3, per_dev), F32),
             VMEM((max(BLK, peers * slots), BLK), F32),
             VMEM((TOTACT, 8, BLK), F32),
             VMEM((TOTACT, 8, BLK), F32),
+            DMA((PIECES + 1,)),
         ]
-        + fetch_scratch(small),
+        + fetch_scratch([packed]),
     )
     return density_out.reshape(-1), accel
 

time: 41.4 us -> 39.6 us (0.957)
  local copies, waits for them, and re-layouts: 4.58 us -> 1.13 us
  waiting for transfers between devices: 1.37 us -> 3.55 us
  Pallas kernels: 21.9 us -> 21.4 us
    unnamed x10, local copies, waits for them, and re-layouts: 4.58 us -> 0.02 us
    ppermute x8, waiting for transfers between devices: 1.37 us -> 3.55 us  [crossed(): lax.ppermute(block, axis, [(i, i ^ bits) for i in range(size) if i ^ bits...]
    pad x0 -> x1, local copies, waits for them, and re-layouts: none -> 1.11 us  [shards(): state = jnp.pad(particles, ((0, 1), (0, 0)))]
    pallas_call x10, Pallas kernels: 21.9 us -> 21.4 us  [call(): pl.pallas_call(kernel, out_shape=out_shape, in_specs=[pl.BlockSpec(memory...]
  transfers between devices with their start and end apart: 8 -> 8, of which waited for: 2 -> 4; matrix products, arithmetic and copies ran while one was open for 4% -> 0% of each run, Pallas kernels for 18% -> 19%
where the time goes in v6:
time: 39.6 us; the launch traced here: 39 us
  Pallas kernels  21.4 us (54%)
  starting transfers between devices  11.4 us (29%)
  waiting for transfers between devices  3.55 us (9%)
  local copies, waits for them, and re-layouts  1.13 us (3%)
  between operations  0.8 us (2%)
  other arithmetic  0.74 us (2%)
    pallas_call x10, Pallas kernels, call(): pl.pallas_call(kernel, out_shape=out_shape, in_specs=[pl.BlockSpec(memory...  21.4 us
    ppermute x8, starting transfers between devices, crossed(): lax.ppermute(block, axis, [(i, i ^ bits) for i in range(size) if i ^ bits...  11.4 us
    ppermute x8, waiting for transfers between devices, crossed(): lax.ppermute(block, axis, [(i, i ^ bits) for i in range(size) if i ^ bits...  3.55 us
    pad x1, local copies, waits for them, and re-layouts, shards(): state = jnp.pad(particles, ((0, 1), (0, 0)))  1.11 us
  transfers between devices with their start and end apart: 8, of which 4 were waited for; matrix products, arithmetic and copies ran while one was open for 0% of the time, Pallas kernels for 19%

profile of v6, /device:TPU:0, one launch (start us, length us, event | category | flops | bytes accessed | tf_op | source)
XLA Modules:
  0.0 39.0 jit_solution(11801442820341272176)
XLA Ops:
  0.6 0.0 copy-start
  0.6 0.0 copy-start.2
  0.7 0.0 copy-start.1
  0.7 0.0 copy-start.3
  0.7 1.1 %pad.12.state = f32[8,16384]{1,0:T(8,128)S(1)} pad(f32[7,16384]{1,0:T(8,128)} %param.8, f32[]{:T(128)} %constant.2.clone.1), padding=0_1x0_0 | pad | bytes 983044 | tf_op jit(solution)/shard_map/jit(_pad)/pad | solution.py:674
  1.8 0.7 %pad_add_fusion.ints = s32[12,512]{1,0:T(8,128)S(1)} fusion(s32[4,8]{1,0:T(4,128)} %bitcast.5, s32[1,4]{1,0:T(1,128)} %param.9, s32[4,512]{1,0:T(4,128)} %bitcast.8), kind=kLoop, calls=%fused_computation | loop fusion | flops 12288 | bytes 32912 | tf_op jit(solution)/shard_map/concatenate | solution.py:666
  2.5 0.6 %shard_map.95 = f32[8,512]{1,0:T(8,128)S(1)} custom-call(f32[8,16384]{1,0:T(8,128)S(1)} %pad.12.state, s32[12,512]{1,0:T(8,128)S(1)} %pad_add_fusion.ints), custom_call_target="tpu_custom_call" | custom-call | tf_op jit(solution)/shard_map/pallas_call | solution.py:29
  3.2 3.0 %collective-permute-start = (f32[8,512]{1,0:T(8,128)S(1)}, f32[8,512]{1,0:T(8,128)S(1)}, u32[]{:S(2)}, u32[]{:S(2)}) collective-permute-start(f32[8,512]{1,0:T(8,128)S(1)} %shard_map.95), channel_id=1, source_target_pairs={{0,8},{4,12},{8,0},{12,4},{16,24},{20,28},{24,16},{28,20},{1,9},{5... | collective-permute-start | bytes 49160 | tf_op jit(solution)/shard_map/ppermute | solution.py:639
  6.2 0.5 %shard_map.96.codes = s32[4,128,128]{2,1,0:T(8,128)S(1)} custom-call(s32[12,512]{1,0:T(8,128)S(1)} %pad_add_fusion.ints), custom_call_target="tpu_custom_call" | custom-call | tf_op jit(solution)/shard_map/pallas_call | solution.py:29
  6.7 1.0 %shard_map.97 = (f32[8,512]{1,0:T(8,128)S(1)}, s32[8,512]{1,0:T(8,128)S(1)}, s32[4,128,128]{2,1,0:T(8,128)S(1)}) custom-call(f32[8,16384]{1,0:T(8,128)S(1)} %pad.12.state, s32[12,512]{1,0:T(8,128)S(1)} %pad_add_fusion.ints, s32[4,128,128]{2,1,0:T(8,128)S(1)} %shard_map.96.codes), custom_call_target="tpu_custom_call" | custom-call | tf_op jit(solution)/shard_map/pallas_call | solution.py:29
  7.7 0.2 collective-permute-done.got0
  7.9 0.1 shard_map.98.after
  8.0 0.1 collective-permute-start.1
  8.1 1.3 %shard_map.100 = (f32[2,8,512]{2,1,0:T(8,128)S(1)}, f32[8,4096]{1,0:T(8,128)S(1)}, s32[4,8,128]{2,1,0:T(8,128)S(1)}) custom-call(f32[8,16384]{1,0:T(8,128)S(1)} %pad.12.state, s32[12,512]{1,0:T(8,128)S(1)} %pad_add_fusion.ints, s32[4,128,128]{2,1,0:T(8,128)S(1)} %get-tuple-element.33.codes.tables, f32[8,512]{1,0:T(8,128)S(1)} %shard_map.98.after), custom_call_target="tpu_custom_call" | custom-call | tf_op jit(solution)/shard_map/pallas_call | solution.py:29
  9.3 0.0 collective-permute-done.1.got1
  9.3 0.6 %shard_map.101 = (f32[8,2048]{1,0:T(8,128)S(1)}, f32[8,1792]{1,0:T(8,128)S(1)}, f32[8,1792]{1,0:T(8,128)S(1)}, f32[8,1792]{1,0:T(8,128)S(1)}) custom-call(f32[2,8,512]{2,1,0:T(8,128)S(1)} %get-tuple-element.37.cols, s32[8,512]{1,0:T(8,128)S(1)} %get-tuple-element.32.marks, f32[8,512]{1,0:T(8,128)S(1)} %collective-permute-done.got0, ...), custom_call_target="tpu_custom_call" | custom-call | tf_op jit(solution)/shard_map/pallas_call | solution.py:29
  9.9 3.2 %collective-permute-start.2 = (f32[8,1792]{1,0:T(8,128)S(1)}, f32[8,1792]{1,0:T(8,128)S(1)}, u32[]{:S(2)}, u32[]{:S(2)}) collective-permute-start(f32[8,1792]{1,0:T(8,128)S(1)} %get-tuple-element.41), channel_id=1, source_target_pairs={{0,2},{1,3},{2,0},{3,1},{4,6},{5,7},{6,4},{7,5},{8,10},{9,11},{10,... | collective-permute-start | bytes 172040 | tf_op jit(solution)/shard_map/ppermute | solution.py:639
  13.1 1.3 %collective-permute-start.3 = (f32[8,1792]{1,0:T(8,128)S(1)}, f32[8,1792]{1,0:T(8,128)S(1)}, u32[]{:S(2)}, u32[]{:S(2)}) collective-permute-start(f32[8,1792]{1,0:T(8,128)S(1)} %get-tuple-element.42), channel_id=1, source_target_pairs={{0,3},{1,2},{2,1},{3,0},{4,7},{5,6},{6,5},{7,4},{8,11},{9,10},{10,... | collective-permute-start | bytes 172040 | tf_op jit(solution)/shard_map/ppermute | solution.py:639
  14.4 0.2 collective-permute-start.4
  14.7 1.6 %shard_map.99 = (f32[12,4,8,128]{3,2,1,0:T(8,128)S(1)}, f32[128,128]{1,0:T(8,128)S(1)}, f32[96,128]{1,0:T(8,128)S(1)}, f32[96,128]{1,0:T(8,128)S(1)}, s32[21,8]{1,0:T(8,128)S(1)}) custom-call(f32[8,16384]{1,0:T(8,128)S(1)} %pad.12.state, f32[8,512]{1,0:T(8,128)S(1)} %collective-permute-done.got0, f32[8,512]{1,0:T(8,128)S(1)} %collective-permute-done.1.got1, ...), custom_call_target="tpu_custom_call" | custom-call | tf_op jit(solution)/shard_map/pallas_call | solution.py:29
  16.3 0.6 %collective-permute-done.2.refs_1_ = f32[8,1792]{1,0:T(8,128)S(1)} collective-permute-done((f32[8,1792]{1,0:T(8,128)S(1)}, f32[8,1792]{1,0:T(8,128)S(1)}, u32[]{:S(2)}, u32[]{:S(2)}) %collective-permute-start.2) | collective-permute-done | bytes 57376 | tf_op jit(solution)/shard_map/ppermute | solution.py:639
  16.9 2.7 %collective-permute-done.3.refs_2_ = f32[8,1792]{1,0:T(8,128)S(1)} collective-permute-done((f32[8,1792]{1,0:T(8,128)S(1)}, f32[8,1792]{1,0:T(8,128)S(1)}, u32[]{:S(2)}, u32[]{:S(2)}) %collective-permute-start.3) | collective-permute-done | bytes 57376 | tf_op jit(solution)/shard_map/ppermute | solution.py:639
  19.5 0.1 collective-permute-done.4.refs_3_
  19.6 10.1 %shard_map.102 = (f32[12,8,8,128]{3,2,1,0:T(8,128)S(1)}, f32[128,128]{1,0:T(8,128)S(1)}, f32[12,5,128,128]{3,2,1,0:T(8,128)S(1)}, f32[12,128,128]{2,1,0:T(8,128)...) custom-call(f32[12,4,8,128]{3,2,1,0:T(8,128)S(1)} %get-tuple-element, ...), custom_call_target="tpu_custom_call" | custom-call | tf_op jit(solution)/shard_map/pallas_call | solution.py:29
  29.7 0.1 collective-permute-start.5
  29.8 0.2 collective-permute-start.6
  30.0 3.3 %collective-permute-start.7 = (f32[8,1024]{1,0:T(8,128)S(1)}, f32[8,1024]{1,0:T(8,128)S(1)}, u32[]{:S(2)}, u32[]{:S(2)}) collective-permute-start(f32[8,1024]{1,0:T(8,128)S(1)} %get-tuple-element.55.refs_1_), channel_id=1, source_target_pairs={{0,1},{1,0},{2,3},{3,2},{4,5},{5,4},{6,7},{7,6},{8,9},{9,8},{10,11... | collective-permute-start | bytes 98312 | tf_op jit(solution)/shard_map/ppermute | solution.py:639
  33.3 3.0 %shard_map.103 = (f32[8,16384]{1,0:T(8,128)S(1)}, f32[12,3,128,128]{3,2,1,0:T(8,128)S(1)}) custom-call(f32[12,8,8,128]{3,2,1,0:T(8,128)S(1)} %get-tuple-element.44.near, f32[128,128]{1,0:T(8,128)S(1)} %get-tuple-element.45.density, f32[12,5,128,128]{3,2,1,0:T(8,128)S(1)} %get-tuple-element.48.centre, f32[12,128,128]{2,1,0:T(8,128)S(1)} %get-tuple-element.46.press, ...), custom_call_target="tpu_custom_call" | custom-call | tf_op jit(solution)/shard_map/pallas_call | solution.py:29
  36.3 0.0 collective-permute-done.5.refs_5_
  36.3 0.0 collective-permute-done.6.refs_6_
  36.3 0.0 collective-permute-done.7.refs_7_
  36.4 2.6 %shard_map.104 = (f32[3,16384]{1,0:T(4,128)}, f32[128,128]{1,0:T(8,128)}) custom-call(f32[12,8,8,128]{3,2,1,0:T(8,128)S(1)} %get-tuple-element.44.near, f32[128,128]{1,0:T(8,128)S(1)} %get-tuple-element.45.density, f32[12,128,128]{2,1,0:T(8,128)S(1)} %get-tuple-element.46.press, f32[12,3,512,128]{3,2,1,0:T(8,128)S(1)} %get-tuple-element.47.outside, ...), custom_call_target="tpu_custom_call" | custom-call | tf_op jit(solution)/shard_map/pallas_call | solution.py:29
  (6 shorter events, 0.0 us)
Async XLA Ops:
  0.6 14.0 %copy-start = (s32[1,4,8]{2,1,0:T(4,128)S(1)}, s32[1,4,8]{2,1,0:T(4,128)}, u32[]{:S(2)}) copy-start(s32[1,4,8]{2,1,0:T(4,128)} %exports.1) | copy-start | bytes 388
  0.6 14.0 %copy-start.2 = (s32[1,2,8,3]{2,1,3,0:T(2,128)S(1)}, s32[1,2,8,3]{2,1,3,0:T(2,128)}, u32[]{:S(2)}) copy-start(s32[1,2,8,3]{2,1,3,0:T(2,128)} %param.13) | copy-start | bytes 580
  0.7 14.0 %copy-start.1 = (s32[1,2,8,4]{2,3,1,0:T(4,128)S(1)}, s32[1,2,8,4]{2,3,1,0:T(4,128)}, u32[]{:S(2)}) copy-start(s32[1,2,8,4]{2,3,1,0:T(4,128)} %param.14) | copy-start | bytes 772
  0.7 14.0 %copy-start.3 = (s32[1,2,8]{2,1,0:T(2,128)S(1)}, s32[1,2,8]{2,1,0:T(2,128)}, u32[]{:S(2)}) copy-start(s32[1,2,8]{2,1,0:T(2,128)} %ids.1) | copy-start | bytes 196
  0.7 14.0 %copy-start.4 = (s32[1,2]{1,0:T(1,128)S(1)}, s32[1,2]{1,0:T(1,128)}, u32[]{:S(2)}) copy-start(s32[1,2]{1,0:T(1,128)} %counts.1) | copy-start | bytes 28
  3.2 4.7 %collective-permute-start = (f32[8,512]{1,0:T(8,128)S(1)}, f32[8,512]{1,0:T(8,128)S(1)}, u32[]{:S(2)}, u32[]{:S(2)}) collective-permute-start(f32[8,512]{1,0:T(8,128)S(1)} %shard_map.95), channel_id=1, source_target_pairs={{0,8},{4,12},{8,0},{12,4},{16,24},{20,28},{24,16},{28,20},{1,9},{5... | collective-permute-start | bytes 49160 | tf_op jit(solution)/shard_map/ppermute | solution.py:639
  8.0 1.4 %collective-permute-start.1 = (f32[8,512]{1,0:T(8,128)S(1)}, f32[8,512]{1,0:T(8,128)S(1)}, u32[]{:S(2)}, u32[]{:S(2)}) collective-permute-start(f32[8,512]{1,0:T(8,128)S(1)} %shard_map.98.after), channel_id=1, source_target_pairs={{0,4},{4,0},{8,12},{12,8},{16,20},{20,16},{24,28},{28,24},{1,5},{5... | collective-permute-start | bytes 49160 | tf_op jit(solution)/shard_map/ppermute | solution.py:639
  9.9 7.0 %collective-permute-start.2 = (f32[8,1792]{1,0:T(8,128)S(1)}, f32[8,1792]{1,0:T(8,128)S(1)}, u32[]{:S(2)}, u32[]{:S(2)}) collective-permute-start(f32[8,1792]{1,0:T(8,128)S(1)} %get-tuple-element.41), channel_id=1, source_target_pairs={{0,2},{1,3},{2,0},{3,1},{4,6},{5,7},{6,4},{7,5},{8,10},{9,11},{10,... | collective-permute-start | bytes 172040 | tf_op jit(solution)/shard_map/ppermute | solution.py:639
  13.1 6.5 %collective-permute-start.3 = (f32[8,1792]{1,0:T(8,128)S(1)}, f32[8,1792]{1,0:T(8,128)S(1)}, u32[]{:S(2)}, u32[]{:S(2)}) collective-permute-start(f32[8,1792]{1,0:T(8,128)S(1)} %get-tuple-element.42), channel_id=1, source_target_pairs={{0,3},{1,2},{2,1},{3,0},{4,7},{5,6},{6,5},{7,4},{8,11},{9,10},{10,... | collective-permute-start | bytes 172040 | tf_op jit(solution)/shard_map/ppermute | solution.py:639
  14.4 5.2 %collective-permute-start.4 = (f32[8,1792]{1,0:T(8,128)S(1)}, f32[8,1792]{1,0:T(8,128)S(1)}, u32[]{:S(2)}, u32[]{:S(2)}) collective-permute-start(f32[8,1792]{1,0:T(8,128)S(1)} %get-tuple-element.43), channel_id=1, source_target_pairs={{0,1},{1,0},{2,3},{3,2},{4,5},{5,4},{6,7},{7,6},{8,9},{9,8},{10,11... | collective-permute-start | bytes 172040 | tf_op jit(solution)/shard_map/ppermute | solution.py:639
  29.7 6.6 %collective-permute-start.5 = (f32[8,1024]{1,0:T(8,128)S(1)}, f32[8,1024]{1,0:T(8,128)S(1)}, u32[]{:S(2)}, u32[]{:S(2)}) collective-permute-start(f32[8,1024]{1,0:T(8,128)S(1)} %get-tuple-element.56.refs_2_), channel_id=1, source_target_pairs={{0,2},{1,3},{2,0},{3,1},{4,6},{5,7},{6,4},{7,5},{8,10},{9,11},{10,... | collective-permute-start | bytes 98312 | tf_op jit(solution)/shard_map/ppermute | solution.py:639
  29.8 6.5 %collective-permute-start.6 = (f32[8,1024]{1,0:T(8,128)S(1)}, f32[8,1024]{1,0:T(8,128)S(1)}, u32[]{:S(2)}, u32[]{:S(2)}) collective-permute-start(f32[8,1024]{1,0:T(8,128)S(1)} %get-tuple-element.57.refs_3_), channel_id=1, source_target_pairs={{0,3},{1,2},{2,1},{3,0},{4,7},{5,6},{6,5},{7,4},{8,11},{9,10},{10,... | collective-permute-start | bytes 98312 | tf_op jit(solution)/shard_map/ppermute | solution.py:639
  30.0 6.3 %collective-permute-start.7 = (f32[8,1024]{1,0:T(8,128)S(1)}, f32[8,1024]{1,0:T(8,128)S(1)}, u32[]{:S(2)}, u32[]{:S(2)}) collective-permute-start(f32[8,1024]{1,0:T(8,128)S(1)} %get-tuple-element.55.refs_1_), channel_id=1, source_target_pairs={{0,1},{1,0},{2,3},{3,2},{4,5},{5,4},{6,7},{7,6},{8,9},{9,8},{10,11... | collective-permute-start | bytes 98312 | tf_op jit(solution)/shard_map/ppermute | solution.py:639

commit v7 on v6

--- a/solution.py
+++ b/solution.py
@@ -12,9 +12,9 @@
 KERNEL_NORM = 21.0 / (16.0 * math.pi)
 FORCE_NORM = 5.0 * KERNEL_NORM * 32.0 * (2.0 / 3.0)
 TINY = 1e-30
-BLOCK_ORDER = (2, 3, 1)
+BLOCK_ORDER = (3, 2, 1)
 RETURN_ORDER = (2, 3, 1)
-PIECES = 4
+PIECES = 8
 F32 = jnp.float32
 I32 = jnp.int32
 VMEM = pltpu.VMEM
@@ -361,17 +361,18 @@
     for g in range(BLK // 8):
         part = slice(8 * g, 8 * g + 8)
         cx, cy, cz, cm, ch, cu = (centre[k, part, :] for k in range(6))
-        half = 0.5 / ch
+        reach = 2.0 * ch
+        edge = 2.5 * ch
         total = None
         pushes = []
-        for t in range(8):
+        for t in (4, 0, 5, 1, 6, 2, 7, 3):
             x, y, z, m, h = (wide(near[n, k, t : t + 1, :]) for k in range(5))
             apart = (cx - x, cy - y, cz - z)
             square = apart[0] * apart[0] + apart[1] * apart[1] + apart[2] * apart[2]
             distance = square * lax.rsqrt(jnp.maximum(square, TINY))
-            fall = jnp.maximum(1.0 - distance * half, 0.0)
+            fall = jnp.maximum(reach - distance, 0.0)
             fall2 = fall * fall
-            total = added(total, fall2 * fall2 * (1.25 - fall) * m)
+            total = added(total, fall2 * fall2 * (edge - fall) * m)
             if t < local:
                 at = 8 * (g * local + t)
                 inside[n, at : at + 8, :] = distance
@@ -384,7 +385,9 @@
                     plain[t - local][k] = added(plain[t - local][k], push[k])
                 pushes.append(push)
         total = jnp.broadcast_to(jnp.sum(total, axis=1, keepdims=True), (8, BLK))
-        rho = total * (4.0 * KERNEL_NORM / (ch * ch * ch))
+        inverse = 1.0 / reach
+        inv2 = inverse * inverse
+        rho = total * (inv2 * inv2 * inverse) * ((32.0 * KERNEL_NORM) * (inv2 * inverse))
         pressure = cu / rho
         press[n, part, :] = pressure
         own = added(own, jnp.where(row + 8 * g == lane, rho, 0.0))
@@ -487,11 +490,9 @@
             for t, g in enumerate(indices.ghosts(n, me * slots)):
                 back[0:6, lanes(g)] += jnp.where(n < live, rows[n, 0:6, t, :], 0.0)
 
-        def place(n, _):
-            density[pl.ds(indices.active(n), 1), :] = fresh[pl.ds(n, 1), :]
-            return 0
-
-        lax.fori_loop(0, live, place, 0)
+        for n in range(TOTACT):
+            block = pl.ds(indices.active(n), 1)
+            density[block, :] = jnp.where(n < live, fresh[n : n + 1, :], density[block, :])
         for q in range(peers):
             outs[q][...] = back[:, q * slots * BLK : (q + 1) * slots * BLK]
             for t in range(slots):
@@ -605,11 +606,11 @@
             others_press[n] = near[n, 5] / rho[8 * n : 8 * n + 8]
 
         def step(n, _):
-            outer_sums(near, 2 * n, press, others_press, outside, before, rows)
-            outer_sums(near, 2 * n + 1, press, others_press, outside, before, rows)
+            for k in range(4):
+                outer_sums(near, 4 * n + k, press, others_press, outside, before, rows)
             return 0
 
-        lax.fori_loop(0, TOTACT // 2, step, 0)
+        lax.fori_loop(0, TOTACT // 4, step, 0)
         for copy in copies:
             copy.wait()
         me = lax.axis_index("gy")

time: 39.6 us -> 39.1 us (0.987)
  Pallas kernels: 21.4 us -> 21 us
    pallas_call x10, Pallas kernels: 21.4 us -> 21 us  [call(): pl.pallas_call(kernel, out_shape=out_shape, in_specs=[pl.BlockSpec(memory...]
  transfers between devices with their start and end apart: 8 -> 8, of which waited for: 4 -> 3; matrix products, arithmetic and copies ran while one was open for 0% -> 0% of each run, Pallas kernels for 19% -> 19%
where the time goes in v7:
time: 39.1 us; the launch traced here: 38.5 us
  Pallas kernels  21 us (54%)
  starting transfers between devices  11.5 us (29%)
  waiting for transfers between devices  3.35 us (9%)
  local copies, waits for them, and re-layouts  1.13 us (3%)
  between operations  0.81 us (2%)
  other arithmetic  0.74 us (2%)
    pallas_call x10, Pallas kernels, call(): pl.pallas_call(kernel, out_shape=out_shape, in_specs=[pl.BlockSpec(memory...  21 us
    ppermute x8, starting transfers between devices, crossed(): lax.ppermute(block, axis, [(i, i ^ bits) for i in range(size) if i ^ bits...  11.5 us
    ppermute x8, waiting for transfers between devices, crossed(): lax.ppermute(block, axis, [(i, i ^ bits) for i in range(size) if i ^ bits...  3.35 us
    pad x1, local copies, waits for them, and re-layouts, shards(): state = jnp.pad(particles, ((0, 1), (0, 0)))  1.11 us
  transfers between devices with their start and end apart: 8, of which 3 were waited for; matrix products, arithmetic and copies ran while one was open for 0% of the time, Pallas kernels for 19%

profile of v7, /device:TPU:0, one launch (start us, length us, event | category | flops | bytes accessed | tf_op | source)
XLA Modules:
  0.0 38.5 jit_solution(4617864853975462580)
XLA Ops:
  0.6 0.0 copy-start
  0.6 0.0 copy-start.2
  0.7 0.0 copy-start.1
  0.7 1.1 %pad.12.state = f32[8,16384]{1,0:T(8,128)S(1)} pad(f32[7,16384]{1,0:T(8,128)} %param.8, f32[]{:T(128)} %constant.2.clone.1), padding=0_1x0_0 | pad | bytes 983044 | tf_op jit(solution)/shard_map/jit(_pad)/pad | solution.py:675
  1.8 0.7 %pad_add_fusion.ints = s32[12,512]{1,0:T(8,128)S(1)} fusion(s32[4,8]{1,0:T(4,128)} %bitcast.5, s32[1,4]{1,0:T(1,128)} %param.9, s32[4,512]{1,0:T(4,128)} %bitcast.8), kind=kLoop, calls=%fused_computation | loop fusion | flops 12288 | bytes 32912 | tf_op jit(solution)/shard_map/concatenate | solution.py:667
  2.5 0.6 %shard_map.95 = f32[8,512]{1,0:T(8,128)S(1)} custom-call(f32[8,16384]{1,0:T(8,128)S(1)} %pad.12.state, s32[12,512]{1,0:T(8,128)S(1)} %pad_add_fusion.ints), custom_call_target="tpu_custom_call" | custom-call | tf_op jit(solution)/shard_map/pallas_call | solution.py:29
  3.2 3.0 %collective-permute-start = (f32[8,512]{1,0:T(8,128)S(1)}, f32[8,512]{1,0:T(8,128)S(1)}, u32[]{:S(2)}, u32[]{:S(2)}) collective-permute-start(f32[8,512]{1,0:T(8,128)S(1)} %shard_map.95), channel_id=1, source_target_pairs={{0,8},{4,12},{8,0},{12,4},{16,24},{20,28},{24,16},{28,20},{1,9},{5... | collective-permute-start | bytes 49160 | tf_op jit(solution)/shard_map/ppermute | solution.py:640
  6.2 0.5 %shard_map.96.codes = s32[4,128,128]{2,1,0:T(8,128)S(1)} custom-call(s32[12,512]{1,0:T(8,128)S(1)} %pad_add_fusion.ints), custom_call_target="tpu_custom_call" | custom-call | tf_op jit(solution)/shard_map/pallas_call | solution.py:29
  6.7 1.0 %shard_map.97 = (f32[8,512]{1,0:T(8,128)S(1)}, s32[8,512]{1,0:T(8,128)S(1)}, s32[4,128,128]{2,1,0:T(8,128)S(1)}) custom-call(f32[8,16384]{1,0:T(8,128)S(1)} %pad.12.state, s32[12,512]{1,0:T(8,128)S(1)} %pad_add_fusion.ints, s32[4,128,128]{2,1,0:T(8,128)S(1)} %shard_map.96.codes), custom_call_target="tpu_custom_call" | custom-call | tf_op jit(solution)/shard_map/pallas_call | solution.py:29
  7.7 0.2 collective-permute-done.got0
  7.9 0.1 shard_map.98.after
  8.0 0.1 collective-permute-start.1
  8.1 1.3 %shard_map.100 = (f32[2,8,512]{2,1,0:T(8,128)S(1)}, f32[8,4096]{1,0:T(8,128)S(1)}, s32[4,8,128]{2,1,0:T(8,128)S(1)}) custom-call(f32[8,16384]{1,0:T(8,128)S(1)} %pad.12.state, s32[12,512]{1,0:T(8,128)S(1)} %pad_add_fusion.ints, s32[4,128,128]{2,1,0:T(8,128)S(1)} %get-tuple-element.33.codes.tables, f32[8,512]{1,0:T(8,128)S(1)} %shard_map.98.after), custom_call_target="tpu_custom_call" | custom-call | tf_op jit(solution)/shard_map/pallas_call | solution.py:29
  9.3 0.0 collective-permute-done.1.got1
  9.3 0.6 %shard_map.101 = (f32[8,2048]{1,0:T(8,128)S(1)}, f32[8,1792]{1,0:T(8,128)S(1)}, f32[8,1792]{1,0:T(8,128)S(1)}, f32[8,1792]{1,0:T(8,128)S(1)}) custom-call(f32[2,8,512]{2,1,0:T(8,128)S(1)} %get-tuple-element.37.cols, s32[8,512]{1,0:T(8,128)S(1)} %get-tuple-element.32.marks, f32[8,512]{1,0:T(8,128)S(1)} %collective-permute-done.got0, ...), custom_call_target="tpu_custom_call" | custom-call | tf_op jit(solution)/shard_map/pallas_call | solution.py:29
  9.9 4.2 %collective-permute-start.2 = (f32[8,1792]{1,0:T(8,128)S(1)}, f32[8,1792]{1,0:T(8,128)S(1)}, u32[]{:S(2)}, u32[]{:S(2)}) collective-permute-start(f32[8,1792]{1,0:T(8,128)S(1)} %get-tuple-element.41), channel_id=1, source_target_pairs={{0,3},{1,2},{2,1},{3,0},{4,7},{5,6},{6,5},{7,4},{8,11},{9,10},{10,... | collective-permute-start | bytes 172040 | tf_op jit(solution)/shard_map/ppermute | solution.py:640
  14.1 0.0 collective-permute-start.3
  14.1 0.6 %collective-permute-start.4 = (f32[8,1792]{1,0:T(8,128)S(1)}, f32[8,1792]{1,0:T(8,128)S(1)}, u32[]{:S(2)}, u32[]{:S(2)}) collective-permute-start(f32[8,1792]{1,0:T(8,128)S(1)} %get-tuple-element.43), channel_id=1, source_target_pairs={{0,1},{1,0},{2,3},{3,2},{4,5},{5,4},{6,7},{7,6},{8,9},{9,8},{10,11... | collective-permute-start | bytes 172040 | tf_op jit(solution)/shard_map/ppermute | solution.py:640
  14.7 0.0 copy-done.2
  14.8 1.6 %shard_map.99 = (f32[12,4,8,128]{3,2,1,0:T(8,128)S(1)}, f32[128,128]{1,0:T(8,128)S(1)}, f32[96,128]{1,0:T(8,128)S(1)}, f32[96,128]{1,0:T(8,128)S(1)}, s32[21,8]{1,0:T(8,128)S(1)}) custom-call(f32[8,16384]{1,0:T(8,128)S(1)} %pad.12.state, f32[8,512]{1,0:T(8,128)S(1)} %collective-permute-done.got0, f32[8,512]{1,0:T(8,128)S(1)} %collective-permute-done.1.got1, ...), custom_call_target="tpu_custom_call" | custom-call | tf_op jit(solution)/shard_map/pallas_call | solution.py:29
  16.4 0.4 %collective-permute-done.2.refs_1_ = f32[8,1792]{1,0:T(8,128)S(1)} collective-permute-done((f32[8,1792]{1,0:T(8,128)S(1)}, f32[8,1792]{1,0:T(8,128)S(1)}, u32[]{:S(2)}, u32[]{:S(2)}) %collective-permute-start.2) | collective-permute-done | bytes 57376 | tf_op jit(solution)/shard_map/ppermute | solution.py:640
  16.8 2.7 %collective-permute-done.3.refs_2_ = f32[8,1792]{1,0:T(8,128)S(1)} collective-permute-done((f32[8,1792]{1,0:T(8,128)S(1)}, f32[8,1792]{1,0:T(8,128)S(1)}, u32[]{:S(2)}, u32[]{:S(2)}) %collective-permute-start.3) | collective-permute-done | bytes 57376 | tf_op jit(solution)/shard_map/ppermute | solution.py:640
  19.5 0.0 collective-permute-done.4.refs_3_
  19.5 9.9 %shard_map.102 = (f32[12,8,8,128]{3,2,1,0:T(8,128)S(1)}, f32[128,128]{1,0:T(8,128)S(1)}, f32[12,5,128,128]{3,2,1,0:T(8,128)S(1)}, f32[12,128,128]{2,1,0:T(8,128)...) custom-call(f32[12,4,8,128]{3,2,1,0:T(8,128)S(1)} %get-tuple-element, ...), custom_call_target="tpu_custom_call" | custom-call | tf_op jit(solution)/shard_map/pallas_call | solution.py:29
  29.4 0.1 collective-permute-start.5
  29.5 0.1 collective-permute-start.6
  29.6 3.4 %collective-permute-start.7 = (f32[8,1024]{1,0:T(8,128)S(1)}, f32[8,1024]{1,0:T(8,128)S(1)}, u32[]{:S(2)}, u32[]{:S(2)}) collective-permute-start(f32[8,1024]{1,0:T(8,128)S(1)} %get-tuple-element.55.refs_1_), channel_id=1, source_target_pairs={{0,1},{1,0},{2,3},{3,2},{4,5},{5,4},{6,7},{7,6},{8,9},{9,8},{10,11... | collective-permute-start | bytes 98312 | tf_op jit(solution)/shard_map/ppermute | solution.py:640
  33.0 3.0 %shard_map.103 = (f32[8,16384]{1,0:T(8,128)S(1)}, f32[12,3,128,128]{3,2,1,0:T(8,128)S(1)}) custom-call(f32[12,8,8,128]{3,2,1,0:T(8,128)S(1)} %get-tuple-element.44.near, f32[128,128]{1,0:T(8,128)S(1)} %get-tuple-element.45.density, f32[12,5,128,128]{3,2,1,0:T(8,128)S(1)} %get-tuple-element.48.centre, f32[12,128,128]{2,1,0:T(8,128)S(1)} %get-tuple-element.46.press, ...), custom_call_target="tpu_custom_call" | custom-call | tf_op jit(solution)/shard_map/pallas_call | solution.py:29
  36.0 0.0 collective-permute-done.5.refs_5_
  36.0 0.0 collective-permute-done.6.refs_6_
  36.0 0.0 collective-permute-done.7.refs_7_
  36.0 2.4 %shard_map.104 = (f32[3,16384]{1,0:T(4,128)}, f32[128,128]{1,0:T(8,128)}) custom-call(f32[12,8,8,128]{3,2,1,0:T(8,128)S(1)} %get-tuple-element.44.near, f32[128,128]{1,0:T(8,128)S(1)} %get-tuple-element.45.density, f32[12,128,128]{2,1,0:T(8,128)S(1)} %get-tuple-element.46.press, f32[12,3,512,128]{3,2,1,0:T(8,128)S(1)} %get-tuple-element.47.outside, ...), custom_call_target="tpu_custom_call" | custom-call | tf_op jit(solution)/shard_map/pallas_call | solution.py:29
  (6 shorter events, 0.0 us)
Async XLA Ops:
  0.6 14.1 %copy-start = (s32[1,4,8]{2,1,0:T(4,128)S(1)}, s32[1,4,8]{2,1,0:T(4,128)}, u32[]{:S(2)}) copy-start(s32[1,4,8]{2,1,0:T(4,128)} %exports.1) | copy-start | bytes 388
  0.6 14.1 %copy-start.2 = (s32[1,2,8,3]{2,1,3,0:T(2,128)S(1)}, s32[1,2,8,3]{2,1,3,0:T(2,128)}, u32[]{:S(2)}) copy-start(s32[1,2,8,3]{2,1,3,0:T(2,128)} %param.13) | copy-start | bytes 580
  0.7 14.1 %copy-start.1 = (s32[1,2,8,4]{2,3,1,0:T(4,128)S(1)}, s32[1,2,8,4]{2,3,1,0:T(4,128)}, u32[]{:S(2)}) copy-start(s32[1,2,8,4]{2,3,1,0:T(4,128)} %param.14) | copy-start | bytes 772
  0.7 14.1 %copy-start.3 = (s32[1,2,8]{2,1,0:T(2,128)S(1)}, s32[1,2,8]{2,1,0:T(2,128)}, u32[]{:S(2)}) copy-start(s32[1,2,8]{2,1,0:T(2,128)} %ids.1) | copy-start | bytes 196
  0.7 14.1 %copy-start.4 = (s32[1,2]{1,0:T(1,128)S(1)}, s32[1,2]{1,0:T(1,128)}, u32[]{:S(2)}) copy-start(s32[1,2]{1,0:T(1,128)} %counts.1) | copy-start | bytes 28
  3.2 4.7 %collective-permute-start = (f32[8,512]{1,0:T(8,128)S(1)}, f32[8,512]{1,0:T(8,128)S(1)}, u32[]{:S(2)}, u32[]{:S(2)}) collective-permute-start(f32[8,512]{1,0:T(8,128)S(1)} %shard_map.95), channel_id=1, source_target_pairs={{0,8},{4,12},{8,0},{12,4},{16,24},{20,28},{24,16},{28,20},{1,9},{5... | collective-permute-start | bytes 49160 | tf_op jit(solution)/shard_map/ppermute | solution.py:640
  8.0 1.4 %collective-permute-start.1 = (f32[8,512]{1,0:T(8,128)S(1)}, f32[8,512]{1,0:T(8,128)S(1)}, u32[]{:S(2)}, u32[]{:S(2)}) collective-permute-start(f32[8,512]{1,0:T(8,128)S(1)} %shard_map.98.after), channel_id=1, source_target_pairs={{0,4},{4,0},{8,12},{12,8},{16,20},{20,16},{24,28},{28,24},{1,5},{5... | collective-permute-start | bytes 49160 | tf_op jit(solution)/shard_map/ppermute | solution.py:640
  9.9 6.9 %collective-permute-start.2 = (f32[8,1792]{1,0:T(8,128)S(1)}, f32[8,1792]{1,0:T(8,128)S(1)}, u32[]{:S(2)}, u32[]{:S(2)}) collective-permute-start(f32[8,1792]{1,0:T(8,128)S(1)} %get-tuple-element.41), channel_id=1, source_target_pairs={{0,3},{1,2},{2,1},{3,0},{4,7},{5,6},{6,5},{7,4},{8,11},{9,10},{10,... | collective-permute-start | bytes 172040 | tf_op jit(solution)/shard_map/ppermute | solution.py:640
  14.1 5.4 %collective-permute-start.3 = (f32[8,1792]{1,0:T(8,128)S(1)}, f32[8,1792]{1,0:T(8,128)S(1)}, u32[]{:S(2)}, u32[]{:S(2)}) collective-permute-start(f32[8,1792]{1,0:T(8,128)S(1)} %get-tuple-element.42), channel_id=1, source_target_pairs={{0,2},{1,3},{2,0},{3,1},{4,6},{5,7},{6,4},{7,5},{8,10},{9,11},{10,... | collective-permute-start | bytes 172040 | tf_op jit(solution)/shard_map/ppermute | solution.py:640
  14.1 5.4 %collective-permute-start.4 = (f32[8,1792]{1,0:T(8,128)S(1)}, f32[8,1792]{1,0:T(8,128)S(1)}, u32[]{:S(2)}, u32[]{:S(2)}) collective-permute-start(f32[8,1792]{1,0:T(8,128)S(1)} %get-tuple-element.43), channel_id=1, source_target_pairs={{0,1},{1,0},{2,3},{3,2},{4,5},{5,4},{6,7},{7,6},{8,9},{9,8},{10,11... | collective-permute-start | bytes 172040 | tf_op jit(solution)/shard_map/ppermute | solution.py:640
  29.4 6.6 %collective-permute-start.5 = (f32[8,1024]{1,0:T(8,128)S(1)}, f32[8,1024]{1,0:T(8,128)S(1)}, u32[]{:S(2)}, u32[]{:S(2)}) collective-permute-start(f32[8,1024]{1,0:T(8,128)S(1)} %get-tuple-element.56.refs_2_), channel_id=1, source_target_pairs={{0,2},{1,3},{2,0},{3,1},{4,6},{5,7},{6,4},{7,5},{8,10},{9,11},{10,... | collective-permute-start | bytes 98312 | tf_op jit(solution)/shard_map/ppermute | solution.py:640
  29.5 6.5 %collective-permute-start.6 = (f32[8,1024]{1,0:T(8,128)S(1)}, f32[8,1024]{1,0:T(8,128)S(1)}, u32[]{:S(2)}, u32[]{:S(2)}) collective-permute-start(f32[8,1024]{1,0:T(8,128)S(1)} %get-tuple-element.57.refs_3_), channel_id=1, source_target_pairs={{0,3},{1,2},{2,1},{3,0},{4,7},{5,6},{6,5},{7,4},{8,11},{9,10},{10,... | collective-permute-start | bytes 98312 | tf_op jit(solution)/shard_map/ppermute | solution.py:640
  29.6 6.4 %collective-permute-start.7 = (f32[8,1024]{1,0:T(8,128)S(1)}, f32[8,1024]{1,0:T(8,128)S(1)}, u32[]{:S(2)}, u32[]{:S(2)}) collective-permute-start(f32[8,1024]{1,0:T(8,128)S(1)} %get-tuple-element.55.refs_1_), channel_id=1, source_target_pairs={{0,1},{1,0},{2,3},{3,2},{4,5},{5,4},{6,7},{7,6},{8,9},{9,8},{10,11... | collective-permute-start | bytes 98312 | tf_op jit(solution)/shard_map/ppermute | solution.py:640
